TPU v7x, 32 devices: a whole 2x2x4 slice. The times are simulated.
32 devices in a mesh: dp: 8 (over z, x), tensor: 4 (over y, core).
Axes of the slice: x: 2, y: 2, z: 4, core: 2. Of those that a mesh axis runs over, the one named last changes fastest.
Arguments:
- hidden_in: bfloat16 [8192, 768], P(('dp', 'tensor')), may hold values from -6 to 6
- cotangent: bfloat16 [8192, 768], P(('dp', 'tensor')), may hold values from -6 to 6
- w_query: bfloat16 [2, 768, 768], P(None, 'dp', 'tensor'), may hold values from -0.21875 to 0.21875
- w_key: bfloat16 [2, 768, 768], P(None, 'dp', 'tensor'), may hold values from -0.21875 to 0.21875
- w_value: bfloat16 [2, 768, 768], P(None, 'dp', 'tensor'), may hold values from -0.21875 to 0.21875
- w_outgate: bfloat16 [2, 768, 768], P(None, 'dp', 'tensor'), may hold values from -0.21875 to 0.21875
- w_rate: bfloat16 [2, 768, 12], P(None, 'dp', 'tensor'), may hold values from -0.21875 to 0.21875
- w_output: bfloat16 [2, 768, 768], P(None, 'tensor', 'dp'), may hold values from -0.21875 to 0.21875
- init_first: bfloat16 [2, 12, 64, 256], P(None, 'tensor', None, 'dp'), may hold values from -0.75 to 0.75
- init_first_bias: bfloat16 [2, 12, 256], P(None, 'tensor', 'dp'), may hold values from -2 to 2
- init_second: bfloat16 [2, 12, 256, 64], P(None, 'tensor', 'dp'), may hold values from -0.375 to 0.375
- init_second_bias: bfloat16 [2, 12, 64], P(None, 'tensor', 'dp'), may hold values from -2 to 2
- inner_gain: bfloat16 [2, 12, 64], P(None, 'tensor', 'dp'), may hold values from 0.5 to 1.5
- inner_shift: bfloat16 [2, 12, 64], P(None, 'tensor', 'dp'), may hold values from -2 to 2
- post_gain: bfloat16 [2, 12, 64], P(None, 'tensor', 'dp'), may hold values from 0.5 to 1.5
- post_shift: bfloat16 [2, 12, 64], P(None, 'tensor', 'dp'), may hold values from -2 to 2
- mixer_gain: bfloat16 [2, 768], P(None, ('dp', 'tensor')), may hold values from 0.5 to 1.5
- mlp_gain: bfloat16 [2, 768], P(None, ('dp', 'tensor')), may hold values from 0.5 to 1.5
- w_gate: bfloat16 [2, 768, 2048], P(None, 'dp', 'tensor'), may hold values from -0.21875 to 0.21875
- w_up: bfloat16 [2, 768, 2048], P(None, 'dp', 'tensor'), may hold values from -0.21875 to 0.21875
- w_down: bfloat16 [2, 2048, 768], P(None, 'tensor', 'dp'), may hold values from -0.125 to 0.125
Outputs:
- block_out: bfloat16 [8192, 768], P(('dp', 'tensor'))
- grad_in: float32 [8192, 768], P(('dp', 'tensor'))
- grad_query: float32 [2, 768, 768], P(None, 'dp', 'tensor')
- grad_key: float32 [2, 768, 768], P(None, 'dp', 'tensor')
- grad_value: float32 [2, 768, 768], P(None, 'dp', 'tensor')
- grad_outgate: float32 [2, 768, 768], P(None, 'dp', 'tensor')
- grad_rate: float32 [2, 768, 12], P(None, 'dp', 'tensor')
- grad_output: float32 [2, 768, 768], P(None, 'tensor', 'dp')
- gradient_hidden_weight: float32 [2, 12, 64, 256], P(None, 'tensor', None, 'dp')
- grad_first_bias: float32 [2, 12, 256], P(None, 'tensor', 'dp')
- gradient_output_weight: float32 [2, 12, 256, 64], P(None, 'tensor', 'dp')
- grad_second_bias: float32 [2, 12, 64], P(None, 'tensor', 'dp')
- grad_inner_gain: float32 [2, 12, 64], P(None, 'tensor', 'dp')
- grad_inner_shift: float32 [2, 12, 64], P(None, 'tensor', 'dp')
- grad_post_gain: float32 [2, 12, 64], P(None, 'tensor', 'dp')
- grad_post_shift: float32 [2, 12, 64], P(None, 'tensor', 'dp')
- grad_mixer_gain: float32 [2, 768], P(None, ('dp', 'tensor'))
- grad_mlp_gain: float32 [2, 768], P(None, ('dp', 'tensor'))
- grad_w_gate: float32 [2, 768, 2048], P(None, 'dp', 'tensor')
- grad_w_up: float32 [2, 768, 2048], P(None, 'dp', 'tensor')
- grad_w_down: float32 [2, 2048, 768], P(None, 'tensor', 'dp')
All inputs are finite; a program needn't handle non-finite values.
Results may differ from a plain program's by a relative error of at most 0.03.
Values may be sent and summed in bfloat16 or wider, within the bound.
No kernel may reach another device: no remote copies, remote signals or barrier semaphores. Data moves between devices by JAX's collectives and lax.ppermute only.
A program may use at most 128 MiB of HBM per device.

v0:
```python
import math

import jax
import jax.numpy as jnp
from jax import lax
from jax.sharding import PartitionSpec as P

D = 768
CS = 16
LEN = 1024
LAYERS = 2


epsilon = 1e-06
base_rate = 1.0
precision_level = lax.Precision.HIGHEST


def layer_norm(row_vals, weight, shift_vec):
    center = row_vals - jnp.mean(row_vals, axis=-1, keepdims=True)
    return (
        center * lax.rsqrt(jnp.mean(center * center, axis=-1, keepdims=True) + epsilon) * weight
        + shift_vec
    )


def gelu_tanh(values_in):
    return jax.nn.gelu(values_in, approximate=True)


def activation_slope(values_in):
    tanh_val = jnp.tanh(
        0.7978845608028654 * (values_in + 0.044715 * values_in * values_in * values_in)
    )
    return 0.5 * (1.0 + tanh_val) + 0.5 * values_in * (
        1.0 - tanh_val * tanh_val
    ) * 0.7978845608028654 * (1.0 + 3.0 * 0.044715 * values_in * values_in)


def inner_step(ln_weight, ln_shift, state_now, block_in):
    hidden_weight, hidden_bias, output_weight, output_bias = state_now
    query_rows_all, key_matrix_rows, value_rows, step_rates = block_in
    mini_size = query_rows_all.shape[1]
    position = jnp.arange(mini_size, dtype=jnp.float32)
    causal = (jnp.arange(mini_size)[:, None] >= jnp.arange(mini_size)[None, :]).astype(jnp.float32)
    inner_rate_matrix = (
        (1.0 / (position + 1.0))[None, :, None] * step_rates[:, None, :] * causal[None]
    )
    hidden_preactivation = (
        jnp.einsum("umr,urt->umt", key_matrix_rows, hidden_weight, precision=precision_level)
        + hidden_bias[:, None, :]
    )
    activation_hidden = gelu_tanh(hidden_preactivation)
    output_preactivation = (
        jnp.einsum("uez,uzy->uey", activation_hidden, output_weight, precision=precision_level)
        + output_bias[:, None, :]
    )
    center = output_preactivation - jnp.mean(output_preactivation, axis=-1, keepdims=True)
    inv_std = lax.rsqrt(jnp.mean(center * center, axis=-1, keepdims=True) + epsilon)
    unit_rows = center * inv_std
    grad_out = (
        unit_rows * ln_weight[:, None, :] + ln_shift[:, None, :] - (value_rows - key_matrix_rows)
    )
    grad_hat = grad_out * ln_weight[:, None, :]
    gradient_output_weight = inv_std * (
        grad_hat
        - jnp.mean(grad_hat, axis=-1, keepdims=True)
        - unit_rows * jnp.mean(grad_hat * unit_rows, axis=-1, keepdims=True)
    )
    gradient_hidden_weight = jnp.einsum(
        "qml,qrl->qmr", gradient_output_weight, output_weight, precision=precision_level
    ) * activation_slope(hidden_preactivation)
    attention_scores_inner = (
        jnp.einsum("cbd,ced->cbe", query_rows_all, key_matrix_rows, precision=precision_level) + 1.0
    )
    hidden_preactivation_cotangent = (
        jnp.einsum("umr,urt->umt", query_rows_all, hidden_weight, precision=precision_level)
        + hidden_bias[:, None, :]
        - jnp.einsum(
            "suz,szt->sut",
            inner_rate_matrix * attention_scores_inner,
            gradient_hidden_weight,
            precision=precision_level,
        )
    )
    activation_cotangent = gelu_tanh(hidden_preactivation_cotangent)
    attention_scores_outer = (
        jnp.einsum(
            "psj,ptj->pst", activation_cotangent, activation_hidden, precision=precision_level
        )
        + 1.0
    )
    output_preactivation_cotangent = (
        jnp.einsum("uez,uzy->uey", activation_cotangent, output_weight, precision=precision_level)
        + output_bias[:, None, :]
        - jnp.einsum(
            "ntl,nlp->ntp",
            inner_rate_matrix * attention_scores_outer,
            gradient_output_weight,
            precision=precision_level,
        )
    )
    final_row_slice = inner_rate_matrix[:, -1, :]
    updated_hidden_weight = hidden_weight - jnp.einsum(
        "ki,kir,kil->krl",
        final_row_slice,
        key_matrix_rows,
        gradient_hidden_weight,
        precision=precision_level,
    )
    updated_hidden_bias = hidden_bias - jnp.einsum(
        "qg,qgx->qx", final_row_slice, gradient_hidden_weight, precision=precision_level
    )
    updated_output_weight = output_weight - jnp.einsum(
        "ae,aet,aeu->atu",
        final_row_slice,
        activation_hidden,
        gradient_output_weight,
        precision=precision_level,
    )
    second_bias_new = output_bias - jnp.einsum(
        "cb,cbd->cd", final_row_slice, gradient_output_weight, precision=precision_level
    )
    output = query_rows_all + layer_norm(
        output_preactivation_cotangent, ln_weight[:, None, :], ln_shift[:, None, :]
    )
    return (
        (updated_hidden_weight, updated_hidden_bias, updated_output_weight, second_bias_new),
        output,
    )


def inner_chains(
    query_rows_all,
    key_matrix_rows,
    value_rows,
    rate_logit,
    hidden_weight,
    hidden_bias,
    output_weight,
    output_bias,
    ln_weight,
    ln_shift,
):
    head_count = hidden_weight.shape[0]
    head_dim = hidden_weight.shape[1]
    seq_count = query_rows_all.shape[0] // LEN
    blocks = LEN // CS
    group_size = math.gcd(blocks, 8)
    outer = blocks // group_size
    chains = seq_count * head_count

    def arrange(field_in):
        return (
            field_in.reshape(seq_count, outer, group_size, CS, head_count, head_dim)
            .transpose(1, 2, 0, 4, 3, 5)
            .reshape(outer, group_size, chains, CS, head_dim)
        )

    step_rates = base_rate * jax.nn.sigmoid(rate_logit) / head_dim
    step_rates = (
        step_rates.reshape(seq_count, outer, group_size, CS, head_count)
        .transpose(1, 2, 0, 4, 3)
        .reshape(outer, group_size, chains, CS)
    )
    weight_all = jnp.tile(ln_weight, (seq_count, 1))
    shift_all = jnp.tile(ln_shift, (seq_count, 1))
    state_now = (
        jnp.tile(hidden_weight, (seq_count, 1, 1)),
        jnp.tile(hidden_bias, (seq_count, 1)),
        jnp.tile(output_weight, (seq_count, 1, 1)),
        jnp.tile(output_bias, (seq_count, 1)),
    )

    def single(state_in, block_in):
        return inner_step(weight_all, shift_all, state_in, block_in)

    single_saved = jax.checkpoint(single)

    def grouped(state_in, blocks_in):
        return lax.scan(single_saved, state_in, blocks_in)

    final_state, outputs = lax.scan(
        jax.checkpoint(grouped),
        state_now,
        (arrange(query_rows_all), arrange(key_matrix_rows), arrange(value_rows), step_rates),
    )
    return (
        outputs.reshape(outer, group_size, seq_count, head_count, CS, head_dim)
        .transpose(2, 0, 1, 4, 3, 5)
        .reshape(seq_count * LEN, head_count * head_dim)
    )


def contract_rows(left, right):
    return lax.dot_general(
        left, right, (((0,), (0,)), ((), ())), preferred_element_type=jnp.float32
    )


def contract_cols(left, right):
    return lax.dot_general(
        left, right, (((1,), (1,)), ((), ())), preferred_element_type=jnp.float32
    )


def widen(normed):
    return lax.all_gather(normed, "tensor", axis=0, tiled=True)


def widen_back(grad_rows):
    return lax.all_gather(grad_rows, "tensor", axis=0, tiled=True)


def narrow(source_rows, matrix, row_count):

    def term_rows(start_row, count_rows):
        return jnp.dot(source_rows, matrix, preferred_element_type=jnp.float32)

    return lax.psum_scatter(
        term_rows(jnp.int32(0), row_count * lax.axis_size("tensor")).astype(jnp.bfloat16),
        "tensor",
        scatter_dimension=0,
        tiled=True,
    ).astype(jnp.float32)


def narrow_back(grad_pairs, row_count):

    def term_rows(start_row, count_rows):
        total_sum = None
        for grad_part, matrix in grad_pairs:
            product = contract_cols(grad_part, matrix)
            total_sum = product if total_sum is None else total_sum + product
        return total_sum

    return lax.psum_scatter(
        term_rows(jnp.int32(0), row_count * lax.axis_size("tensor")).astype(jnp.bfloat16),
        "tensor",
        scatter_dimension=0,
        tiled=True,
    ).astype(jnp.float32)


def fetch_layer(stacked, layer_idx):
    return (
        lax.all_gather(stacked[0][layer_idx], "dp", axis=0, tiled=True),
        lax.all_gather(stacked[1][layer_idx], "dp", axis=0, tiled=True),
        lax.all_gather(stacked[2][layer_idx], "dp", axis=0, tiled=True),
        lax.all_gather(stacked[3][layer_idx], "dp", axis=0, tiled=True),
        lax.all_gather(stacked[4][layer_idx], "dp", axis=0, tiled=True),
        lax.all_gather(stacked[5][layer_idx], "dp", axis=1, tiled=True),
        lax.all_gather(stacked[6][layer_idx], "dp", axis=2, tiled=True),
        lax.all_gather(stacked[7][layer_idx], "dp", axis=1, tiled=True),
        lax.all_gather(stacked[8][layer_idx], "dp", axis=1, tiled=True),
        lax.all_gather(stacked[9][layer_idx], "dp", axis=1, tiled=True),
        lax.all_gather(stacked[10][layer_idx], "dp", axis=1, tiled=True),
        lax.all_gather(stacked[11][layer_idx], "dp", axis=1, tiled=True),
        lax.all_gather(stacked[12][layer_idx], "dp", axis=1, tiled=True),
        lax.all_gather(stacked[13][layer_idx], "dp", axis=1, tiled=True),
        lax.all_gather(stacked[14][layer_idx], "dp", axis=0, tiled=True),
        lax.all_gather(stacked[15][layer_idx], "dp", axis=0, tiled=True),
        lax.all_gather(stacked[16][layer_idx], "dp", axis=1, tiled=True),
    )


def reduce_grads(parts):
    return (
        lax.psum_scatter(
            parts[0].astype(jnp.bfloat16), "dp", scatter_dimension=0, tiled=True
        ).astype(jnp.float32),
        lax.psum_scatter(
            parts[1].astype(jnp.bfloat16), "dp", scatter_dimension=0, tiled=True
        ).astype(jnp.float32),
        lax.psum_scatter(
            parts[2].astype(jnp.bfloat16), "dp", scatter_dimension=0, tiled=True
        ).astype(jnp.float32),
        lax.psum_scatter(
            parts[3].astype(jnp.bfloat16), "dp", scatter_dimension=0, tiled=True
        ).astype(jnp.float32),
        lax.psum_scatter(
            parts[4].astype(jnp.bfloat16), "dp", scatter_dimension=0, tiled=True
        ).astype(jnp.float32),
        lax.psum_scatter(
            parts[5].astype(jnp.bfloat16), "dp", scatter_dimension=1, tiled=True
        ).astype(jnp.float32),
        lax.psum_scatter(
            parts[6].astype(jnp.bfloat16), "dp", scatter_dimension=2, tiled=True
        ).astype(jnp.float32),
        lax.psum_scatter(
            parts[7].astype(jnp.bfloat16), "dp", scatter_dimension=1, tiled=True
        ).astype(jnp.float32),
        lax.psum_scatter(
            parts[8].astype(jnp.bfloat16), "dp", scatter_dimension=1, tiled=True
        ).astype(jnp.float32),
        lax.psum_scatter(
            parts[9].astype(jnp.bfloat16), "dp", scatter_dimension=1, tiled=True
        ).astype(jnp.float32),
        lax.psum_scatter(
            parts[10].astype(jnp.bfloat16), "dp", scatter_dimension=1, tiled=True
        ).astype(jnp.float32),
        lax.psum_scatter(
            parts[11].astype(jnp.bfloat16), "dp", scatter_dimension=1, tiled=True
        ).astype(jnp.float32),
        lax.psum_scatter(
            parts[12].astype(jnp.bfloat16), "dp", scatter_dimension=1, tiled=True
        ).astype(jnp.float32),
        lax.psum_scatter(
            parts[13].astype(jnp.bfloat16), "dp", scatter_dimension=1, tiled=True
        ).astype(jnp.float32),
        lax.psum_scatter(
            parts[14].astype(jnp.bfloat16), "dp", scatter_dimension=0, tiled=True
        ).astype(jnp.float32),
        lax.psum_scatter(
            parts[15].astype(jnp.bfloat16), "dp", scatter_dimension=0, tiled=True
        ).astype(jnp.float32),
        lax.psum_scatter(
            parts[16].astype(jnp.bfloat16), "dp", scatter_dimension=1, tiled=True
        ).astype(jnp.float32),
    )


def rms_forward(residual, gain_vec):
    inv_rms = lax.rsqrt(jnp.mean(residual * residual, axis=1, keepdims=True) + epsilon)
    return ((residual * inv_rms * gain_vec.astype(jnp.float32)).astype(jnp.bfloat16), inv_rms)


def rms_backward(residual, inv_rms, gain_vec, grad_norm):
    scaled = grad_norm * gain_vec.astype(jnp.float32)
    grad_back = inv_rms * scaled - residual * (inv_rms * inv_rms * inv_rms) * jnp.mean(
        scaled * residual, axis=1, keepdims=True
    )
    grad_gain = jnp.sum(grad_norm * residual * inv_rms, axis=0)
    return (grad_back, grad_gain)


def inner_params(weights):
    return (
        weights[6].astype(jnp.float32),
        weights[7].astype(jnp.float32),
        weights[8].astype(jnp.float32),
        weights[9].astype(jnp.float32),
        weights[10].astype(jnp.float32),
        weights[11].astype(jnp.float32),
    )


def mixer_forward(residual, weights, gain_vec):
    normed, inv_rms = rms_forward(residual, gain_vec)
    wide_rows = widen(normed)
    query_rows_all = jnp.dot(wide_rows, weights[0], preferred_element_type=jnp.float32).astype(
        jnp.bfloat16
    )
    key_matrix_rows = jnp.dot(wide_rows, weights[1], preferred_element_type=jnp.float32).astype(
        jnp.bfloat16
    )
    value_rows = jnp.dot(wide_rows, weights[2], preferred_element_type=jnp.float32).astype(
        jnp.bfloat16
    )
    gate_pre = jnp.dot(wide_rows, weights[3], preferred_element_type=jnp.float32)
    rate_logit = jnp.dot(wide_rows, weights[4], preferred_element_type=jnp.float32)
    inner_out = inner_chains(
        query_rows_all.astype(jnp.float32),
        key_matrix_rows.astype(jnp.float32),
        value_rows.astype(jnp.float32),
        rate_logit,
        *inner_params(weights)
    )
    mean_sum, square_sum = lax.psum(
        (jnp.sum(inner_out, axis=1), jnp.sum(inner_out * inner_out, axis=1)), "tensor"
    )
    mean_val = mean_sum / D
    inv_std = lax.rsqrt(square_sum / D - mean_val * mean_val + epsilon)
    unit_rows = (inner_out - mean_val[:, None]) * inv_std[:, None]
    post_weight = weights[12].astype(jnp.float32).reshape(-1)
    post_bias = weights[13].astype(jnp.float32).reshape(-1)
    post_out = unit_rows * post_weight + post_bias
    heads_out = (gelu_tanh(gate_pre) * post_out).astype(jnp.bfloat16)
    branch = narrow(heads_out, weights[5], residual.shape[0])
    saved = (
        residual,
        inv_rms,
        wide_rows,
        query_rows_all,
        key_matrix_rows,
        value_rows,
        gate_pre,
        rate_logit,
        unit_rows,
        inv_std,
        heads_out,
    )
    return (residual + branch, saved)


def mixer_backward(grad_res, saved, weights, gain_vec, row_count):
    (
        residual,
        inv_rms,
        wide_rows,
        query_rows_all,
        key_matrix_rows,
        value_rows,
        gate_pre,
        rate_logit,
        unit_rows,
        inv_std,
        heads_out,
    ) = saved
    grad_branch = widen_back(grad_res.astype(jnp.bfloat16))
    grad_heads = contract_cols(grad_branch, weights[5])
    grad_output = contract_rows(heads_out, grad_branch)
    post_weight = weights[12].astype(jnp.float32).reshape(-1)
    post_bias = weights[13].astype(jnp.float32).reshape(-1)
    post_out = unit_rows * post_weight + post_bias
    grad_gate = (grad_heads * post_out * activation_slope(gate_pre)).astype(jnp.bfloat16)
    grad_post = grad_heads * gelu_tanh(gate_pre)
    grad_post_gain = jnp.sum(grad_post * unit_rows, axis=0).reshape(weights[12].shape)
    grad_post_shift = jnp.sum(grad_post, axis=0).reshape(weights[13].shape)
    scaled = grad_post * post_weight
    first_sum, second_sum = lax.psum(
        (jnp.sum(scaled, axis=1), jnp.sum(scaled * unit_rows, axis=1)), "tensor"
    )
    grad_inner = inv_std[:, None] * (
        scaled - first_sum[:, None] / D - unit_rows * second_sum[:, None] / D
    )
    inner_again, pull_back = jax.vjp(
        inner_chains,
        query_rows_all.astype(jnp.float32),
        key_matrix_rows.astype(jnp.float32),
        value_rows.astype(jnp.float32),
        rate_logit,
        *inner_params(weights)
    )
    grads_inner = pull_back(grad_inner)
    grad_queries = grads_inner[0].astype(jnp.bfloat16)
    grad_keys = grads_inner[1].astype(jnp.bfloat16)
    grad_values = grads_inner[2].astype(jnp.bfloat16)
    grad_rates = grads_inner[3].astype(jnp.bfloat16)
    parts = (
        contract_rows(wide_rows, grad_queries),
        contract_rows(wide_rows, grad_keys),
        contract_rows(wide_rows, grad_values),
        contract_rows(wide_rows, grad_gate),
        contract_rows(wide_rows, grad_rates),
        grad_output,
        grads_inner[4],
        grads_inner[5],
        grads_inner[6],
        grads_inner[7],
        grads_inner[8],
        grads_inner[9],
        grad_post_gain,
        grad_post_shift,
    )
    grad_norm = narrow_back(
        (
            (grad_queries, weights[0]),
            (grad_keys, weights[1]),
            (grad_values, weights[2]),
            (grad_gate, weights[3]),
            (grad_rates, weights[4]),
        ),
        row_count,
    )
    grad_back, grad_gain = rms_backward(residual, inv_rms, gain_vec, grad_norm)
    return (grad_res + grad_back, parts, grad_gain)


def mlp_forward(residual, weights, gain_vec):
    normed, inv_rms = rms_forward(residual, gain_vec)
    wide_rows = widen(normed)
    gate_proj = jnp.dot(wide_rows, weights[14], preferred_element_type=jnp.float32)
    up_proj = jnp.dot(wide_rows, weights[15], preferred_element_type=jnp.float32)
    hidden = (jax.nn.silu(gate_proj) * up_proj).astype(jnp.bfloat16)
    branch = narrow(hidden, weights[16], residual.shape[0])
    return (residual + branch, (residual, inv_rms, wide_rows, gate_proj, up_proj, hidden))


def mlp_backward(grad_res, saved, weights, gain_vec, row_count):
    residual, inv_rms, wide_rows, gate_proj, up_proj, hidden = saved
    grad_branch = widen_back(grad_res.astype(jnp.bfloat16))
    grad_hidden = contract_cols(grad_branch, weights[16])
    grad_down = contract_rows(hidden, grad_branch)
    sig_vals = jax.nn.sigmoid(gate_proj)
    swish_vals = gate_proj * sig_vals
    grad_gate = (grad_hidden * up_proj * (sig_vals + swish_vals * (1.0 - sig_vals))).astype(
        jnp.bfloat16
    )
    grad_up = (grad_hidden * swish_vals).astype(jnp.bfloat16)
    parts = (contract_rows(wide_rows, grad_gate), contract_rows(wide_rows, grad_up), grad_down)
    grad_norm = narrow_back(((grad_gate, weights[14]), (grad_up, weights[15])), row_count)
    grad_back, grad_gain = rms_backward(residual, inv_rms, gain_vec, grad_norm)
    return (grad_res + grad_back, parts, grad_gain)


def per_device(
    hidden_in,
    cotangent,
    w_query,
    w_key,
    w_value,
    w_outgate,
    w_rate,
    w_output,
    init_first,
    init_first_bias,
    init_second,
    init_second_bias,
    inner_gain,
    inner_shift,
    post_gain,
    post_shift,
    mixer_gain,
    mlp_gain,
    w_gate,
    w_up,
    w_down,
):
    stacked = (
        w_query,
        w_key,
        w_value,
        w_outgate,
        w_rate,
        w_output,
        init_first,
        init_first_bias,
        init_second,
        init_second_bias,
        inner_gain,
        inner_shift,
        post_gain,
        post_shift,
        w_gate,
        w_up,
        w_down,
    )
    gain_mix, gain_mlp = (
        lax.all_gather(mixer_gain, ("dp", "tensor"), axis=1, tiled=True),
        lax.all_gather(mlp_gain, ("dp", "tensor"), axis=1, tiled=True),
    )
    row_count = hidden_in.shape[0]
    residual = hidden_in.astype(jnp.float32)
    fetched = []
    saved_all = []
    for layer_idx in range(LAYERS):
        weights = fetch_layer(stacked, layer_idx)
        residual, saved_mix = mixer_forward(residual, weights, gain_mix[layer_idx])
        residual, saved_mlp = mlp_forward(residual, weights, gain_mlp[layer_idx])
        fetched.append(weights)
        saved_all.append((saved_mix, saved_mlp))
    block_out = residual.astype(jnp.bfloat16)
    grad_res = cotangent.astype(jnp.float32)
    layer_grads = [None] * LAYERS
    mix_gain_grads = [None] * LAYERS
    mlp_gain_grads = [None] * LAYERS
    for layer_idx in reversed(range(LAYERS)):
        weights = fetch_layer(stacked, layer_idx)
        saved_mix, saved_mlp = saved_all[layer_idx]
        grad_res, mlp_parts, gain_two = mlp_backward(
            grad_res, saved_mlp, weights, gain_mlp[layer_idx], row_count
        )
        grad_res, mix_parts, gain_one = mixer_backward(
            grad_res, saved_mix, weights, gain_mix[layer_idx], row_count
        )
        parts = mix_parts + mlp_parts
        parts = reduce_grads(parts)
        layer_grads[layer_idx] = parts
        mix_gain_grads[layer_idx] = gain_one
        mlp_gain_grads[layer_idx] = gain_two
    merged = tuple(
        (
            jnp.stack([layer_grads[layer_pos][member] for layer_pos in range(LAYERS)])
            for member in range(17)
        )
    )
    grad_mixer_gain, grad_mlp_gain = (
        lax.psum_scatter(
            jnp.stack(mix_gain_grads), ("dp", "tensor"), scatter_dimension=1, tiled=True
        ),
        lax.psum_scatter(
            jnp.stack(mlp_gain_grads), ("dp", "tensor"), scatter_dimension=1, tiled=True
        ),
    )
    return (
        block_out,
        grad_res,
        merged[0],
        merged[1],
        merged[2],
        merged[3],
        merged[4],
        merged[5],
        merged[6],
        merged[7],
        merged[8],
        merged[9],
        merged[10],
        merged[11],
        merged[12],
        merged[13],
        grad_mixer_gain,
        grad_mlp_gain,
        merged[14],
        merged[15],
        merged[16],
    )


def solution(mesh):
    placed = (
        P(("dp", "tensor"), None),
        P(("dp", "tensor"), None),
        P(None, "dp", "tensor"),
        P(None, "dp", "tensor"),
        P(None, "dp", "tensor"),
        P(None, "dp", "tensor"),
        P(None, "dp", "tensor"),
        P(None, "tensor", "dp"),
        P(None, "tensor", None, "dp"),
        P(None, "tensor", "dp"),
        P(None, "tensor", "dp", None),
        P(None, "tensor", "dp"),
        P(None, "tensor", "dp"),
        P(None, "tensor", "dp"),
        P(None, "tensor", "dp"),
        P(None, "tensor", "dp"),
        P(None, ("dp", "tensor")),
        P(None, ("dp", "tensor")),
        P(None, "dp", "tensor"),
        P(None, "dp", "tensor"),
        P(None, "tensor", "dp"),
    )
    return jax.shard_map(
        per_device,
        mesh=mesh,
        in_specs=placed,
        out_specs=(
            P(("dp", "tensor"), None),
            P(("dp", "tensor"), None),
            P(None, "dp", "tensor"),
            P(None, "dp", "tensor"),
            P(None, "dp", "tensor"),
            P(None, "dp", "tensor"),
            P(None, "dp", "tensor"),
            P(None, "tensor", "dp"),
            P(None, "tensor", None, "dp"),
            P(None, "tensor", "dp"),
            P(None, "tensor", "dp", None),
            P(None, "tensor", "dp"),
            P(None, "tensor", "dp"),
            P(None, "tensor", "dp"),
            P(None, "tensor", "dp"),
            P(None, "tensor", "dp"),
            P(None, ("dp", "tensor")),
            P(None, ("dp", "tensor")),
            P(None, "dp", "tensor"),
            P(None, "dp", "tensor"),
            P(None, "tensor", "dp"),
        ),
        check_vma=False,
    )
```

profile of v0, /device:TPU:0, one launch (start us, length us, event | category | flops | bytes accessed | tf_op | source)
XLA Modules:
  0.0 6776.0 jit_solution(9436103819196557844)
XLA Ops:
  530.6 303.7 %while.469 = (s32[]{:T(128)}, f32[3,64,256]{2,1,0:T(8,128)S(1)}, f32[3,256]{1,0:T(4,128)S(1)}, f32[3,256,64]{1,2,0:T(8,128)S(1)}, f32[3,64]{1,0:T(4,128)S(1)}, /...) while((s32[]{:T(128)}, f32[3,64,256]{2,1,0:T(8,128)S(1)}, ...), condition=%wide.region_10.11_spmd, body=%wide.region_1.10_spmd.sunk | while | flops 73006144 | bytes 3841182 | solution.py:183
  1504.5 407.5 %while.471 = (s32[]{:T(128)}, f32[3,64,256]{2,1,0:T(8,128)S(1)}, f32[3,256]{1,0:T(4,128)S(1)}, f32[3,256,64]{1,2,0:T(8,128)S(1)}, f32[3,64]{1,0:T(4,128)S(1)}, /...) while((s32[]{:T(128)}, f32[3,64,256]{2,1,0:T(8,128)S(1)}, ...), condition=%wide.region_28.29_spmd, body=%wide.region_19.28_spmd.sunk | while | flops 73006144 | bytes 3909146 | solution.py:183
  2113.6 283.8 %while.473 = (s32[]{:T(128)}, f32[3,64,256]{2,1,0:T(8,128)S(1)}, f32[3,256]{1,0:T(4,128)S(1)}, f32[3,256,64]{1,2,0:T(8,128)S(1)}, f32[3,64]{1,0:T(4,128)S(1)}, /...) while((s32[]{:T(128)}, f32[3,64,256]{2,1,0:T(8,128)S(1)}, ...), condition=%wide.region_49.50_spmd, body=%wide.region_42.49_spmd.sunk | while | flops 47970928 | bytes 4751754 | solution.py:183
  2416.3 1361.3 %while.478 = (s32[]{:T(128)}, f32[3,64]{1,0:T(4,128)S(1)}, f32[3,64]{1,0:T(4,128)S(1)}, f32[3,64,256]{2,1,0:T(8,128)S(1)}, f32[3,256]{1,0:T(4,128)S(1)}, /*index...) while((s32[]{:T(128)}, f32[3,64]{1,0:T(4,128)S(1)}, ...), condition=%wide.region_82.83_spmd.clone, body=%wide.region_50.82_spmd.clone.sunk | while | flops 248723552 | bytes 13955192 | solution.py:183
  2470.6 113.9 %while.487 = (s32[]{:T(128)}, f32[3,64]{1,0:T(4,128)S(1)}, f32[3,64]{1,0:T(4,128)S(1)}, f32[3,64,256]{2,1,0:T(8,128)S(1)}, f32[3,256]{1,0:T(4,128)S(1)}, /*index...) while((s32[]{:T(128)}, f32[3,64]{1,0:T(4,128)S(1)}, ...), condition=%wide.region_81.81_spmd.clone, body=%wide.region_57.80_spmd.clone.sunk | while | flops 200751856 | bytes 9011680 | solution.py:181
  2640.7 113.9 %while.487 = (s32[]{:T(128)}, f32[3,64]{1,0:T(4,128)S(1)}, f32[3,64]{1,0:T(4,128)S(1)}, f32[3,64,256]{2,1,0:T(8,128)S(1)}, f32[3,256]{1,0:T(4,128)S(1)}, /*index...) while((s32[]{:T(128)}, f32[3,64]{1,0:T(4,128)S(1)}, ...), condition=%wide.region_81.81_spmd.clone, body=%wide.region_57.80_spmd.clone.sunk | while | flops 200751856 | bytes 9011680 | solution.py:181
  2810.9 113.9 %while.487 = (s32[]{:T(128)}, f32[3,64]{1,0:T(4,128)S(1)}, f32[3,64]{1,0:T(4,128)S(1)}, f32[3,64,256]{2,1,0:T(8,128)S(1)}, f32[3,256]{1,0:T(4,128)S(1)}, /*index...) while((s32[]{:T(128)}, f32[3,64]{1,0:T(4,128)S(1)}, ...), condition=%wide.region_81.81_spmd.clone, body=%wide.region_57.80_spmd.clone.sunk | while | flops 200751856 | bytes 9011680 | solution.py:181
  2981.1 113.9 %while.487 = (s32[]{:T(128)}, f32[3,64]{1,0:T(4,128)S(1)}, f32[3,64]{1,0:T(4,128)S(1)}, f32[3,64,256]{2,1,0:T(8,128)S(1)}, f32[3,256]{1,0:T(4,128)S(1)}, /*index...) while((s32[]{:T(128)}, f32[3,64]{1,0:T(4,128)S(1)}, ...), condition=%wide.region_81.81_spmd.clone, body=%wide.region_57.80_spmd.clone.sunk | while | flops 200751856 | bytes 9011680 | solution.py:181
  3151.3 113.9 %while.487 = (s32[]{:T(128)}, f32[3,64]{1,0:T(4,128)S(1)}, f32[3,64]{1,0:T(4,128)S(1)}, f32[3,64,256]{2,1,0:T(8,128)S(1)}, f32[3,256]{1,0:T(4,128)S(1)}, /*index...) while((s32[]{:T(128)}, f32[3,64]{1,0:T(4,128)S(1)}, ...), condition=%wide.region_81.81_spmd.clone, body=%wide.region_57.80_spmd.clone.sunk | while | flops 200751856 | bytes 9011680 | solution.py:181
  3321.4 113.9 %while.487 = (s32[]{:T(128)}, f32[3,64]{1,0:T(4,128)S(1)}, f32[3,64]{1,0:T(4,128)S(1)}, f32[3,64,256]{2,1,0:T(8,128)S(1)}, f32[3,256]{1,0:T(4,128)S(1)}, /*index...) while((s32[]{:T(128)}, f32[3,64]{1,0:T(4,128)S(1)}, ...), condition=%wide.region_81.81_spmd.clone, body=%wide.region_57.80_spmd.clone.sunk | while | flops 200751856 | bytes 9011680 | solution.py:181
  3491.6 113.9 %while.487 = (s32[]{:T(128)}, f32[3,64]{1,0:T(4,128)S(1)}, f32[3,64]{1,0:T(4,128)S(1)}, f32[3,64,256]{2,1,0:T(8,128)S(1)}, f32[3,256]{1,0:T(4,128)S(1)}, /*index...) while((s32[]{:T(128)}, f32[3,64]{1,0:T(4,128)S(1)}, ...), condition=%wide.region_81.81_spmd.clone, body=%wide.region_57.80_spmd.clone.sunk | while | flops 200751856 | bytes 9011680 | solution.py:181
  3661.8 113.9 %while.487 = (s32[]{:T(128)}, f32[3,64]{1,0:T(4,128)S(1)}, f32[3,64]{1,0:T(4,128)S(1)}, f32[3,64,256]{2,1,0:T(8,128)S(1)}, f32[3,256]{1,0:T(4,128)S(1)}, /*index...) while((s32[]{:T(128)}, f32[3,64]{1,0:T(4,128)S(1)}, ...), condition=%wide.region_81.81_spmd.clone, body=%wide.region_57.80_spmd.clone.sunk | while | flops 200751856 | bytes 9011680 | solution.py:181
  3948.6 280.4 %while.475 = (s32[]{:T(128)}, f32[3,64,256]{2,1,0:T(8,128)S(1)}, f32[3,256]{1,0:T(4,128)S(1)}, f32[3,256,64]{1,2,0:T(8,128)S(1)}, f32[3,64]{1,0:T(4,128)S(1)}, /...) while((s32[]{:T(128)}, f32[3,64,256]{2,1,0:T(8,128)S(1)}, ...), condition=%wide.region_98.99_spmd, body=%wide.region_91.98_spmd.sunk | while | flops 47970928 | bytes 4753566 | solution.py:183
  4252.4 1657.4 %while.481 = (s32[]{:T(128)}, f32[3,64]{1,0:T(4,128)}, f32[3,64]{1,0:T(4,128)}, f32[3,64,256]{2,1,0:T(8,128)S(1)}, f32[3,256]{1,0:T(4,128)}, /*index=5*/f32[3,25...) while((s32[]{:T(128)}, f32[3,64]{1,0:T(4,128)}, ...), condition=%wide.region_131.132_spmd.clone, body=%wide.region_99.131_spmd.clone.sunk | while | flops 248723552 | bytes 14048084 | solution.py:183
  4319.3 138.5 %while.489 = (s32[]{:T(128)}, f32[3,64]{1,0:T(4,128)S(1)}, f32[3,64]{1,0:T(4,128)S(1)}, f32[3,64,256]{2,1,0:T(8,128)S(1)}, f32[3,256]{1,0:T(4,128)}, /*index=5*/...) while((s32[]{:T(128)}, f32[3,64]{1,0:T(4,128)S(1)}, ...), condition=%wide.region_130.130_spmd.clone, body=%wide.region_106.129_spmd.clone.sunk | while | flops 200751856 | bytes 9042512 | solution.py:181
  4526.4 138.4 %while.489 = (s32[]{:T(128)}, f32[3,64]{1,0:T(4,128)S(1)}, f32[3,64]{1,0:T(4,128)S(1)}, f32[3,64,256]{2,1,0:T(8,128)S(1)}, f32[3,256]{1,0:T(4,128)}, /*index=5*/...) while((s32[]{:T(128)}, f32[3,64]{1,0:T(4,128)S(1)}, ...), condition=%wide.region_130.130_spmd.clone, body=%wide.region_106.129_spmd.clone.sunk | while | flops 200751856 | bytes 9042512 | solution.py:181
  4733.6 138.4 %while.489 = (s32[]{:T(128)}, f32[3,64]{1,0:T(4,128)S(1)}, f32[3,64]{1,0:T(4,128)S(1)}, f32[3,64,256]{2,1,0:T(8,128)S(1)}, f32[3,256]{1,0:T(4,128)}, /*index=5*/...) while((s32[]{:T(128)}, f32[3,64]{1,0:T(4,128)S(1)}, ...), condition=%wide.region_130.130_spmd.clone, body=%wide.region_106.129_spmd.clone.sunk | while | flops 200751856 | bytes 9042512 | solution.py:181
  4940.7 138.4 %while.489 = (s32[]{:T(128)}, f32[3,64]{1,0:T(4,128)S(1)}, f32[3,64]{1,0:T(4,128)S(1)}, f32[3,64,256]{2,1,0:T(8,128)S(1)}, f32[3,256]{1,0:T(4,128)}, /*index=5*/...) while((s32[]{:T(128)}, f32[3,64]{1,0:T(4,128)S(1)}, ...), condition=%wide.region_130.130_spmd.clone, body=%wide.region_106.129_spmd.clone.sunk | while | flops 200751856 | bytes 9042512 | solution.py:181
  5147.9 138.4 %while.489 = (s32[]{:T(128)}, f32[3,64]{1,0:T(4,128)S(1)}, f32[3,64]{1,0:T(4,128)S(1)}, f32[3,64,256]{2,1,0:T(8,128)S(1)}, f32[3,256]{1,0:T(4,128)}, /*index=5*/...) while((s32[]{:T(128)}, f32[3,64]{1,0:T(4,128)S(1)}, ...), condition=%wide.region_130.130_spmd.clone, body=%wide.region_106.129_spmd.clone.sunk | while | flops 200751856 | bytes 9042512 | solution.py:181
  5355.0 138.4 %while.489 = (s32[]{:T(128)}, f32[3,64]{1,0:T(4,128)S(1)}, f32[3,64]{1,0:T(4,128)S(1)}, f32[3,64,256]{2,1,0:T(8,128)S(1)}, f32[3,256]{1,0:T(4,128)}, /*index=5*/...) while((s32[]{:T(128)}, f32[3,64]{1,0:T(4,128)S(1)}, ...), condition=%wide.region_130.130_spmd.clone, body=%wide.region_106.129_spmd.clone.sunk | while | flops 200751856 | bytes 9042512 | solution.py:181
  5562.2 138.4 %while.489 = (s32[]{:T(128)}, f32[3,64]{1,0:T(4,128)S(1)}, f32[3,64]{1,0:T(4,128)S(1)}, f32[3,64,256]{2,1,0:T(8,128)S(1)}, f32[3,256]{1,0:T(4,128)}, /*index=5*/...) while((s32[]{:T(128)}, f32[3,64]{1,0:T(4,128)S(1)}, ...), condition=%wide.region_130.130_spmd.clone, body=%wide.region_106.129_spmd.clone.sunk | while | flops 200751856 | bytes 9042512 | solution.py:181
  5769.4 138.4 %while.489 = (s32[]{:T(128)}, f32[3,64]{1,0:T(4,128)S(1)}, f32[3,64]{1,0:T(4,128)S(1)}, f32[3,64,256]{2,1,0:T(8,128)S(1)}, f32[3,256]{1,0:T(4,128)}, /*index=5*/...) while((s32[]{:T(128)}, f32[3,64]{1,0:T(4,128)S(1)}, ...), condition=%wide.region_130.130_spmd.clone, body=%wide.region_106.129_spmd.clone.sunk | while | flops 200751856 | bytes 9042512 | solution.py:181
  6041.2 81.0 %all-reduce.27.cloned.1.call-done = (bf16[3,64,256]{1,0,2:T(4,128)(2,1)}, bf16[3,64,256]{1,0,2:T(4,128)(2,1)}, bf16[3,256,64]{2,0,1:T(4,128)(2,1)}, bf16[3,256,64]{2,0,1:T(4,128)(2,1)}) async-done(((bf16[3,64,256]{1,0,2:T(4,128)(2,1)}, bf16[3,64,256]{1,0,2:T(4,128)(2,1)}, bf16[3,256,64]{2,0,1:T(4,128)(2,1)}, bf16[3,256,64]{2,0,1:T(4,128)(2,1)}), (bf16[3,64,256]{1,0,2:T(4,128)(2,1)}, ...) | async-done | bytes 393232
  6125.4 60.8 reduce-scatter.101.cloned.1.call-done
  6187.8 62.1 reduce-scatter.83.cloned.1.call-done
  6249.9 63.6 reduce-scatter.81.cloned.1.call-done
  6314.9 62.2 reduce-scatter.79.cloned.1.call-done
  6377.1 63.7 reduce-scatter.77.cloned.1.call-done
  6442.4 62.0 reduce-scatter.75.cloned.1.call-done
  6504.4 63.7 reduce-scatter.73.cloned.1.call-done
  6569.6 62.2 reduce-scatter.71.cloned.1.call-done
  6631.8 63.6 reduce-scatter.69.cloned.1.call-done
  (22163 shorter events, 7984.1 us)
Async XLA Ops:
  7.2 496.2 %all-gather.45.cloned.1.call-start = ((), (), s32[]{:S(2)}) async-start(), calls=%async_computation.28 | async-start | bytes 1966080 | tf_op jit(solution)/shard_map/all_gather | solution.py:208
  54.3 837.1 %reduce-scatter.53.cloned.1.call-start = ((), (), s32[]{:S(2)}) async-start(), calls=%async_computation.29 | async-start | bytes 1966080 | tf_op jit(solution)/shard_map/reduce_scatter | solution.py:220
  854.4 139.7 %all-gather.47.cloned.1.call-start = ((), (), s32[]{:S(2)}) async-start(), calls=%async_computation.30 | async-start | bytes 1966080 | tf_op jit(solution)/shard_map/all_gather | solution.py:208
  895.2 133.5 %reduce-scatter.55.cloned.1.call-start = ((), (), s32[]{:S(2)}) async-start(), calls=%async_computation.31 | async-start | bytes 1966080 | tf_op jit(solution)/shard_map/reduce_scatter | solution.py:220
  1002.5 470.5 %all-gather.49.cloned.1.call-start = ((), (), s32[]{:S(2)}) async-start(), calls=%async_computation.32 | async-start | bytes 1966080 | tf_op jit(solution)/shard_map/all_gather | solution.py:208
  1031.5 931.3 %reduce-scatter.57.cloned.1.call-start = ((), (), s32[]{:S(2)}) async-start(), calls=%async_computation.33 | async-start | bytes 1966080 | tf_op jit(solution)/shard_map/reduce_scatter | solution.py:220
  1934.1 129.7 %all-gather.51.cloned.1.call-start = ((), (), s32[]{:S(2)}) async-start(), calls=%async_computation.34 | async-start | bytes 1966080 | tf_op jit(solution)/shard_map/all_gather | solution.py:208
  1966.8 140.8 %reduce-scatter.61.cloned.1.call-start = ((), (), s32[]{:S(2)}) async-start(), calls=%async_computation.37 | async-start | bytes 1966080 | tf_op jit(solution)/shard_map/reduce_scatter | solution.py:237
  2079.2 318.2 %all-gather.55.cloned.1.call-start = ((), (), s32[]{:S(2)}) async-start(), calls=%async_computation.38 | async-start | bytes 1966080 | tf_op jit(solution)/shard_map/all_gather | solution.py:212
  2110.7 1716.7 %reduce-scatter.63.cloned.1.call-start = ((), (), s32[]{:S(2)}) async-start(), calls=%async_computation.39 | async-start | bytes 1966080 | tf_op jit(solution)/shard_map/reduce_scatter | solution.py:237
  3889.2 343.4 %all-gather.59.cloned.1.call-start = ((), (), s32[]{:S(2)}) async-start(), calls=%async_computation.42 | async-start | bytes 1966080 | tf_op jit(solution)/shard_map/all_gather | solution.py:212
  3921.6 2049.8 %reduce-scatter.107.cloned.1.call-start = ((), (), s32[]{:S(2)}) async-start(), calls=%async_computation.63 | async-start | bytes 73728
  3922.5 2049.8 %reduce-scatter.99.cloned.1.call-start = ((), (), s32[]{:S(2)}) async-start(), calls=%async_computation.59 | async-start | bytes 221184
  3923.7 2049.3 %reduce-scatter.103.cloned.1.call-start = ((), (), s32[]{:S(2)}) async-start(), calls=%async_computation.61 | async-start | bytes 442368
  3926.2 2047.8 %reduce-scatter.95.cloned.1.call-start = ((), (), s32[]{:S(2)}) async-start(), calls=%async_computation.57 | async-start | bytes 884736 | tf_op jit(solution)/shard_map/reduce_scatter | solution.py:317
  3930.1 2043.9 %reduce-scatter.93.cloned.1.call-start = ((), (), s32[]{:S(2)}) async-start(), calls=%async_computation.56 | async-start | bytes 884736 | tf_op jit(solution)/shard_map/reduce_scatter | solution.py:317
  3933.4 2042.4 %reduce-scatter.91.cloned.1.call-start = ((), (), s32[]{:S(2)}) async-start(), calls=%async_computation.55 | async-start | bytes 884736 | tf_op jit(solution)/shard_map/reduce_scatter | solution.py:314
  3936.9 2038.9 %reduce-scatter.89.cloned.1.call-start = ((), (), s32[]{:S(2)}) async-start(), calls=%async_computation.54 | async-start | bytes 884736 | tf_op jit(solution)/shard_map/reduce_scatter | solution.py:314
  3940.4 2037.1 %reduce-scatter.87.cloned.1.call-start = ((), (), s32[]{:S(2)}) async-start(), calls=%async_computation.53 | async-start | bytes 884736 | tf_op jit(solution)/shard_map/reduce_scatter | solution.py:311
  3945.7 2031.8 %reduce-scatter.85.cloned.1.call-start = ((), (), s32[]{:S(2)}) async-start(), calls=%async_computation.52 | async-start | bytes 884736 | tf_op jit(solution)/shard_map/reduce_scatter | solution.py:311
  4232.5 1787.5 %reduce-scatter.105.cloned.1.call-start = ((), (), s32[]{:S(2)}) async-start(), calls=%async_computation.62 | async-start | bytes 73728
  5914.4 207.9 %all-reduce.27.cloned.1.call-start = ((), (), s32[]{:S(2)}) async-start(), calls=%async_computation.64 | async-start | bytes 2097152
  5918.0 268.2 %reduce-scatter.101.cloned.1.call-start = ((), (), s32[]{:S(2)}) async-start(), calls=%async_computation.60 | async-start | bytes 442368
  5921.1 328.8 %reduce-scatter.83.cloned.1.call-start = ((), (), s32[]{:S(2)}) async-start(), calls=%async_computation.51 | async-start | bytes 442368 | tf_op jit(solution)/shard_map/reduce_scatter | solution.py:278
  5923.9 389.5 %reduce-scatter.81.cloned.1.call-start = ((), (), s32[]{:S(2)}) async-start(), calls=%async_computation.50 | async-start | bytes 442368 | tf_op jit(solution)/shard_map/reduce_scatter | solution.py:278
  5926.4 450.7 %reduce-scatter.79.cloned.1.call-start = ((), (), s32[]{:S(2)}) async-start(), calls=%async_computation.49 | async-start | bytes 442368 | tf_op jit(solution)/shard_map/reduce_scatter | solution.py:275
  5929.6 511.3 %reduce-scatter.77.cloned.1.call-start = ((), (), s32[]{:S(2)}) async-start(), calls=%async_computation.48 | async-start | bytes 442368 | tf_op jit(solution)/shard_map/reduce_scatter | solution.py:275
  5935.1 569.3 %reduce-scatter.75.cloned.1.call-start = ((), (), s32[]{:S(2)}) async-start(), calls=%async_computation.47 | async-start | bytes 442368 | tf_op jit(solution)/shard_map/reduce_scatter | solution.py:272
  5938.1 630.0 %reduce-scatter.73.cloned.1.call-start = ((), (), s32[]{:S(2)}) async-start(), calls=%async_computation.46 | async-start | bytes 442368 | tf_op jit(solution)/shard_map/reduce_scatter | solution.py:272
  5945.4 686.4 %reduce-scatter.71.cloned.1.call-start = ((), (), s32[]{:S(2)}) async-start(), calls=%async_computation.45 | async-start | bytes 442368 | tf_op jit(solution)/shard_map/reduce_scatter | solution.py:269
  5948.3 747.1 %reduce-scatter.69.cloned.1.call-start = ((), (), s32[]{:S(2)}) async-start(), calls=%async_computation.44 | async-start | bytes 442368 | tf_op jit(solution)/shard_map/reduce_scatter | solution.py:269
  5961.8 763.2 %reduce-scatter.67.cloned.1.call-start = ((), (), s32[]{:S(2)}) async-start(), calls=%async_computation.43 | async-start | bytes 1966080 | tf_op jit(solution)/shard_map/reduce_scatter | solution.py:237
  (508 other events, 23481.1 us)
Sparse Core Ops, SparseCore 0:
  854.5 24.5 reduce-scatter.52
  1002.6 26.0 reduce-scatter.54
  1934.2 28.6 reduce-scatter.56
  1966.2 19.6 all-gather.50
  2079.3 28.2 reduce-scatter.60
  2110.8 19.6 all-gather.54
  3798.2 29.2 reduce-scatter.62
  3830.0 28.1 reduce-scatter.58
  3861.0 19.6 all-gather.56
  3889.3 28.1 reduce-scatter.64
  3945.6 61.4 reduce-scatter.106
  4011.2 60.3 reduce-scatter.98
  4075.6 60.7 reduce-scatter.102
  4140.0 61.4 reduce-scatter.94
  4204.6 61.4 reduce-scatter.92
  4269.8 61.6 reduce-scatter.90
  4334.9 61.5 reduce-scatter.88
  4400.1 61.7 reduce-scatter.86
  4465.0 61.7 reduce-scatter.84
  5913.2 62.3 reduce-scatter.104
  5979.6 60.1 reduce-scatter.96
  6044.0 78.1 all-reduce.26
  6125.5 60.5 reduce-scatter.100
  6189.4 60.3 reduce-scatter.82
  6253.0 60.4 reduce-scatter.80
  6316.7 60.3 reduce-scatter.78
  6380.4 60.3 reduce-scatter.76
  6444.0 60.3 reduce-scatter.74
  6507.7 60.3 reduce-scatter.72
  6571.4 60.4 reduce-scatter.70
  6634.9 60.4 reduce-scatter.68
  6697.8 27.1 reduce-scatter.66
  (5 shorter events, 91.8 us)
where the time goes:
time: 6820 us; the launch traced here: 6780 us
  matrix products  2320 us (34%)
  local copies, waits for them, and re-layouts  1440 us (21%)
  blocking collectives  1240 us (18%)
  waiting for transfers between devices  875 us (13%)
  other arithmetic  771 us (11%)
  loops' own time  111 us (2%)
    squeeze x736, local copies, waits for them, and re-layouts, inner_chains(): lax.scan(jax.checkpoint(grouped), state_now, (arrange(query_rows_all), ar...  569 us
    dynamic_update_slice x640, local copies, waits for them, and re-layouts, inner_chains(): lax.scan(jax.checkpoint(grouped), state_now, (arrange(query_rows_all), ar...  359 us
    dot_general x768, matrix products, inner_step(): jnp.einsum('uez,uzy->uey', activation_hidden, output_weight, precision=pr...  285 us
    dot_general x640, matrix products, inner_step(): jnp.einsum('ki,kir,kil->krl', final_row_slice, key_matrix_rows, gradient_...  263 us
    dot_general x640, matrix products, inner_step(): jnp.einsum('ae,aet,aeu->atu', final_row_slice, activation_hidden, gradien...  259 us
    dot_general x768, matrix products, inner_step(): jnp.einsum('qml,qrl->qmr', gradient_output_weight, output_weight, precisi...  224 us
    dot_general x768, matrix products, inner_step(): jnp.einsum('umr,urt->umt', key_matrix_rows, hidden_weight, precision=prec...  192 us
    squeeze x256, other arithmetic, inner_step(): final_row_slice = inner_rate_matrix[:, -1, :]  166 us

commit v1 on v0

v1 whole, which is shorter than its diff:
```python
import functools

import jax
import jax.numpy as jnp
from jax import lax
from jax.experimental import pallas as pl
from jax.sharding import PartitionSpec as P
from jax.experimental.pallas import tpu as pltpu

F32 = jnp.float32
BF = jnp.bfloat16
HD = 64
INNER = 256
CS = 16
CH = 128
STEPS = CH // CS
PACK = 640
EPS = 1e-6
K0 = 0.7978845608028654
K1 = 0.7978845608028654 * 0.044715


def mm(a, b, ca, cb):
    return lax.dot_general(
        a.astype(BF), b.astype(BF), (((ca,), (cb,)), ((), ())), preferred_element_type=F32
    )


def nn(a, b):
    return mm(a, b, 1, 0)


def nt(a, b):
    return mm(a, b, 1, 1)


def tn(a, b):
    return mm(a, b, 0, 0)


def gelu_two(z):
    zz = z * z
    t = jnp.tanh(z * (K0 + K1 * zz))
    half = 0.5 + 0.5 * t
    return z * half, half + 0.5 * z * (1.0 - t * t) * (K0 + 3.0 * K1 * zz)


def gelu_three(z):
    zz = z * z
    t = jnp.tanh(z * (K0 + K1 * zz))
    half = 0.5 + 0.5 * t
    rest = 1.0 - t * t
    p = K0 + 3.0 * K1 * zz
    return z * half, half + 0.5 * z * rest * p, rest * (p + 3.0 * K1 * zz - z * t * p * p)


def mean(x):
    return jnp.sum(x, axis=1, keepdims=True) * (1.0 / HD)


def masks():
    row = lax.broadcasted_iota(jnp.int32, (CH, CH), 0)
    col = lax.broadcasted_iota(jnp.int32, (CH, CH), 1)
    row_block, col_block = row // CS, col // CS
    inside = (row_block == col_block) & (col <= row)
    earlier = col_block < row_block
    own = 1.0 / ((row % CS) + 1).astype(F32)
    coef = jnp.where(earlier, 1.0 / CS, jnp.where(inside, own, 0.0))
    return coef, jnp.where(earlier, 1.0, 0.0)


def split_pack(pack, heads):
    wide = pack.astype(F32)
    first = wide[:, :CH]
    turned = first.T
    rates_row = [jax.nn.sigmoid(turned[h : h + 1]) * (1.0 / HD) for h in range(heads)]
    rates_col = [jax.nn.sigmoid(first[:, h : h + 1]) * (1.0 / HD) for h in range(heads)]
    off = HD
    xq = [wide[:, off + HD * h : off + HD * (h + 1)] for h in range(heads)]
    off += HD * heads
    xk = [wide[:, off + HD * h : off + HD * (h + 1)] for h in range(heads)]
    off += HD * heads
    xv = [wide[:, off + HD * h : off + HD * (h + 1)] for h in range(heads)]
    return xq, xk, xv, rates_row, rates_col


def forward_kernel(
    heads, place_ref, pack_ref, w1_ref, b1_ref, w2_ref, b2_ref, g_ref, h_ref,
    o_ref, z1_ref, a_ref, z1b_ref, c_ref, z2b_ref, w1s_ref, w2s_ref,
    w1, b1, w2, b2, pre, kke, cc, ecol, g1buf, g2buf, x2buf,
):
    H = range(heads)

    @pl.when(pl.program_id(0) == 0)
    def _():
        w1[...] = w1_ref[...]
        b1[...] = b1_ref[...]
        w2[...] = w2_ref[...]
        b2[...] = b2_ref[...]
        g1buf[...] = jnp.zeros_like(g1buf)

    coef, before = masks()
    xq, xk, xv, rrow, rcol = split_pack(pack_ref[...], heads)
    b2_start = [b2[h] for h in H]
    mcc = []
    for h in H:
        pre[h] = nn(xk[h], w1[h]) + b1[h]
        kke[h] = ((nt(xk[h], xk[h]) + 1.0) * (before * (rrow[h] * (1.0 / CS)))).astype(BF)
        g, sh = g_ref[h], h_ref[h]
        cval = (sh - xv[h] + xk[h]) * g
        cc[h] = cval
        mcc.append(mean(cval))
        ecol[h] = jnp.broadcast_to(rcol[h] * (1.0 / CS), (CH, HD))
        w1s_ref[0, h] = w1[h].astype(w1s_ref.dtype)
    ma = [mean(g_ref[h] * g_ref[h]) for h in H]
    w2v = [w2[h] for h in H]
    b2v = list(b2_start)
    for i in range(STEPS):
        rows = slice(CS * i, CS * (i + 1))
        z1 = [pre[h, rows, :] for h in H]
        if i >= 2:
            z1 = [z1[h] - nn(kke[h, rows, : CS * (i - 1)], g1buf[h, : CS * (i - 1), :]) for h in H]
        if i >= 1:
            z1 = [z1[h] - nn(kke[h, rows, :][:, CS * (i - 1) : CS * i], g1buf[h, CS * (i - 1) : CS * i, :]) for h in H]
        xd = [gelu_two(z1[h]) for h in H]
        x2b = [xd[h][0].astype(BF) for h in H]
        w2b = [w2v[h].astype(BF) for h in H]
        c = [nt(x2b[h], w2b[h]) + b2v[h] for h in H]
        g2 = []
        for h in H:
            g = g_ref[h]
            a = g * g
            ca = c[h] * a
            cch = cc[h, rows, :]
            mc = mcc[h][rows]
            mu, q1, q2, q3, q4 = mean(c[h]), mean(c[h] * c[h]), mean(ca), mean(ca * c[h]), mean(c[h] * cch)
            s = lax.rsqrt(q1 - mu * mu + EPS)
            m1 = s * (q2 - mu * ma[h]) + mc
            m2 = s * (s * (q3 - mu * (2.0 * q2 - mu * ma[h])) + (q4 - mu * mc))
            c[h] = c[h] - mu
            g2.append(s * (c[h] * (s * (a - m2)) + cch - m1))
        av = [nn(g2[h], w2b[h]) for h in H]
        g1 = [av[h] * xd[h][1] for h in H]
        for h in H:
            g1buf[h, rows, :] = g1[h].astype(BF)
            g2buf[h, rows, :] = g2[h].astype(BF)
            x2buf[h, rows, :] = x2b[h]
            w2s_ref[i, h] = w2b[h].astype(w2s_ref.dtype)
            z1_ref[rows, INNER * h : INNER * (h + 1)] = z1[h]
            a_ref[rows, INNER * h : INNER * (h + 1)] = av[h]
            c_ref[h, rows, :] = c[h]
            eg2 = ecol[h, rows, :] * g2[h]
            w2v[h] = w2v[h] - tn(eg2, x2b[h])
            b2v[h] = b2v[h] - jnp.sum(eg2, axis=0, keepdims=True)
    for h in H:
        mask = coef * rrow[h]
        g1, g2, x2 = g1buf[h], g2buf[h], x2buf[h]
        z1b = nn(xq[h], w1[h]) + b1[h] - nn((nt(xq[h], xk[h]) + 1.0) * mask, g1)
        z1b_ref[:, INNER * h : INNER * (h + 1)] = z1b
        x2q = jax.nn.gelu(z1b, approximate=True).astype(BF)
        z2b = nt(x2q, w2[h]) + b2_start[h] - nn((nt(x2q, x2) + 1.0) * mask, g2)
        z2b = z2b - mean(z2b)
        z2b_ref[h] = z2b
        unit = z2b * lax.rsqrt(mean(z2b * z2b) + EPS)
        o_ref[:, HD * h : HD * (h + 1)] = xq[h] + unit * g_ref[h] + h_ref[h]
        ek = ecol[h] * xk[h]
        w1[h] = w1[h] - tn(ek, g1)
        b1[h] = b1[h] - jnp.sum(ecol[h][:, :1] * g1.astype(F32), axis=0, keepdims=True)
        w2[h] = w2v[h]
        b2[h] = b2v[h]


def forward_call(place, pack, w1, b1, w2, b2, g, h):
    heads = w1.shape[0]
    rows = pack.shape[0]
    chunks = rows // CH
    per_block = chunks // 4

    def spot(c, place):
        return ((c // per_block) ^ place[0]) * per_block + c % per_block

    def whole(*shape):
        return pl.BlockSpec(shape, lambda c, place: (0,) * len(shape))

    def moved(n):
        return pl.BlockSpec((CH, n), lambda c, place: (spot(c, place), 0))

    def kept(n):
        return pl.BlockSpec((CH, n), lambda c, place: (c, 0))

    by_head = pl.BlockSpec((heads, CH, HD), lambda c, place: (0, c, 0))
    sds = jax.ShapeDtypeStruct
    return pl.pallas_call(
        functools.partial(forward_kernel, heads),
        grid_spec=pltpu.PrefetchScalarGridSpec(
            num_scalar_prefetch=1,
            grid=(chunks,),
            in_specs=[
                moved(PACK),
                whole(heads, HD, INNER),
                whole(heads, 1, INNER),
                whole(heads, HD, INNER),
                whole(heads, 1, HD),
                whole(heads, 1, HD),
                whole(heads, 1, HD),
            ],
            out_specs=[
                moved(heads * HD),
                kept(heads * INNER),
                kept(heads * INNER),
                kept(heads * INNER),
                by_head,
                by_head,
                pl.BlockSpec((1, heads, HD, INNER), lambda c, place: (c, 0, 0, 0)),
                pl.BlockSpec((STEPS, heads, HD, INNER), lambda c, place: (c, 0, 0, 0)),
            ],
            scratch_shapes=[
                pltpu.VMEM((heads, HD, INNER), F32),
                pltpu.VMEM((heads, 1, INNER), F32),
                pltpu.VMEM((heads, HD, INNER), F32),
                pltpu.VMEM((heads, 1, HD), F32),
                pltpu.VMEM((heads, CH, INNER), F32),
                pltpu.VMEM((heads, CH, CH), BF),
                pltpu.VMEM((heads, CH, HD), F32),
                pltpu.VMEM((heads, CH, HD), F32),
                pltpu.VMEM((heads, CH, INNER), BF),
                pltpu.VMEM((heads, CH, HD), BF),
                pltpu.VMEM((heads, CH, INNER), BF),
            ],
        ),
        out_shape=[
            sds((rows, heads * HD), F32),
            sds((rows, heads * INNER), F32),
            sds((rows, heads * INNER), F32),
            sds((rows, heads * INNER), F32),
            sds((heads, rows, HD), F32),
            sds((heads, rows, HD), F32),
            sds((chunks, heads, HD, INNER), BF),
            sds((chunks * STEPS, heads, HD, INNER), BF),
        ],
        compiler_params=pltpu.CompilerParams(vmem_limit_bytes=40 * 2**20),
        cost_estimate=pl.CostEstimate(flops=65 * 10**9, bytes_accessed=25 * 10**6, transcendentals=0),
    )(place, pack, w1, b1, w2, b2, g, h)


def backward_kernel(
    heads, place_ref, pack_ref, do_ref, z1_ref, a_ref, z1b_ref, c_ref, z2b_ref, w1s_ref, w2s_ref, g_ref, h_ref,
    dpack_ref, dw1, db1, dw2, db2, dg_ref, dh_ref,
    dg1b, dg2b, dx2b, d1v, ad2, g2v, kkt, dz1buf, k1v, k2v, dyv, ecol, x2buf,
):
    H = range(heads)

    @pl.when(pl.program_id(0) == 0)
    def _():
        dw1[...] = jnp.zeros_like(dw1)
        db1[...] = jnp.zeros_like(db1)
        dw2[...] = jnp.zeros_like(dw2)
        db2[...] = jnp.zeros_like(db2)
        dg_ref[...] = jnp.zeros_like(dg_ref)
        dh_ref[...] = jnp.zeros_like(dh_ref)
        dz1buf[...] = jnp.zeros_like(dz1buf)

    coef, before = masks()
    xq, xk, xv, rrow, rcol = split_pack(pack_ref[...], heads)
    uv, yv, st = [], [], []
    dxq, dxk, dr_row = [], [], []
    dw1_out, db1_out, dw2_out, db2_out = [], [], [], []
    x2_all, g1_all, g2_all, ccv = [], [], [], []
    for h in H:
        wide = slice(INNER * h, INNER * (h + 1))
        g, sh = g_ref[h], h_ref[h]
        a = g * g
        x2, d1, d2 = gelu_three(z1_ref[:, wide])
        av = a_ref[:, wide]
        d1v[h] = d1
        ad2[h] = av * d2
        x2 = x2.astype(BF)
        x2buf[h] = x2
        g1 = (av * d1).astype(BF)
        c = c_ref[h]
        cch = (sh - xv[h] + xk[h]) * g
        ca = c * a
        q1, q2, q3, q4 = mean(c * c), mean(ca), mean(ca * c), mean(c * cch)
        s = lax.rsqrt(q1 + EPS)
        m1 = s * q2 + mean(cch)
        m2 = s * (s * q3 + q4)
        u = c * s
        y = u * a + cch
        g2 = s * (y - m1 - u * m2)
        uv.append(u)
        yv.append(y)
        st.append((s, m2, s * q2, s * s * q3, mean(y), mean(a)))
        g2v[h] = g2
        x2_all.append(x2)
        g1_all.append(g1)
        g2_all.append(g2)
        ccv.append(cch)
        ecol[h] = jnp.broadcast_to(rcol[h] * (1.0 / CS), (CH, HD))
        do = do_ref[:, HD * h : HD * (h + 1)].astype(F32)
        z2b = z2b_ref[h]
        sb = lax.rsqrt(mean(z2b * z2b) + EPS)
        ub = z2b * sb
        dog = do * g
        dg_ref[h] += jnp.sum(do * ub, axis=0, keepdims=True)
        dh_ref[h] += jnp.sum(do, axis=0, keepdims=True)
        dz2b = sb * (dog - mean(dog) - ub * mean(dog * ub))
        x2q, d1b = gelu_two(z1b_ref[:, wide])
        x2q = x2q.astype(BF)
        w2_start, w1_start = w2s_ref[0, h], w1s_ref[0, h]
        mask = coef * rrow[h]
        p = nt(x2q, x2) + 1.0
        dm2 = -nt(dz2b, g2)
        dp = (mask * dm2).astype(BF)
        dg2b[h] = -tn(mask * p, dz2b)
        dx2b[h] = tn(dp, x2q)
        dx2q = nn(dz2b, w2_start) + nn(dp, x2)
        dz1b = dx2q * d1b
        sc = nt(xq[h], xk[h]) + 1.0
        dm1 = -nt(dz1b, g1)
        ds = (mask * dm1).astype(BF)
        kk = nt(xk[h], xk[h]) + 1.0
        kkt[h] = (kk * before.T).astype(BF)
        k1 = nn(xk[h], dw1[h]) + db1[h]
        k1v[h] = k1
        dg1b[h] = -tn(mask * sc, dz1b)
        dr_row.append(jnp.sum(coef * (sc * dm1 + p * dm2), axis=0, keepdims=True))
        dxq.append(do + nt(dz1b, w1_start) + nn(ds, xk[h]))
        dxk.append(tn(ds, xq[h]) - nt((rcol[h] * (1.0 / CS)) * g1.astype(F32), dw1[h]))
        dw1_out.append(tn(xq[h], dz1b))
        db1_out.append(jnp.sum(dz1b, axis=0, keepdims=True))
        dw2_out.append(tn(dz2b, x2q))
        db2_out.append(jnp.sum(dz2b, axis=0, keepdims=True))
    d2 = [dw2[h] for h in H]
    e2 = [db2[h] for h in H]
    for i in reversed(range(STEPS)):
        rows = slice(CS * i, CS * (i + 1))
        k1 = [k1v[h, rows, :] for h in H]
        if i < STEPS - 2:
            k1 = [k1[h] + nn(kkt[h, rows, :][:, CS * (i + 2) :], dz1buf[h, CS * (i + 2) :, :]) for h in H]
        if i < STEPS - 1:
            k1 = [k1[h] + nn(kkt[h, rows, :][:, CS * (i + 1) : CS * (i + 2)], dz1buf[h, CS * (i + 1) : CS * (i + 2), :]) for h in H]
        dg1 = [dg1b[h, rows, :] - ecol[h, rows, :][:, :1] * k1[h] for h in H]
        da = [(dg1[h] * d1v[h, rows, :]).astype(BF) for h in H]
        d2b = [d2[h].astype(BF) for h in H]
        w2i = [w2s_ref[i, h] for h in H]
        g2 = [g2v[h, rows, :] for h in H]
        k2 = [nt(x2buf[h, rows, :], d2b[h]) + e2[h] for h in H]
        dg2 = [dg2b[h, rows, :] - ecol[h, rows, :] * k2[h] + nt(da[h], w2i[h]) for h in H]
        l2 = [dx2b[h, rows, :] - nn(ecol[h, rows, :] * g2[h], d2b[h]) for h in H]
        dz2 = []
        for h in H:
            g = g_ref[h]
            a = g * g
            s, m2, mau, mauu, my = (q[rows] for q in st[h][:5])
            ma = st[h][5]
            u, y = uv[h][rows], yv[h][rows]
            dv = dg2[h]
            dva = dv * a
            n1, n2, n3, n4, n5 = mean(dv), mean(dv * u), mean(dv * g2[h]), mean(dva * u), mean(dva)
            dy = s * (dv - n1 - u * n2)
            muu = s * (n4 - n1 * mau - n2 * (mauu + 2.0 * m2))
            mu = s * (n5 - n1 * (ma + m2) - n2 * (mau + my))
            dz2.append(s * (dy * a - (s * m2) * dv - (s * n2) * y - mu - u * (muu + n3)))
            dyv[h, rows, :] = dy
            k2v[h, rows, :] = k2[h]
        dx2 = [l2[h] + nn(dz2[h], w2i[h]) for h in H]
        dz1 = [dx2[h] * d1v[h, rows, :] + dg1[h] * ad2[h, rows, :] for h in H]
        for h in H:
            dz1buf[h, rows, :] = dz1[h].astype(BF)
            d2[h] = d2[h] + tn(
                jnp.concatenate([g2[h], dz2[h]], axis=0), jnp.concatenate([da[h], x2buf[h, rows, :]], axis=0)
            )
            e2[h] = e2[h] + jnp.sum(dz2[h], axis=0, keepdims=True)
    dq_out, dk_out, dv_out, de_col = [], [], [], []
    for h in H:
        g = g_ref[h]
        dz1 = dz1buf[h]
        dy = dyv[h]
        g1, g2 = g1_all[h], g2_all[h]
        k1 = k1v[h] + nn(kkt[h], dz1)
        de_col.append(jnp.sum(g1.astype(F32) * k1, axis=1, keepdims=True) + jnp.sum(g2 * k2v[h], axis=1, keepdims=True))
        dkk = (-nt(dz1, g1) * (before * (rrow[h] * (1.0 / CS)))).astype(BF)
        dyg = dy * g
        dk = dxk[h] + nn(dkk, xk[h]) + tn(dkk, xk[h]) + nt(dz1, w1s_ref[0, h]) + dyg
        dg_ref[h] += jnp.sum(dy * (uv[h] * g * 2.0 + h_ref[h] - xv[h] + xk[h]), axis=0, keepdims=True)
        dh_ref[h] += jnp.sum(dyg, axis=0, keepdims=True)
        off = HD + HD * h
        dpack_ref[:, off : off + HD] = dxq[h].astype(dpack_ref.dtype)
        off += HD * heads
        dpack_ref[:, off : off + HD] = dk.astype(dpack_ref.dtype)
        off += HD * heads
        dpack_ref[:, off : off + HD] = (-dyg).astype(dpack_ref.dtype)
        dw1[h] = dw1[h] + dw1_out[h] + tn(xk[h], dz1)
        db1[h] = db1[h] + db1_out[h] + jnp.sum(dz1.astype(F32), axis=0, keepdims=True)
        dw2[h] = d2[h] + dw2_out[h]
        db2[h] = e2[h] + db2_out[h]
    sub = lax.broadcasted_iota(jnp.int32, (CH, CH), 0)
    lane = lax.broadcasted_iota(jnp.int32, (CH, CH), 1)
    stack = jnp.zeros((CH, CH), F32)
    cols = jnp.zeros((CH, CH), F32)
    for h in H:
        stack = stack + jnp.where(sub == h, dr_row[h], 0.0)
        slope = rcol[h] * (1.0 - HD * rcol[h])
        cols = cols + jnp.where(lane == h, slope, 0.0)
    turned = stack.T
    for h in H:
        turned = turned - jnp.where(lane == h, de_col[h] * (1.0 / CS), 0.0)
    dpack_ref[:, :HD] = (turned * cols)[:, :HD].astype(dpack_ref.dtype)


def backward_call(place, pack, do, saved, g, h):
    z1, a, z1b, c, z2b, w1s, w2s = saved
    heads = g.shape[0]
    rows = pack.shape[0]
    chunks = rows // CH
    last = chunks - 1
    per_block = chunks // 4

    def spot(c, place):
        return (((last - c) // per_block) ^ place[0]) * per_block + (last - c) % per_block

    def whole(*shape):
        return pl.BlockSpec(shape, lambda c, place: (0,) * len(shape))

    def moved(n):
        return pl.BlockSpec((CH, n), lambda c, place: (spot(c, place), 0))

    def kept(n):
        return pl.BlockSpec((CH, n), lambda c, place: (last - c, 0))

    by_head = pl.BlockSpec((heads, CH, HD), lambda c, place: (0, last - c, 0))
    sds = jax.ShapeDtypeStruct
    return pl.pallas_call(
        functools.partial(backward_kernel, heads),
        grid_spec=pltpu.PrefetchScalarGridSpec(
            num_scalar_prefetch=1,
            grid=(chunks,),
            in_specs=[
                moved(PACK),
                moved(heads * HD),
                kept(heads * INNER),
                kept(heads * INNER),
                kept(heads * INNER),
                by_head,
                by_head,
                pl.BlockSpec((1, heads, HD, INNER), lambda c, place: (last - c, 0, 0, 0)),
                pl.BlockSpec((STEPS, heads, HD, INNER), lambda c, place: (last - c, 0, 0, 0)),
                whole(heads, 1, HD),
                whole(heads, 1, HD),
            ],
            out_specs=[
                moved(PACK),
                whole(heads, HD, INNER),
                whole(heads, 1, INNER),
                whole(heads, HD, INNER),
                whole(heads, 1, HD),
                whole(heads, 1, HD),
                whole(heads, 1, HD),
            ],
            scratch_shapes=[
                pltpu.VMEM((heads, CH, INNER), F32),
                pltpu.VMEM((heads, CH, HD), F32),
                pltpu.VMEM((heads, CH, INNER), F32),
                pltpu.VMEM((heads, CH, INNER), F32),
                pltpu.VMEM((heads, CH, INNER), F32),
                pltpu.VMEM((heads, CH, HD), F32),
                pltpu.VMEM((heads, CH, CH), BF),
                pltpu.VMEM((heads, CH, INNER), BF),
                pltpu.VMEM((heads, CH, INNER), F32),
                pltpu.VMEM((heads, CH, HD), F32),
                pltpu.VMEM((heads, CH, HD), F32),
                pltpu.VMEM((heads, CH, HD), F32),
                pltpu.VMEM((heads, CH, INNER), BF),
            ],
        ),
        out_shape=[
            sds((rows, PACK), BF),
            sds((heads, HD, INNER), F32),
            sds((heads, 1, INNER), F32),
            sds((heads, HD, INNER), F32),
            sds((heads, 1, HD), F32),
            sds((heads, 1, HD), F32),
            sds((heads, 1, HD), F32),
        ],
        compiler_params=pltpu.CompilerParams(vmem_limit_bytes=40 * 2**20),
        cost_estimate=pl.CostEstimate(flops=70 * 10**9, bytes_accessed=25 * 10**6, transcendentals=0),
    )(place, pack, do, z1, a, z1b, c, z2b, w1s, w2s, g, h)


D = 768


def swap(x, bit):
    size = lax.axis_size("tensor")
    return lax.ppermute(x, "tensor", [(i, i ^ bit) for i in range(size)])


def widen(x):
    far = swap(x, 2)
    return jnp.concatenate([x, swap(x, 1), far, swap(far, 1)], axis=0)


def narrow(total):
    quarter = total.shape[0] // 4
    near, pair, far, cross = [total[quarter * i : quarter * (i + 1)] for i in range(4)]
    far = (far + swap(cross.astype(BF), 1).astype(F32)).astype(BF)
    far = swap(far, 2)
    return near + swap(pair.astype(BF), 1).astype(F32) + far.astype(F32)


def dot(a, b):
    return lax.dot_general(a, b, (((1,), (0,)), ((), ())), preferred_element_type=F32)


def dot_t(a, b):
    return lax.dot_general(a, b, (((1,), (1,)), ((), ())), preferred_element_type=F32)


def t_dot(a, b):
    return lax.dot_general(a, b, (((0,), (0,)), ((), ())), preferred_element_type=F32)


def rms(x, gain):
    scale = lax.rsqrt(jnp.mean(x * x, axis=1, keepdims=True) + EPS)
    return (x * scale * gain).astype(BF), scale


def rms_back(x, scale, gain, grad):
    q = grad * gain
    back = scale * q - x * (scale * scale * scale) * jnp.mean(q * x, axis=1, keepdims=True)
    return back, jnp.sum(grad * (x * scale), axis=0)


def gather(x):
    return lax.all_gather(x, "dp", axis=0, tiled=True)


def scatter(x):
    return lax.psum_scatter(x, "dp", scatter_dimension=0, tiled=True).astype(F32)


def exchange_sum(x):
    moved = lax.all_to_all(x, "dp", split_axis=0, concat_axis=0, tiled=True)
    return jnp.sum(moved.astype(F32), axis=0)


def per_device(
    hidden_in, cotangent, w_query, w_key, w_value, w_outgate, w_rate, w_output, init_first, init_first_bias,
    init_second, init_second_bias, inner_gain, inner_shift, post_gain, post_shift, mixer_gain, mlp_gain,
    w_gate, w_up, w_down,
):
    layers, part, mine = w_query.shape
    heads = w_rate.shape[2]
    ff = w_gate.shape[2]
    inner_part = init_first.shape[3]
    small_part = inner_gain.shape[2]
    gain_part = mixer_gain.shape[1]
    dp = lax.axis_size("dp")
    tp = lax.axis_size("tensor")
    rows = hidden_in.shape[0]
    place = lax.axis_index("tensor").astype(jnp.int32).reshape(1)
    lead = HD - heads

    gains_here = jnp.concatenate([mixer_gain, mlp_gain], axis=0)
    gains_group = lax.all_gather(gains_here, "tensor", axis=1, tiled=True)
    span = 2 * mine + 6 * heads
    blocks = []
    for l in range(layers):
        first = init_first[l].transpose(2, 0, 1).reshape(inner_part, mine)
        second = init_second[l].transpose(1, 0, 2).reshape(inner_part, mine)
        small = jnp.concatenate(
            [init_second_bias[l], inner_gain[l], inner_shift[l], post_gain[l], post_shift[l]], axis=0
        )
        small = jnp.pad(small.T, ((0, inner_part - small_part), (0, 0)))
        blocks += [first, second, init_first_bias[l].T, small]
    tail = gains_group.reshape(inner_part, -1) if gains_group.size % inner_part == 0 else None
    blocks.append(tail)
    inner_all = gather(jnp.concatenate(blocks, axis=1))
    gains = inner_all[:, layers * span :].reshape(dp, 2 * layers, tp * gain_part)
    gains = gains.transpose(1, 0, 2).reshape(2 * layers, D).astype(F32)
    inner = []
    for l in range(layers):
        own = inner_all[:, l * span : (l + 1) * span]
        turned = own[:, : 2 * mine + heads].T.astype(F32)
        w1 = turned[:mine].reshape(heads, HD, INNER)
        w2 = turned[mine : 2 * mine].reshape(heads, HD, INNER)
        b1 = turned[2 * mine :].reshape(heads, 1, INNER)
        small = own[:, 2 * mine + heads :].reshape(dp, inner_part, 5 * heads)[:, :small_part]
        small = small.reshape(HD, 5 * heads).T.astype(F32).reshape(5, heads, HD)
        w2 = w2 - jnp.mean(w2, axis=1, keepdims=True)
        b2 = small[0] - jnp.mean(small[0], axis=1, keepdims=True)
        inner.append((w1, b1, w2, b2[:, None], small[1][:, None], small[2][:, None], small[3], small[4]))

    blank = jnp.zeros((part, lead), BF)
    mix_w = [
        gather(jnp.concatenate([w_rate[l], blank, w_query[l], w_key[l], w_value[l]], axis=1)) for l in range(layers)
    ]
    rest_w = [
        gather(jnp.concatenate([w_outgate[l], w_gate[l], w_up[l], w_output[l].T, w_down[l].T], axis=1))
        for l in range(layers)
    ]
    edges = [0, mine, mine + ff, mine + 2 * ff, 2 * mine + 2 * ff, 2 * mine + 3 * ff]

    def piece(l, i):
        return rest_w[l][:, edges[i] : edges[i + 1]]

    residual = hidden_in.astype(F32)
    raw_wide = widen(hidden_in)
    kept = []
    for l in range(layers):
        w1, b1, w2, b2, g, h, pg, ps = inner[l]
        gain_one, gain_two = gains[l], gains[layers + l]
        res_one = residual
        if l == 0:
            wide, _ = rms(raw_wide.astype(F32), gain_one)
            scale_one = lax.rsqrt(jnp.mean(residual * residual, axis=1, keepdims=True) + EPS)
        else:
            normed, scale_one = rms(residual, gain_one)
            wide = widen(normed)
        pack = dot(wide, mix_w[l]).astype(BF)
        outs = forward_call(place, pack, w1, b1, w2, b2, g, h)
        inner_out, saved = outs[0], outs[1:]
        gate_pre = dot(wide, piece(l, 0))
        sums = jnp.stack([jnp.sum(inner_out, axis=1), jnp.sum(inner_out * inner_out, axis=1)])
        sums = order_sum(sums)
        mean_all = sums[0] / D
        inv = lax.rsqrt(sums[1] / D - mean_all * mean_all + EPS)[:, None]
        unit = (inner_out - mean_all[:, None]) * inv
        post = unit * pg.reshape(-1) + ps.reshape(-1)
        heads_out = (jax.nn.gelu(gate_pre, approximate=True) * post).astype(BF)
        residual = residual + narrow(dot_t(heads_out, piece(l, 3)))
        res_two = residual
        normed, scale_two = rms(residual, gain_two)
        wide_two = widen(normed)
        gate = dot(wide_two, piece(l, 1))
        up = dot(wide_two, piece(l, 2))
        hidden = (jax.nn.silu(gate) * up).astype(BF)
        residual = residual + narrow(dot_t(hidden, piece(l, 4)))
        kept.append(
            (res_one, scale_one, wide, pack, saved, gate_pre, unit, inv, heads_out, res_two, scale_two, wide_two,
             gate, up, hidden)
        )
    block_out = residual.astype(BF)

    grad = cotangent.astype(F32)
    mix_grads, rest_grads = [None] * layers, [None] * layers
    gain_grads = [None] * (2 * layers)
    for l in reversed(range(layers)):
        w1, b1, w2, b2, g, h, pg, ps = inner[l]
        gain_one, gain_two = gains[l], gains[layers + l]
        (res_one, scale_one, wide, pack, saved, gate_pre, unit, inv, heads_out, res_two, scale_two, wide_two,
         gate, up, hidden) = kept[l]
        branch = widen(cotangent if l == layers - 1 else grad.astype(BF))
        d_hidden = dot(branch, piece(l, 4))
        q = jax.nn.sigmoid(gate)
        swish = gate * q
        d_gate = (d_hidden * up * (q + swish * (1.0 - q))).astype(BF)
        d_up = (d_hidden * swish).astype(BF)
        d_down = t_dot(branch, hidden)
        d_norm = narrow(dot_t(d_gate, piece(l, 1)) + dot_t(d_up, piece(l, 2)))
        back, gain_grads[layers + l] = rms_back(res_two, scale_two, gain_two, d_norm)
        grad = grad + back
        branch_two = widen(grad.astype(BF))
        d_heads = dot(branch_two, piece(l, 3))
        post = unit * pg.reshape(-1) + ps.reshape(-1)
        ge, slope = gelu_two(gate_pre)
        d_pre = (d_heads * post * slope).astype(BF)
        d_post = d_heads * ge
        d_pg = jnp.sum(d_post * unit, axis=0)
        d_ps = jnp.sum(d_post, axis=0)
        p = d_post * pg.reshape(-1)
        sums = order_sum(jnp.stack([jnp.sum(p, axis=1), jnp.sum(p * unit, axis=1)])) / D
        d_inner = inv * (p - sums[0][:, None] - unit * sums[1][:, None])
        rest_grads[l] = scatter(
            jnp.concatenate(
                [t_dot(wide, d_pre), t_dot(wide_two, d_gate), t_dot(wide_two, d_up), t_dot(branch_two, heads_out), d_down],
                axis=1,
            ).astype(BF)
        )
        d_pack, dw1, db1, dw2, db2, dg, dh = backward_call(place, pack, d_inner, saved, g, h)
        d_norm = narrow(dot_t(d_pack, mix_w[l]) + dot_t(d_pre, piece(l, 0)))
        back, gain_grads[l] = rms_back(res_one, scale_one, gain_one, d_norm)
        grad = grad + back
        turned = jnp.concatenate([dw1.reshape(mine, INNER), dw2.reshape(mine, INNER), db1[:, 0]], axis=0).T
        small = jnp.concatenate([db2[:, 0], dg[:, 0], dh[:, 0], d_pg.reshape(heads, HD), d_ps.reshape(heads, HD)], axis=0)
        small = jnp.pad(small.T.reshape(dp, small_part, 5 * heads), ((0, 0), (0, inner_part - small_part), (0, 0)))
        block = [turned.reshape(dp, inner_part, 2 * mine + heads), small]
        if l == 0:
            all_gains = jnp.stack(gain_grads).reshape(2 * layers, dp, tp * gain_part)
            block.append(all_gains.transpose(1, 0, 2).reshape(dp, inner_part, -1))
        block = jnp.concatenate(block, axis=2)
        block = jnp.pad(block, ((0, 0), (0, 0), (0, PACK - block.shape[2])))
        mixed = jnp.concatenate([t_dot(wide, d_pack).reshape(dp, part, PACK), block], axis=1).astype(BF)
        mix_grads[l] = exchange_sum(mixed) if l == 0 else scatter(mixed)[0]
    grad_in = grad

    both = jnp.stack(mix_grads)
    mats, block = both[:, :part], both[:, part:]
    rest = jnp.stack(rest_grads)
    d_gains = mix_grads[0][part:, span : span + gains_group.size // inner_part].reshape(2 * layers, tp, gain_part)
    d_gains = lax.psum(d_gains, "tensor")
    d_gains = lax.dynamic_index_in_dim(d_gains, lax.axis_index("tensor"), axis=1, keepdims=False)
    small = block[:, :small_part, 2 * mine + heads : span].transpose(0, 2, 1).reshape(layers, 5, heads, small_part)

    def matrix(i):
        return mats[:, :, HD + mine * i : HD + mine * (i + 1)]

    def tail_piece(i):
        return rest[:, :, edges[i] : edges[i + 1]]

    def states(i):
        return block[:, :, mine * i : mine * (i + 1)].reshape(layers, inner_part, heads, HD)

    return (
        block_out,
        grad_in,
        matrix(0),
        matrix(1),
        matrix(2),
        tail_piece(0),
        mats[:, :, :heads],
        tail_piece(3).transpose(0, 2, 1),
        states(0).transpose(0, 2, 3, 1),
        block[:, :, 2 * mine : 2 * mine + heads].transpose(0, 2, 1),
        states(1).transpose(0, 2, 1, 3),
        small[:, 0],
        small[:, 1],
        small[:, 2],
        small[:, 3],
        small[:, 4],
        d_gains[:layers],
        d_gains[layers:],
        tail_piece(1),
        tail_piece(2),
        tail_piece(4).transpose(0, 2, 1),
    )


def order_sum(sums):
    def turn(x, bit):
        parts = jnp.split(x, 4, axis=1)
        return jnp.concatenate([parts[i ^ bit] for i in range(4)], axis=1)

    sums = sums + turn(swap(sums, 1), 1)
    return sums + turn(swap(sums, 2), 2)


def solution(mesh):
    placed = (
        P(("dp", "tensor"), None),
        P(("dp", "tensor"), None),
        P(None, "dp", "tensor"),
        P(None, "dp", "tensor"),
        P(None, "dp", "tensor"),
        P(None, "dp", "tensor"),
        P(None, "dp", "tensor"),
        P(None, "tensor", "dp"),
        P(None, "tensor", None, "dp"),
        P(None, "tensor", "dp"),
        P(None, "tensor", "dp", None),
        P(None, "tensor", "dp"),
        P(None, "tensor", "dp"),
        P(None, "tensor", "dp"),
        P(None, "tensor", "dp"),
        P(None, "tensor", "dp"),
        P(None, ("dp", "tensor")),
        P(None, ("dp", "tensor")),
        P(None, "dp", "tensor"),
        P(None, "dp", "tensor"),
        P(None, "tensor", "dp"),
    )
    return jax.shard_map(
        per_device,
        mesh=mesh,
        in_specs=placed,
        out_specs=(
            P(("dp", "tensor"), None),
            P(("dp", "tensor"), None),
            P(None, "dp", "tensor"),
            P(None, "dp", "tensor"),
            P(None, "dp", "tensor"),
            P(None, "dp", "tensor"),
            P(None, "dp", "tensor"),
            P(None, "tensor", "dp"),
            P(None, "tensor", None, "dp"),
            P(None, "tensor", "dp"),
            P(None, "tensor", "dp", None),
            P(None, "tensor", "dp"),
            P(None, "tensor", "dp"),
            P(None, "tensor", "dp"),
            P(None, "tensor", "dp"),
            P(None, "tensor", "dp"),
            P(None, ("dp", "tensor")),
            P(None, ("dp", "tensor")),
            P(None, "dp", "tensor"),
            P(None, "dp", "tensor"),
            P(None, "tensor", "dp"),
        ),
        check_vma=False,
    )
```

time: 6820 us -> 745 us (0.11)
  matrix products: 2320 us -> 85.2 us
  local copies, waits for them, and re-layouts: 1440 us -> 68.1 us
  blocking collectives: 1240 us -> 113 us
  other arithmetic: 771 us -> 36.6 us
  waiting for transfers between devices: 875 us -> 177 us
  Pallas kernels: 0 us -> 206 us
  loops' own time: 111 us -> 0 us
    dot_general x7734 -> x36, matrix products: 2320 us -> 85.2 us  [the longest x12 36.5 us: dot(): lax.dot_general(a, b, (((1,), (0,)), ((), ())), preferred_element_type=F32)]
    all_gather x36 -> x4, blocking collectives: 1140 us -> 107 us  [the longest x3 102 us: gather(): return lax.all_gather(x, 'dp', axis=0, tiled=True)]
    squeeze x1376 -> x9, local copies, waits for them, and re-layouts: 711 us -> 4.93 us  [the longest x1 1.45 us: per_device(): w_outgate[l]]
    reduce_scatter x22 -> x1, waiting for transfers between devices: 694 us -> 0.01 us  [scatter(): lax.psum_scatter(x, 'dp', scatter_dimension=0, tiled=True).astype(F32)]
    reduce_sum x2058 -> x15, other arithmetic: 393 us -> 11.5 us  [the longest x4 7.19 us: rms(): scale = lax.rsqrt(jnp.mean(x * x, axis=1, keepdims=True) + EPS)]
    dynamic_update_slice x768 -> x0, local copies, waits for them, and re-layouts: 360 us -> none  [the longest x640 359 us: inner_chains(): lax.scan(jax.checkpoint(grouped), state_now, (arrange(query_rows_all), ar...]
    pallas_call x0 -> x4, Pallas kernels: none -> 206 us  [the longest x2 111 us: backward_call(): pl.pallas_call(functools.partial(backward_kernel, heads), grid_spec=pltpu...]
    squeeze x256 -> x0, other arithmetic: 166 us -> none  [inner_step(): final_row_slice = inner_rate_matrix[:, -1, :]]
where the time goes in v1:
time: 745 us; the launch traced here: 735 us
  Pallas kernels  206 us (28%)
  waiting for transfers between devices  177 us (24%)
  blocking collectives  113 us (15%)
  matrix products  85.2 us (11%)
  local copies, waits for them, and re-layouts  68.1 us (9%)
  other arithmetic  36.6 us (5%)
  starting transfers between devices  32.4 us (4%)
  between operations  16.5 us (2%)
    ppermute x56, waiting for transfers between devices, swap(): return lax.ppermute(x, 'tensor', [(i, i ^ bit) for i in range(size)])  147 us
    pallas_call x2, Pallas kernels, backward_call(): pl.pallas_call(functools.partial(backward_kernel, heads), grid_spec=pltpu...  111 us
    all_gather x3, blocking collectives, gather(): return lax.all_gather(x, 'dp', axis=0, tiled=True)  102 us
    pallas_call x2, Pallas kernels, forward_call(): pl.pallas_call(functools.partial(forward_kernel, heads), grid_spec=pltpu....  95.7 us
    unnamed x331, local copies, waits for them, and re-layouts  44.4 us
    dot_general x12, matrix products, dot(): lax.dot_general(a, b, (((1,), (0,)), ((), ())), preferred_element_type=F32)  36.5 us
    dot_general x12, matrix products, t_dot(): lax.dot_general(a, b, (((0,), (0,)), ((), ())), preferred_element_type=F32)  27.3 us
    ppermute x56, starting transfers between devices, swap(): return lax.ppermute(x, 'tensor', [(i, i ^ bit) for i in range(size)])  26.6 us
  transfers between devices with their start and end apart: 62, of which 30 were waited for; matrix products, arithmetic and copies ran while one was open for 17% of the time, Pallas kernels for 21%

profile of v1, /device:TPU:0, one launch (start us, length us, event | category | flops | bytes accessed | tf_op | source)
XLA Modules:
  0.0 735.5 jit_solution(8288716646104998797)
XLA Ops:
  21.5 5.1 all-gather
  26.9 32.8 %all_gather.19 = bf16[256,816]{1,0:T(8,128)(2,1)S(1)} all-gather(bf16[32,816]{1,0:T(8,128)(2,1)S(1)} %concatenate.122), channel_id=1, replica_groups=mesh['dp'=8,'tensor'=4] {'dp'}, dimensions={0}, use_global_device_ids=true | all-gather | bytes 470016 | tf_op jit(solution)/shard_map/all_gather | solution.py:535
  63.7 34.3 %all_gather.21 = bf16[768,640]{1,0:T(8,128)(2,1)S(1)} all-gather(bf16[96,640]{1,0:T(8,128)(2,1)S(1)} %concatenate.124), channel_id=1, replica_groups=mesh['dp'=8,'tensor'=4] {'dp'}, dimensions={0}, use_global_device_ids=true | all-gather | bytes 1105920 | tf_op jit(solution)/shard_map/all_gather | solution.py:535
  102.2 47.6 %shard_map.364 = (f32[1024,192]{1,0:T(8,128)S(1)}, f32[1024,768]{1,0:T(8,128)S(1)}, f32[1024,768]{1,0:T(8,128)S(1)}, f32[1024,768]{1,0:T(8,128)}, f32[3,1024,64]...) custom-call(s32[1]{0:T(128)} %bitcast.23.place_ref, ...), custom_call_target="tpu_custom_call" | custom-call | flops 65000001536 | bytes 25000000 | tf_op jit(solution)/shard_map/pallas_call | solution.py:193
  169.7 10.7 %collective-permute-done.7 = bf16[256,768]{1,0:T(8,128)(2,1)S(1)} collective-permute-done((bf16[256,768]{1,0:T(8,128)(2,1)}, bf16[256,768]{1,0:T(8,128)(2,1)S(1)}, u32[]{:S(2)}, u32[]{:S(2)}) %collective-permute-start.7) | collective-permute-done | bytes 393248 | tf_op jit(solution)/shard_map/ppermute | solution.py:495
  183.8 9.7 %collective-permute-done.9 = bf16[256,768]{1,0:T(8,128)(2,1)S(1)} collective-permute-done((bf16[256,768]{1,0:T(8,128)(2,1)S(1)}, bf16[256,768]{1,0:T(8,128)(2,1)S(1)}, u32[]{:S(2)}, u32[]{:S(2)}) %collective-permute-start.9) | collective-permute-done | bytes 393248 | tf_op jit(solution)/shard_map/ppermute | solution.py:495
  198.7 4.3 multiply_convert_fusion.5
  210.6 10.8 %collective-permute-done.13 = bf16[256,768]{1,0:T(8,128)(2,1)} collective-permute-done((bf16[256,768]{1,0:T(8,128)(2,1)}, bf16[256,768]{1,0:T(8,128)(2,1)}, u32[]{:S(2)}, u32[]{:S(2)}) %collective-permute-start.13) | collective-permute-done | bytes 393248 | tf_op jit(solution)/shard_map/ppermute | solution.py:495
  224.9 9.9 %collective-permute-done.15 = bf16[256,768]{1,0:T(8,128)(2,1)S(1)} collective-permute-done((bf16[256,768]{1,0:T(8,128)(2,1)S(1)}, bf16[256,768]{1,0:T(8,128)(2,1)S(1)}, u32[]{:S(2)}, u32[]{:S(2)}) %collective-permute-start.15) | collective-permute-done | bytes 393248 | tf_op jit(solution)/shard_map/ppermute | solution.py:495
  234.7 35.0 %all_gather.23 = bf16[768,640]{1,0:T(8,128)(2,1)S(1)} all-gather(bf16[96,640]{1,0:T(8,128)(2,1)S(1)} %concatenate.130), channel_id=1, replica_groups=mesh['dp'=8,'tensor'=4] {'dp'}, dimensions={0}, use_global_device_ids=true | all-gather | bytes 1105920 | tf_op jit(solution)/shard_map/all_gather | solution.py:535
  271.3 48.0 %shard_map.365 = (f32[1024,192]{1,0:T(8,128)S(1)}, f32[1024,768]{1,0:T(8,128)S(1)}, f32[1024,768]{1,0:T(8,128)S(1)}, f32[1024,768]{1,0:T(8,128)}, f32[3,1024,64]...) custom-call(s32[1]{0:T(128)} %bitcast.23.place_ref, ...), custom_call_target="tpu_custom_call" | custom-call | flops 65000001536 | bytes 25000000 | tf_op jit(solution)/shard_map/pallas_call | solution.py:193
  344.0 8.9 %collective-permute-done.21 = bf16[256,768]{1,0:T(8,128)(2,1)} collective-permute-done((bf16[256,768]{1,0:T(8,128)(2,1)}, bf16[256,768]{1,0:T(8,128)(2,1)}, u32[]{:S(2)}, u32[]{:S(2)}) %collective-permute-start.21) | collective-permute-done | bytes 393248 | tf_op jit(solution)/shard_map/ppermute | solution.py:495
  356.0 5.3 collective-permute-done.29
  361.8 7.0 collective-permute-done.23
  381.2 9.7 %collective-permute-done.33 = bf16[256,768]{1,0:T(8,128)(2,1)S(1)} collective-permute-done((bf16[256,768]{1,0:T(8,128)(2,1)S(1)}, bf16[256,768]{1,0:T(8,128)(2,1)S(1)}, u32[]{:S(2)}, u32[]{:S(2)}) %collective-permute-start.33) | collective-permute-done | bytes 393248 | tf_op jit(solution)/shard_map/ppermute | solution.py:495
  391.8 7.0 collective-permute-done.27
  401.3 9.6 %collective-permute-done.35 = bf16[256,768]{1,0:T(8,128)(2,1)S(1)} collective-permute-done((bf16[256,768]{1,0:T(8,128)(2,1)S(1)}, bf16[256,768]{1,0:T(8,128)(2,1)S(1)}, u32[]{:S(2)}, u32[]{:S(2)}) %collective-permute-start.35) | collective-permute-done | bytes 393248 | tf_op jit(solution)/shard_map/ppermute | solution.py:495
  412.6 5.0 multiply_reduce_fusion
  430.5 55.4 %shard_map.366 = (bf16[1024,640]{1,0:T(8,128)(2,1)S(1)}, f32[3,64,256]{2,1,0:T(8,128)S(1)}, f32[3,1,256]{2,1,0:T(1,128)S(1)}, f32[3,64,256]{2,1,0:T(8,128)S(1)},...) custom-call(s32[1]{0:T(128)} %bitcast.23.place_ref, ...), custom_call_target="tpu_custom_call" | custom-call | flops 70000001024 | bytes 25000000 | tf_op jit(solution)/shard_map/pallas_call | solution.py:433
  501.4 7.1 collective-permute-done.41
  514.3 5.2 collective-permute-done.43
  522.7 4.7 copy.422
  528.0 5.5 multiply_convert_fusion
  538.9 10.3 %collective-permute-done.47 = bf16[256,768]{1,0:T(8,128)(2,1)S(1)} collective-permute-done((bf16[256,768]{1,0:T(8,128)(2,1)S(1)}, bf16[256,768]{1,0:T(8,128)(2,1)S(1)}, u32[]{:S(2)}, u32[]{:S(2)}) %collective-permute-start.47) | collective-permute-done | bytes 393248 | tf_op jit(solution)/shard_map/ppermute | solution.py:495
  551.9 9.5 %collective-permute-done.49 = bf16[256,768]{1,0:T(8,128)(2,1)S(1)} collective-permute-done((bf16[256,768]{1,0:T(8,128)(2,1)S(1)}, bf16[256,768]{1,0:T(8,128)(2,1)S(1)}, u32[]{:S(2)}, u32[]{:S(2)}) %collective-permute-start.49) | collective-permute-done | bytes 393248 | tf_op jit(solution)/shard_map/ppermute | solution.py:495
  563.2 4.7 multiply_reduce_fusion.1
  581.3 4.7 copy.420
  593.6 55.4 %shard_map.367 = (bf16[1024,640]{1,0:T(8,128)(2,1)S(1)}, f32[3,64,256]{2,1,0:T(8,128)S(1)}, f32[3,1,256]{2,1,0:T(1,128)S(1)}, f32[3,64,256]{2,1,0:T(8,128)S(1)},...) custom-call(s32[1]{0:T(128)} %bitcast.23.place_ref, bf16[1024,640]{1,0:T(8,128)(2,1)S(1)} %copy-done.3, ...), custom_call_target="tpu_custom_call" | custom-call | flops 70000001024 | bytes 25000000 | tf_op jit(solution)/shard_map/pallas_call | solution.py:433
  662.6 6.4 collective-permute-done.55
  672.0 5.1 all-to-all-start
  681.9 26.4 %all-to-all-done = bf16[8,128,640]{2,1,0:T(8,128)(2,1)S(1)} async-done(((bf16[8,128,640]{2,1,0:T(8,128)(2,1)}), bf16[8,128,640]{2,1,0:T(8,128)(2,1)S(1)}, u32[]{:S(2)}, u32[]{:S(2)}) %all-to-all-start) | async-done | bytes 1310752 | tf_op jit(solution)/shard_map/all_to_all | solution.py:543
  711.7 6.1 psum.7
  (683 shorter events, 212.1 us)
Async XLA Ops:
  7.2 153.7 %all-gather.4.cloned.1.call-start = ((), (), s32[]{:S(2)}) async-start(), calls=%async_computation.4 | async-start | bytes 3317760 | tf_op jit(solution)/shard_map/all_gather | solution.py:535
  7.3 56.3 %collective-permute-start.1 = (bf16[256,768]{1,0:T(8,128)(2,1)}, bf16[256,768]{1,0:T(8,128)(2,1)S(1)}, u32[]{:S(2)}, u32[]{:S(2)}) collective-permute-start(bf16[256,768]{1,0:T(8,128)(2,1)} %param.21), channel_id=1, source_target_pairs={{0,2},{1,3},{2,0},{3,1},{4,6},{5,7},{6,4},{7,5},{8,10},{9,11},{10,... | collective-permute-start | bytes 1179656 | tf_op jit(solution)/shard_map/ppermute | solution.py:495
  10.3 87.7 %collective-permute-start = (bf16[256,768]{1,0:T(8,128)(2,1)}, bf16[256,768]{1,0:T(8,128)(2,1)}, u32[]{:S(2)}, u32[]{:S(2)}) collective-permute-start(bf16[256,768]{1,0:T(8,128)(2,1)} %param.21), channel_id=1, source_target_pairs={{0,1},{1,0},{2,3},{3,2},{4,5},{5,4},{6,7},{7,6},{8,9},{9,8},{10,11... | collective-permute-start | bytes 1179656 | tf_op jit(solution)/shard_map/ppermute | solution.py:495
  16.3 315.0 %all-gather.6.cloned.1.call-start = ((), (), s32[]{:S(2)}) async-start(), calls=%async_computation.5 | async-start | bytes 3317760 | tf_op jit(solution)/shard_map/all_gather | solution.py:535
  63.6 34.4 %collective-permute-start.2 = (bf16[256,768]{1,0:T(8,128)(2,1)S(1)}, bf16[256,768]{1,0:T(8,128)(2,1)S(1)}, u32[]{:S(2)}, u32[]{:S(2)}) collective-permute-start(bf16[256,768]{1,0:T(8,128)(2,1)S(1)} %collective-permute-done.1), channel_id=1, source_target_pairs={{0,1},{1,0},{2,3},{3,2},{4,5},{5,4},{6,7},{7,6},{8,9},{9,8},{10,11... | collective-permute-start | bytes 1179656 | tf_op jit(solution)/shard_map/ppermute | solution.py:495
  169.0 11.4 %collective-permute-start.7 = (bf16[256,768]{1,0:T(8,128)(2,1)}, bf16[256,768]{1,0:T(8,128)(2,1)S(1)}, u32[]{:S(2)}, u32[]{:S(2)}) collective-permute-start(bf16[256,768]{1,0:T(8,128)(2,1)} %fusion.78), channel_id=1, source_target_pairs={{0,2},{1,3},{2,0},{3,1},{4,6},{5,7},{6,4},{7,5},{8,10},{9,11},{10,... | collective-permute-start | bytes 1179656 | tf_op jit(solution)/shard_map/ppermute | solution.py:495
  183.1 10.4 %collective-permute-start.9 = (bf16[256,768]{1,0:T(8,128)(2,1)S(1)}, bf16[256,768]{1,0:T(8,128)(2,1)S(1)}, u32[]{:S(2)}, u32[]{:S(2)}) collective-permute-start(bf16[256,768]{1,0:T(8,128)(2,1)S(1)} %multiply_convert_fusion.8), channel_id=1, source_target_pairs={{0,2},{1,3},{2,0},{3,1},{4,6},{5,7},{6,4},{7,5},{8,10},{9,11},{10,... | collective-permute-start | bytes 1179656 | tf_op jit(solution)/shard_map/ppermute | solution.py:495
  183.8 12.2 %collective-permute-start.8 = (bf16[256,768]{1,0:T(8,128)(2,1)S(1)}, bf16[256,768]{1,0:T(8,128)(2,1)}, u32[]{:S(2)}, u32[]{:S(2)}) collective-permute-start(bf16[256,768]{1,0:T(8,128)(2,1)S(1)} %multiply_convert_fusion.8), channel_id=1, source_target_pairs={{0,1},{1,0},{2,3},{3,2},{4,5},{5,4},{6,7},{7,6},{8,9},{9,8},{10,11... | collective-permute-start | bytes 1179656 | tf_op jit(solution)/shard_map/ppermute | solution.py:495
  194.6 482.5 %reduce-scatter.8.cloned.1.call-start = ((), (), s32[]{:S(2)}) async-start(), calls=%async_computation.6 | async-start | bytes 1474560 | tf_op jit(solution)/shard_map/reduce_scatter | solution.py:539
  209.6 11.7 %collective-permute-start.13 = (bf16[256,768]{1,0:T(8,128)(2,1)}, bf16[256,768]{1,0:T(8,128)(2,1)}, u32[]{:S(2)}, u32[]{:S(2)}) collective-permute-start(bf16[256,768]{1,0:T(8,128)(2,1)} %fusion.75), channel_id=1, source_target_pairs={{0,2},{1,3},{2,0},{3,1},{4,6},{5,7},{6,4},{7,5},{8,10},{9,11},{10,... | collective-permute-start | bytes 1179656 | tf_op jit(solution)/shard_map/ppermute | solution.py:495
  224.2 10.6 %collective-permute-start.15 = (bf16[256,768]{1,0:T(8,128)(2,1)S(1)}, bf16[256,768]{1,0:T(8,128)(2,1)S(1)}, u32[]{:S(2)}, u32[]{:S(2)}) collective-permute-start(bf16[256,768]{1,0:T(8,128)(2,1)S(1)} %multiply_convert_fusion.7), channel_id=1, source_target_pairs={{0,2},{1,3},{2,0},{3,1},{4,6},{5,7},{6,4},{7,5},{8,10},{9,11},{10,... | collective-permute-start | bytes 1179656 | tf_op jit(solution)/shard_map/ppermute | solution.py:495
  224.8 45.0 %collective-permute-start.14 = (bf16[256,768]{1,0:T(8,128)(2,1)S(1)}, bf16[256,768]{1,0:T(8,128)(2,1)S(1)}, u32[]{:S(2)}, u32[]{:S(2)}) collective-permute-start(bf16[256,768]{1,0:T(8,128)(2,1)S(1)} %multiply_convert_fusion.7), channel_id=1, source_target_pairs={{0,1},{1,0},{2,3},{3,2},{4,5},{5,4},{6,7},{7,6},{8,9},{9,8},{10,11... | collective-permute-start | bytes 1179656 | tf_op jit(solution)/shard_map/ppermute | solution.py:495
  234.7 35.0 %collective-permute-start.16 = (bf16[256,768]{1,0:T(8,128)(2,1)S(1)}, bf16[256,768]{1,0:T(8,128)(2,1)S(1)}, u32[]{:S(2)}, u32[]{:S(2)}) collective-permute-start(bf16[256,768]{1,0:T(8,128)(2,1)S(1)} %collective-permute-done.15), channel_id=1, source_target_pairs={{0,1},{1,0},{2,3},{3,2},{4,5},{5,4},{6,7},{7,6},{8,9},{9,8},{10,11... | collective-permute-start | bytes 1179656 | tf_op jit(solution)/shard_map/ppermute | solution.py:495
  340.6 12.3 %collective-permute-start.21 = (bf16[256,768]{1,0:T(8,128)(2,1)}, bf16[256,768]{1,0:T(8,128)(2,1)}, u32[]{:S(2)}, u32[]{:S(2)}) collective-permute-start(bf16[256,768]{1,0:T(8,128)(2,1)} %fusion.72), channel_id=1, source_target_pairs={{0,2},{1,3},{2,0},{3,1},{4,6},{5,7},{6,4},{7,5},{8,10},{9,11},{10,... | collective-permute-start | bytes 1179656 | tf_op jit(solution)/shard_map/ppermute | solution.py:495
  341.6 19.7 %collective-permute-start.29 = (bf16[256,768]{1,0:T(8,128)(2,1)S(1)}, bf16[256,768]{1,0:T(8,128)(2,1)}, u32[]{:S(2)}, u32[]{:S(2)}) collective-permute-start(bf16[256,768]{1,0:T(8,128)(2,1)S(1)} %copy-done.35), channel_id=1, source_target_pairs={{0,2},{1,3},{2,0},{3,1},{4,6},{5,7},{6,4},{7,5},{8,10},{9,11},{10,... | collective-permute-start | bytes 1179656 | tf_op jit(solution)/shard_map/ppermute | solution.py:495
  354.9 13.9 %collective-permute-start.23 = (bf16[256,768]{1,0:T(8,128)(2,1)S(1)}, bf16[256,768]{1,0:T(8,128)(2,1)S(1)}, u32[]{:S(2)}, u32[]{:S(2)}) collective-permute-start(bf16[256,768]{1,0:T(8,128)(2,1)S(1)} %multiply_convert_fusion.6), channel_id=1, source_target_pairs={{0,2},{1,3},{2,0},{3,1},{4,6},{5,7},{6,4},{7,5},{8,10},{9,11},{10,... | collective-permute-start | bytes 1179656 | tf_op jit(solution)/shard_map/ppermute | solution.py:495
  356.0 12.9 %collective-permute-start.28 = (bf16[256,768]{1,0:T(8,128)(2,1)S(1)}, bf16[256,768]{1,0:T(8,128)(2,1)S(1)}, u32[]{:S(2)}, u32[]{:S(2)}) collective-permute-start(bf16[256,768]{1,0:T(8,128)(2,1)S(1)} %copy-done.35), channel_id=1, source_target_pairs={{0,1},{1,0},{2,3},{3,2},{4,5},{5,4},{6,7},{7,6},{8,9},{9,8},{10,11... | collective-permute-start | bytes 1179656 | tf_op jit(solution)/shard_map/ppermute | solution.py:495
  378.9 12.0 %collective-permute-start.33 = (bf16[256,768]{1,0:T(8,128)(2,1)S(1)}, bf16[256,768]{1,0:T(8,128)(2,1)S(1)}, u32[]{:S(2)}, u32[]{:S(2)}) collective-permute-start(bf16[256,768]{1,0:T(8,128)(2,1)S(1)} %fusion.66), channel_id=1, source_target_pairs={{0,2},{1,3},{2,0},{3,1},{4,6},{5,7},{6,4},{7,5},{8,10},{9,11},{10,... | collective-permute-start | bytes 1179656 | tf_op jit(solution)/shard_map/ppermute | solution.py:495
  379.9 11.8 %collective-permute-start.25 = (bf16[256,768]{1,0:T(8,128)(2,1)S(1)}, bf16[256,768]{1,0:T(8,128)(2,1)S(1)}, u32[]{:S(2)}, u32[]{:S(2)}) collective-permute-start(bf16[256,768]{1,0:T(8,128)(2,1)S(1)} %get-tuple-element.260), channel_id=1, source_target_pairs={{0,1},{1,0},{2,3},{3,2},{4,5},{5,4},{6,7},{7,6},{8,9},{9,8},{10,11... | collective-permute-start | bytes 1179656 | tf_op jit(solution)/shard_map/ppermute | solution.py:495
  380.1 18.6 %collective-permute-start.27 = (bf16[256,768]{1,0:T(8,128)(2,1)S(1)}, bf16[256,768]{1,0:T(8,128)(2,1)S(1)}, u32[]{:S(2)}, u32[]{:S(2)}) collective-permute-start(bf16[256,768]{1,0:T(8,128)(2,1)S(1)} %fusion.68), channel_id=1, source_target_pairs={{0,2},{1,3},{2,0},{3,1},{4,6},{5,7},{6,4},{7,5},{8,10},{9,11},{10,... | collective-permute-start | bytes 1179656 | tf_op jit(solution)/shard_map/ppermute | solution.py:495
  400.2 10.6 %collective-permute-start.35 = (bf16[256,768]{1,0:T(8,128)(2,1)S(1)}, bf16[256,768]{1,0:T(8,128)(2,1)S(1)}, u32[]{:S(2)}, u32[]{:S(2)}) collective-permute-start(bf16[256,768]{1,0:T(8,128)(2,1)S(1)} %get-tuple-element.237), channel_id=1, source_target_pairs={{0,2},{1,3},{2,0},{3,1},{4,6},{5,7},{6,4},{7,5},{8,10},{9,11},{10,... | collective-permute-start | bytes 1179656 | tf_op jit(solution)/shard_map/ppermute | solution.py:495
  491.8 9.6 %collective-permute-start.39 = (bf16[256,768]{1,0:T(8,128)(2,1)}, bf16[256,768]{1,0:T(8,128)(2,1)S(1)}, u32[]{:S(2)}, u32[]{:S(2)}) collective-permute-start(bf16[256,768]{1,0:T(8,128)(2,1)} %get-tuple-element.256), channel_id=1, source_target_pairs={{0,1},{1,0},{2,3},{3,2},{4,5},{5,4},{6,7},{7,6},{8,9},{9,8},{10,11... | collective-permute-start | bytes 1179656 | tf_op jit(solution)/shard_map/ppermute | solution.py:495
  495.9 184.8 %reduce-scatter.12.cloned.1.call-start = ((), (), s32[]{:S(2)}) async-start(), calls=%async_computation.8 | async-start | bytes 3317760
  497.4 11.1 %collective-permute-start.41 = (bf16[256,768]{1,0:T(8,128)(2,1)S(1)}, bf16[256,768]{1,0:T(8,128)(2,1)S(1)}, u32[]{:S(2)}, u32[]{:S(2)}) collective-permute-start(bf16[256,768]{1,0:T(8,128)(2,1)S(1)} %fusion.64), channel_id=1, source_target_pairs={{0,2},{1,3},{2,0},{3,1},{4,6},{5,7},{6,4},{7,5},{8,10},{9,11},{10,... | collective-permute-start | bytes 1179656 | tf_op jit(solution)/shard_map/ppermute | solution.py:495
  509.2 10.3 %collective-permute-start.43 = (bf16[256,768]{1,0:T(8,128)(2,1)S(1)}, bf16[256,768]{1,0:T(8,128)(2,1)S(1)}, u32[]{:S(2)}, u32[]{:S(2)}) collective-permute-start(bf16[256,768]{1,0:T(8,128)(2,1)S(1)} %get-tuple-element.234), channel_id=1, source_target_pairs={{0,2},{1,3},{2,0},{3,1},{4,6},{5,7},{6,4},{7,5},{8,10},{9,11},{10,... | collective-permute-start | bytes 1179656 | tf_op jit(solution)/shard_map/ppermute | solution.py:495
  514.3 13.6 %collective-permute-start.42 = (bf16[256,768]{1,0:T(8,128)(2,1)S(1)}, bf16[256,768]{1,0:T(8,128)(2,1)S(1)}, u32[]{:S(2)}, u32[]{:S(2)}) collective-permute-start(bf16[256,768]{1,0:T(8,128)(2,1)S(1)} %get-tuple-element.234), channel_id=1, source_target_pairs={{0,1},{1,0},{2,3},{3,2},{4,5},{5,4},{6,7},{7,6},{8,9},{9,8},{10,11... | collective-permute-start | bytes 1179656 | tf_op jit(solution)/shard_map/ppermute | solution.py:495
  527.4 195.6 %reduce-scatter.10.cloned.1.call-start = ((), (), s32[]{:S(2)}) async-start(), calls=%async_computation.7 | async-start | bytes 3317760
  537.8 11.5 %collective-permute-start.47 = (bf16[256,768]{1,0:T(8,128)(2,1)S(1)}, bf16[256,768]{1,0:T(8,128)(2,1)S(1)}, u32[]{:S(2)}, u32[]{:S(2)}) collective-permute-start(bf16[256,768]{1,0:T(8,128)(2,1)S(1)} %fusion.62), channel_id=1, source_target_pairs={{0,2},{1,3},{2,0},{3,1},{4,6},{5,7},{6,4},{7,5},{8,10},{9,11},{10,... | collective-permute-start | bytes 1179656 | tf_op jit(solution)/shard_map/ppermute | solution.py:495
  550.9 10.6 %collective-permute-start.49 = (bf16[256,768]{1,0:T(8,128)(2,1)S(1)}, bf16[256,768]{1,0:T(8,128)(2,1)S(1)}, u32[]{:S(2)}, u32[]{:S(2)}) collective-permute-start(bf16[256,768]{1,0:T(8,128)(2,1)S(1)} %get-tuple-element.232), channel_id=1, source_target_pairs={{0,2},{1,3},{2,0},{3,1},{4,6},{5,7},{6,4},{7,5},{8,10},{9,11},{10,... | collective-permute-start | bytes 1179656 | tf_op jit(solution)/shard_map/ppermute | solution.py:495
  568.0 10.2 %collective-permute-start.51 = (f32[2,1024]{1,0:T(2,128)S(1)}, f32[2,1024]{1,0:T(2,128)S(1)}, u32[]{:S(2)}, u32[]{:S(2)}) collective-permute-start(f32[2,1024]{1,0:T(2,128)S(1)} %pad_maximum_fusion.20), channel_id=1, source_target_pairs={{0,1},{1,0},{2,3},{3,2},{4,5},{5,4},{6,7},{7,6},{8,9},{9,8},{10,11... | collective-permute-start | bytes 24584 | tf_op jit(solution)/shard_map/ppermute | solution.py:495
  657.8 11.2 %collective-permute-start.55 = (bf16[256,768]{1,0:T(8,128)(2,1)S(1)}, bf16[256,768]{1,0:T(8,128)(2,1)S(1)}, u32[]{:S(2)}, u32[]{:S(2)}) collective-permute-start(bf16[256,768]{1,0:T(8,128)(2,1)S(1)} %fusion.60), channel_id=1, source_target_pairs={{0,2},{1,3},{2,0},{3,1},{4,6},{5,7},{6,4},{7,5},{8,10},{9,11},{10,... | collective-permute-start | bytes 1179656 | tf_op jit(solution)/shard_map/ppermute | solution.py:495
  672.0 36.3 %all-to-all-start = ((bf16[8,128,640]{2,1,0:T(8,128)(2,1)}), bf16[8,128,640]{2,1,0:T(8,128)(2,1)S(1)}, u32[]{:S(2)}, u32[]{:S(2)}) async-start(bf16[8,128,640]{2,1,0:T(8,128)(2,1)} %fusion.13), calls=%async_computation | async-start | bytes 2621440 | tf_op jit(solution)/shard_map/all_to_all | solution.py:543
  (179 other events, 1964.1 us)
Sparse Core Ops, SparseCore 0:
  16.5 66.6 all-gather.3
  194.7 69.2 all-gather.5
  496.0 64.1 reduce-scatter.7
  563.7 71.4 reduce-scatter.11
  639.1 83.9 reduce-scatter.9

commit v2 on v1

--- a/solution.py
+++ b/solution.py
@@ -85,18 +85,28 @@
 
 
 def forward_kernel(
-    heads, place_ref, pack_ref, w1_ref, b1_ref, w2_ref, b2_ref, g_ref, h_ref,
-    o_ref, z1_ref, a_ref, z1b_ref, c_ref, z2b_ref, w1s_ref, w2s_ref,
+    heads, dp, place_ref, pack_ref, in_ref,
+    o_ref, z1_ref, a_ref, z1b_ref, c_ref, z2b_ref, w1s_ref, w2s_ref, small_ref,
     w1, b1, w2, b2, pre, kke, cc, ecol, g1buf, g2buf, x2buf,
 ):
     H = range(heads)
 
     @pl.when(pl.program_id(0) == 0)
     def _():
-        w1[...] = w1_ref[...]
-        b1[...] = b1_ref[...]
-        w2[...] = w2_ref[...]
-        b2[...] = b2_ref[...]
+        mine = heads * HD
+        params = in_ref[...].astype(F32)
+        first, second, rest = params[:, :mine].T, params[:, mine : 2 * mine].T, params[:, 2 * mine :]
+        biases = rest.T
+        few, step = HD // dp, INNER // dp
+        small = jnp.concatenate([rest[step * d : step * d + few] for d in range(dp)], axis=0).T
+        small_ref[...] = small[heads:]
+        for h in H:
+            w1[h] = first[HD * h : HD * (h + 1)]
+            w2_own = second[HD * h : HD * (h + 1)]
+            w2[h] = w2_own - jnp.mean(w2_own, axis=0, keepdims=True)
+            b1[h] = biases[h : h + 1]
+            b2_own = small[heads + h : heads + h + 1]
+            b2[h] = b2_own - mean(b2_own)
         g1buf[...] = jnp.zeros_like(g1buf)
 
     coef, before = masks()
@@ -106,13 +116,13 @@
     for h in H:
         pre[h] = nn(xk[h], w1[h]) + b1[h]
         kke[h] = ((nt(xk[h], xk[h]) + 1.0) * (before * (rrow[h] * (1.0 / CS)))).astype(BF)
-        g, sh = g_ref[h], h_ref[h]
+        g, sh = small_ref[heads + h : heads + h + 1], small_ref[2 * heads + h : 2 * heads + h + 1]
         cval = (sh - xv[h] + xk[h]) * g
         cc[h] = cval
         mcc.append(mean(cval))
         ecol[h] = jnp.broadcast_to(rcol[h] * (1.0 / CS), (CH, HD))
         w1s_ref[0, h] = w1[h].astype(w1s_ref.dtype)
-    ma = [mean(g_ref[h] * g_ref[h]) for h in H]
+    ma = [mean(small_ref[heads + h : heads + h + 1] * small_ref[heads + h : heads + h + 1]) for h in H]
     w2v = [w2[h] for h in H]
     b2v = list(b2_start)
     for i in range(STEPS):
@@ -128,7 +138,7 @@
         c = [nt(x2b[h], w2b[h]) + b2v[h] for h in H]
         g2 = []
         for h in H:
-            g = g_ref[h]
+            g = small_ref[heads + h : heads + h + 1]
             a = g * g
             ca = c[h] * a
             cch = cc[h, rows, :]
@@ -146,9 +156,9 @@
             g2buf[h, rows, :] = g2[h].astype(BF)
             x2buf[h, rows, :] = x2b[h]
             w2s_ref[i, h] = w2b[h].astype(w2s_ref.dtype)
-            z1_ref[rows, INNER * h : INNER * (h + 1)] = z1[h]
-            a_ref[rows, INNER * h : INNER * (h + 1)] = av[h]
-            c_ref[h, rows, :] = c[h]
+            z1_ref[rows, INNER * h : INNER * (h + 1)] = z1[h].astype(BF)
+            a_ref[rows, INNER * h : INNER * (h + 1)] = av[h].astype(BF)
+            c_ref[h, rows, :] = c[h].astype(BF)
             eg2 = ecol[h, rows, :] * g2[h]
             w2v[h] = w2v[h] - tn(eg2, x2b[h])
             b2v[h] = b2v[h] - jnp.sum(eg2, axis=0, keepdims=True)
@@ -156,13 +166,13 @@
         mask = coef * rrow[h]
         g1, g2, x2 = g1buf[h], g2buf[h], x2buf[h]
         z1b = nn(xq[h], w1[h]) + b1[h] - nn((nt(xq[h], xk[h]) + 1.0) * mask, g1)
-        z1b_ref[:, INNER * h : INNER * (h + 1)] = z1b
+        z1b_ref[:, INNER * h : INNER * (h + 1)] = z1b.astype(BF)
         x2q = jax.nn.gelu(z1b, approximate=True).astype(BF)
         z2b = nt(x2q, w2[h]) + b2_start[h] - nn((nt(x2q, x2) + 1.0) * mask, g2)
         z2b = z2b - mean(z2b)
-        z2b_ref[h] = z2b
+        z2b_ref[h] = z2b.astype(BF)
         unit = z2b * lax.rsqrt(mean(z2b * z2b) + EPS)
-        o_ref[:, HD * h : HD * (h + 1)] = xq[h] + unit * g_ref[h] + h_ref[h]
+        o_ref[:, HD * h : HD * (h + 1)] = xq[h] + unit * small_ref[heads + h : heads + h + 1] + small_ref[2 * heads + h : 2 * heads + h + 1]
         ek = ecol[h] * xk[h]
         w1[h] = w1[h] - tn(ek, g1)
         b1[h] = b1[h] - jnp.sum(ecol[h][:, :1] * g1.astype(F32), axis=0, keepdims=True)
@@ -170,8 +180,7 @@
         b2[h] = b2v[h]
 
 
-def forward_call(place, pack, w1, b1, w2, b2, g, h):
-    heads = w1.shape[0]
+def forward_call(place, pack, params, heads, dp):
     rows = pack.shape[0]
     chunks = rows // CH
     per_block = chunks // 4
@@ -191,18 +200,13 @@
     by_head = pl.BlockSpec((heads, CH, HD), lambda c, place: (0, c, 0))
     sds = jax.ShapeDtypeStruct
     return pl.pallas_call(
-        functools.partial(forward_kernel, heads),
+        functools.partial(forward_kernel, heads, dp),
         grid_spec=pltpu.PrefetchScalarGridSpec(
             num_scalar_prefetch=1,
             grid=(chunks,),
             in_specs=[
                 moved(PACK),
-                whole(heads, HD, INNER),
-                whole(heads, 1, INNER),
-                whole(heads, HD, INNER),
-                whole(heads, 1, HD),
-                whole(heads, 1, HD),
-                whole(heads, 1, HD),
+                whole(*params.shape),
             ],
             out_specs=[
                 moved(heads * HD),
@@ -213,6 +217,7 @@
                 by_head,
                 pl.BlockSpec((1, heads, HD, INNER), lambda c, place: (c, 0, 0, 0)),
                 pl.BlockSpec((STEPS, heads, HD, INNER), lambda c, place: (c, 0, 0, 0)),
+                whole(5 * heads, HD),
             ],
             scratch_shapes=[
                 pltpu.VMEM((heads, HD, INNER), F32),
@@ -230,22 +235,23 @@
         ),
         out_shape=[
             sds((rows, heads * HD), F32),
-            sds((rows, heads * INNER), F32),
-            sds((rows, heads * INNER), F32),
-            sds((rows, heads * INNER), F32),
-            sds((heads, rows, HD), F32),
-            sds((heads, rows, HD), F32),
+            sds((rows, heads * INNER), BF),
+            sds((rows, heads * INNER), BF),
+            sds((rows, heads * INNER), BF),
+            sds((heads, rows, HD), BF),
+            sds((heads, rows, HD), BF),
             sds((chunks, heads, HD, INNER), BF),
             sds((chunks * STEPS, heads, HD, INNER), BF),
+            sds((5 * heads, HD), F32),
         ],
-        compiler_params=pltpu.CompilerParams(vmem_limit_bytes=40 * 2**20),
+        compiler_params=pltpu.CompilerParams(vmem_limit_bytes=56 * 2**20),
         cost_estimate=pl.CostEstimate(flops=65 * 10**9, bytes_accessed=25 * 10**6, transcendentals=0),
-    )(place, pack, w1, b1, w2, b2, g, h)
+    )(place, pack, params)
 
 
 def backward_kernel(
-    heads, place_ref, pack_ref, do_ref, z1_ref, a_ref, z1b_ref, c_ref, z2b_ref, w1s_ref, w2s_ref, g_ref, h_ref,
-    dpack_ref, dw1, db1, dw2, db2, dg_ref, dh_ref,
+    heads, shares, place_ref, pack_ref, do_ref, z1_ref, a_ref, z1b_ref, c_ref, z2b_ref, w1s_ref, w2s_ref, small_ref, post_ref,
+    dpack_ref, block_ref, dw1, db1, dw2, db2, dg_ref, dh_ref,
     dg1b, dg2b, dx2b, d1v, ad2, g2v, kkt, dz1buf, k1v, k2v, dyv, ecol, x2buf,
 ):
     H = range(heads)
@@ -268,16 +274,16 @@
     x2_all, g1_all, g2_all, ccv = [], [], [], []
     for h in H:
         wide = slice(INNER * h, INNER * (h + 1))
-        g, sh = g_ref[h], h_ref[h]
+        g, sh = small_ref[heads + h : heads + h + 1], small_ref[2 * heads + h : 2 * heads + h + 1]
         a = g * g
-        x2, d1, d2 = gelu_three(z1_ref[:, wide])
-        av = a_ref[:, wide]
+        x2, d1, d2 = gelu_three(z1_ref[:, wide].astype(F32))
+        av = a_ref[:, wide].astype(F32)
         d1v[h] = d1
         ad2[h] = av * d2
         x2 = x2.astype(BF)
         x2buf[h] = x2
         g1 = (av * d1).astype(BF)
-        c = c_ref[h]
+        c = c_ref[h].astype(F32)
         cch = (sh - xv[h] + xk[h]) * g
         ca = c * a
         q1, q2, q3, q4 = mean(c * c), mean(ca), mean(ca * c), mean(c * cch)
@@ -297,14 +303,14 @@
         ccv.append(cch)
         ecol[h] = jnp.broadcast_to(rcol[h] * (1.0 / CS), (CH, HD))
         do = do_ref[:, HD * h : HD * (h + 1)].astype(F32)
-        z2b = z2b_ref[h]
+        z2b = z2b_ref[h].astype(F32)
         sb = lax.rsqrt(mean(z2b * z2b) + EPS)
         ub = z2b * sb
         dog = do * g
         dg_ref[h] += jnp.sum(do * ub, axis=0, keepdims=True)
         dh_ref[h] += jnp.sum(do, axis=0, keepdims=True)
         dz2b = sb * (dog - mean(dog) - ub * mean(dog * ub))
-        x2q, d1b = gelu_two(z1b_ref[:, wide])
+        x2q, d1b = gelu_two(z1b_ref[:, wide].astype(F32))
         x2q = x2q.astype(BF)
         w2_start, w1_start = w2s_ref[0, h], w1s_ref[0, h]
         mask = coef * rrow[h]
@@ -349,7 +355,7 @@
         l2 = [dx2b[h, rows, :] - nn(ecol[h, rows, :] * g2[h], d2b[h]) for h in H]
         dz2 = []
         for h in H:
-            g = g_ref[h]
+            g = small_ref[heads + h : heads + h + 1]
             a = g * g
             s, m2, mau, mauu, my = (q[rows] for q in st[h][:5])
             ma = st[h][5]
@@ -373,7 +379,7 @@
             e2[h] = e2[h] + jnp.sum(dz2[h], axis=0, keepdims=True)
     dq_out, dk_out, dv_out, de_col = [], [], [], []
     for h in H:
-        g = g_ref[h]
+        g = small_ref[heads + h : heads + h + 1]
         dz1 = dz1buf[h]
         dy = dyv[h]
         g1, g2 = g1_all[h], g2_all[h]
@@ -382,7 +388,7 @@
         dkk = (-nt(dz1, g1) * (before * (rrow[h] * (1.0 / CS)))).astype(BF)
         dyg = dy * g
         dk = dxk[h] + nn(dkk, xk[h]) + tn(dkk, xk[h]) + nt(dz1, w1s_ref[0, h]) + dyg
-        dg_ref[h] += jnp.sum(dy * (uv[h] * g * 2.0 + h_ref[h] - xv[h] + xk[h]), axis=0, keepdims=True)
+        dg_ref[h] += jnp.sum(dy * (uv[h] * g * 2.0 + small_ref[2 * heads + h : 2 * heads + h + 1] - xv[h] + xk[h]), axis=0, keepdims=True)
         dh_ref[h] += jnp.sum(dyg, axis=0, keepdims=True)
         off = HD + HD * h
         dpack_ref[:, off : off + HD] = dxq[h].astype(dpack_ref.dtype)
@@ -407,10 +413,28 @@
         turned = turned - jnp.where(lane == h, de_col[h] * (1.0 / CS), 0.0)
     dpack_ref[:, :HD] = (turned * cols)[:, :HD].astype(dpack_ref.dtype)
 
-
-def backward_call(place, pack, do, saved, g, h):
+    @pl.when(pl.program_id(0) == pl.num_programs(0) - 1)
+    def _():
+        mine = heads * HD
+        block_ref[...] = jnp.zeros_like(block_ref)
+        for h in H:
+            block_ref[:, HD * h : HD * (h + 1)] = dw1[h].T
+            block_ref[:, mine + HD * h : mine + HD * (h + 1)] = dw2[h].T
+        bias = jnp.concatenate([db1[h] for h in H] + [jnp.zeros((8 - heads, INNER), F32)], axis=0)
+        block_ref[:, 2 * mine : 2 * mine + heads] = bias.T[:, :heads]
+        lines = [db2[h] for h in H] + [dg_ref[h] for h in H] + [dh_ref[h] for h in H]
+        lines += [post_ref[i : i + 1, HD * h : HD * (h + 1)] for i in range(2) for h in H]
+        few, step = HD // shares, INNER // shares
+        small = jnp.concatenate(lines + [jnp.zeros((16 - 5 * heads, HD), F32)], axis=0).T
+        for d in range(shares):
+            block_ref[step * d : step * d + few, 2 * mine + heads : 2 * mine + 6 * heads] = small[
+                few * d : few * (d + 1), : 5 * heads
+            ]
+
+
+def backward_call(place, pack, do, saved, small, post, dp):
     z1, a, z1b, c, z2b, w1s, w2s = saved
-    heads = g.shape[0]
+    heads = small.shape[0] // 5
     rows = pack.shape[0]
     chunks = rows // CH
     last = chunks - 1
@@ -431,7 +455,7 @@
     by_head = pl.BlockSpec((heads, CH, HD), lambda c, place: (0, last - c, 0))
     sds = jax.ShapeDtypeStruct
     return pl.pallas_call(
-        functools.partial(backward_kernel, heads),
+        functools.partial(backward_kernel, heads, dp),
         grid_spec=pltpu.PrefetchScalarGridSpec(
             num_scalar_prefetch=1,
             grid=(chunks,),
@@ -445,19 +469,17 @@
                 by_head,
                 pl.BlockSpec((1, heads, HD, INNER), lambda c, place: (last - c, 0, 0, 0)),
                 pl.BlockSpec((STEPS, heads, HD, INNER), lambda c, place: (last - c, 0, 0, 0)),
-                whole(heads, 1, HD),
-                whole(heads, 1, HD),
+                whole(*small.shape),
+                whole(*post.shape),
             ],
-            out_specs=[
-                moved(PACK),
-                whole(heads, HD, INNER),
-                whole(heads, 1, INNER),
-                whole(heads, HD, INNER),
-                whole(heads, 1, HD),
-                whole(heads, 1, HD),
-                whole(heads, 1, HD),
-            ],
+            out_specs=[moved(PACK), whole(INNER, PACK)],
             scratch_shapes=[
+                pltpu.VMEM((heads, HD, INNER), F32),
+                pltpu.VMEM((heads, 1, INNER), F32),
+                pltpu.VMEM((heads, HD, INNER), F32),
+                pltpu.VMEM((heads, 1, HD), F32),
+                pltpu.VMEM((heads, 1, HD), F32),
+                pltpu.VMEM((heads, 1, HD), F32),
                 pltpu.VMEM((heads, CH, INNER), F32),
                 pltpu.VMEM((heads, CH, HD), F32),
                 pltpu.VMEM((heads, CH, INNER), F32),
@@ -475,19 +497,15 @@
         ),
         out_shape=[
             sds((rows, PACK), BF),
-            sds((heads, HD, INNER), F32),
-            sds((heads, 1, INNER), F32),
-            sds((heads, HD, INNER), F32),
-            sds((heads, 1, HD), F32),
-            sds((heads, 1, HD), F32),
-            sds((heads, 1, HD), F32),
+            sds((INNER, PACK), F32),
         ],
-        compiler_params=pltpu.CompilerParams(vmem_limit_bytes=40 * 2**20),
+        compiler_params=pltpu.CompilerParams(vmem_limit_bytes=56 * 2**20),
         cost_estimate=pl.CostEstimate(flops=70 * 10**9, bytes_accessed=25 * 10**6, transcendentals=0),
-    )(place, pack, do, z1, a, z1b, c, z2b, w1s, w2s, g, h)
+    )(place, pack, do, z1, a, z1b, c, z2b, w1s, w2s, small, post)
 
 
 D = 768
+DP = ("line", "near")
 
 
 def swap(x, bit):
@@ -532,15 +550,88 @@
 
 
 def gather(x):
-    return lax.all_gather(x, "dp", axis=0, tiled=True)
+    return lax.all_gather(x, DP, axis=0, tiled=True)
+
+
+def turned(x):
+    return x.astype(F32).T.astype(BF)
+
+
+def pack_kernel(
+    q_ref, k_ref, v_ref, og_ref, r_ref, out_ref, i1_ref, i2_ref, gate_ref, up_ref, down_ref,
+    mix_ref, early_ref, late_ref, inner_ref,
+):
+    heads = r_ref.shape[0]
+    mine = heads * HD
+    ff = gate_ref.shape[2]
+    rest = 3 * ff + 2 * mine
+    for l in range(2):
+        mix, at = (mix_ref, 0) if l == 0 else (early_ref, rest)
+        mix[:, at : at + HD] = jnp.zeros((mix.shape[0], HD), BF)
+        mix[:, at : at + heads] = turned(r_ref[:, l])
+        for i, ref in enumerate((q_ref, k_ref, v_ref)):
+            mix[:, at + HD + mine * i : at + HD + mine * (i + 1)] = ref[l]
+        group = early_ref if l == 0 else late_ref
+        group[:, :ff] = gate_ref[l]
+        group[:, ff : 2 * ff] = up_ref[l]
+        group[:, 2 * ff : 3 * ff] = down_ref[l]
+        group[:, 3 * ff : 3 * ff + mine] = og_ref[l]
+        group[:, 3 * ff + mine : rest] = turned(out_ref[l])
+        base = 2 * mine * l
+        for h in range(heads):
+            inner_ref[:, base + HD * h : base + HD * (h + 1)] = i1_ref[l, h]
+            inner_ref[:, base + mine + HD * h : base + mine + HD * (h + 1)] = i2_ref[l, h]
+
+
+def weight_grad_kernel(wide_ref, two_ref, branch_ref, other_ref, pre_ref, gate_ref, up_ref, hid_ref, ho_ref, out_ref):
+    ff = gate_ref.shape[1]
+    mine = pre_ref.shape[1]
+    two = two_ref[...]
+    out_ref[:, :ff] = tn(two, gate_ref[...]).astype(BF)
+    out_ref[:, ff : 2 * ff] = tn(two, up_ref[...]).astype(BF)
+    out_ref[:, 2 * ff : 3 * ff] = tn(branch_ref[...], hid_ref[...]).astype(BF)
+    out_ref[:, 3 * ff : 3 * ff + mine] = tn(wide_ref[...], pre_ref[...]).astype(BF)
+    out_ref[:, 3 * ff + mine :] = tn(other_ref[...], ho_ref[...]).astype(BF)
+
+
+def weight_grads(wide, two, branch, other, pre, gate, up, hid, ho):
+    rows, width = wide.shape
+    step = 256
+    left = pl.BlockSpec((rows, step), lambda i: (0, i))
+
+    def whole(x):
+        return pl.BlockSpec(x.shape, lambda i: (0, 0))
+
+    cols = 3 * gate.shape[1] + 2 * pre.shape[1]
+    return pl.pallas_call(
+        weight_grad_kernel,
+        grid=(width // step,),
+        in_specs=[left] * 4 + [whole(x) for x in (pre, gate, up, hid, ho)],
+        out_specs=pl.BlockSpec((step, cols), lambda i: (i, 0)),
+        out_shape=jax.ShapeDtypeStruct((width, cols), BF),
+        compiler_params=pltpu.CompilerParams(vmem_limit_bytes=32 * 2**20),
+        cost_estimate=pl.CostEstimate(flops=2 * rows * width * cols, bytes_accessed=12 * 10**6, transcendentals=0),
+    )(wide, two, branch, other, pre, gate, up, hid, ho)
+
+
+def gather_small(x):
+    size = lax.axis_size("line")
+    other = lax.ppermute(x, "near", [(0, 1), (1, 0)])
+    first = lax.axis_index("near") == 0
+    pair = jnp.concatenate([jnp.where(first, x, other), jnp.where(first, other, x)], axis=0)
+    if size > 4:
+        return lax.all_gather(pair, "line", axis=0, tiled=True)
+    parts = [pair] + [lax.ppermute(pair, "line", [(i, (i - k) % size) for i in range(size)]) for k in range(1, size)]
+    start = lax.rem(size - lax.axis_index("line"), size) * pair.shape[0]
+    return lax.dynamic_slice_in_dim(jnp.concatenate(parts + parts[:-1], axis=0), start, size * pair.shape[0], axis=0)
 
 
 def scatter(x):
-    return lax.psum_scatter(x, "dp", scatter_dimension=0, tiled=True).astype(F32)
+    return lax.psum_scatter(x, DP, scatter_dimension=0, tiled=True).astype(F32)
 
 
 def exchange_sum(x):
-    moved = lax.all_to_all(x, "dp", split_axis=0, concat_axis=0, tiled=True)
+    moved = lax.all_to_all(x, DP, split_axis=0, concat_axis=0, tiled=True)
     return jnp.sum(moved.astype(F32), axis=0)
 
 
@@ -555,7 +646,7 @@
     inner_part = init_first.shape[3]
     small_part = inner_gain.shape[2]
     gain_part = mixer_gain.shape[1]
-    dp = lax.axis_size("dp")
+    dp = lax.axis_size("line") * lax.axis_size("near")
     tp = lax.axis_size("tensor")
     rows = hidden_in.shape[0]
     place = lax.axis_index("tensor").astype(jnp.int32).reshape(1)
@@ -564,42 +655,44 @@
     gains_here = jnp.concatenate([mixer_gain, mlp_gain], axis=0)
     gains_group = lax.all_gather(gains_here, "tensor", axis=1, tiled=True)
     span = 2 * mine + 6 * heads
-    blocks = []
+    sds = jax.ShapeDtypeStruct
+    rest_cols = 3 * ff + 2 * mine
+    mix_here, early, late, inner_here = pl.pallas_call(
+        pack_kernel,
+        out_shape=[
+            sds((part, PACK), BF),
+            sds((part, rest_cols + PACK), BF),
+            sds((part, rest_cols), BF),
+            sds((inner_part, 2 * mine * layers), BF),
+        ],
+    )(
+        w_query, w_key, w_value, w_outgate, w_rate.transpose(2, 0, 1), w_output, init_first.transpose(0, 1, 3, 2),
+        init_second, w_gate, w_up, w_down.transpose(0, 2, 1),
+    )
+    smalls = jnp.concatenate([init_second_bias, inner_gain, inner_shift, post_gain, post_shift], axis=1)
+    smalls = jnp.pad(smalls.reshape(layers * 5 * heads, small_part), ((0, 0), (0, inner_part - small_part)))
+    biases = init_first_bias.reshape(layers * heads, inner_part)
+    thin = jnp.concatenate([biases, smalls], axis=0).T
+    inner_all = gather_small(jnp.concatenate([inner_here, thin, gains_group.reshape(inner_part, -1)], axis=1))
+    mix_w = [gather(mix_here)]
+    first_group, last_group = gather(early), gather(late)
+    mix_w.append(first_group[:, rest_cols:])
+    rest_w = [first_group[:, :rest_cols], last_group]
+    states = 2 * mine * layers
+    inner_in = []
     for l in range(layers):
-        first = init_first[l].transpose(2, 0, 1).reshape(inner_part, mine)
-        second = init_second[l].transpose(1, 0, 2).reshape(inner_part, mine)
-        small = jnp.concatenate(
-            [init_second_bias[l], inner_gain[l], inner_shift[l], post_gain[l], post_shift[l]], axis=0
+        at = states + heads * layers + 5 * heads * l
+        bias_at = states + heads * l
+        inner_in.append(
+            jnp.concatenate(
+                [inner_all[:, 2 * mine * l : 2 * mine * (l + 1)], inner_all[:, bias_at : bias_at + heads],
+                 inner_all[:, at : at + 5 * heads]],
+                axis=1,
+            )
         )
-        small = jnp.pad(small.T, ((0, inner_part - small_part), (0, 0)))
-        blocks += [first, second, init_first_bias[l].T, small]
-    tail = gains_group.reshape(inner_part, -1) if gains_group.size % inner_part == 0 else None
-    blocks.append(tail)
-    inner_all = gather(jnp.concatenate(blocks, axis=1))
     gains = inner_all[:, layers * span :].reshape(dp, 2 * layers, tp * gain_part)
     gains = gains.transpose(1, 0, 2).reshape(2 * layers, D).astype(F32)
-    inner = []
-    for l in range(layers):
-        own = inner_all[:, l * span : (l + 1) * span]
-        turned = own[:, : 2 * mine + heads].T.astype(F32)
-        w1 = turned[:mine].reshape(heads, HD, INNER)
-        w2 = turned[mine : 2 * mine].reshape(heads, HD, INNER)
-        b1 = turned[2 * mine :].reshape(heads, 1, INNER)
-        small = own[:, 2 * mine + heads :].reshape(dp, inner_part, 5 * heads)[:, :small_part]
-        small = small.reshape(HD, 5 * heads).T.astype(F32).reshape(5, heads, HD)
-        w2 = w2 - jnp.mean(w2, axis=1, keepdims=True)
-        b2 = small[0] - jnp.mean(small[0], axis=1, keepdims=True)
-        inner.append((w1, b1, w2, b2[:, None], small[1][:, None], small[2][:, None], small[3], small[4]))
-
-    blank = jnp.zeros((part, lead), BF)
-    mix_w = [
-        gather(jnp.concatenate([w_rate[l], blank, w_query[l], w_key[l], w_value[l]], axis=1)) for l in range(layers)
-    ]
-    rest_w = [
-        gather(jnp.concatenate([w_outgate[l], w_gate[l], w_up[l], w_output[l].T, w_down[l].T], axis=1))
-        for l in range(layers)
-    ]
-    edges = [0, mine, mine + ff, mine + 2 * ff, 2 * mine + 2 * ff, 2 * mine + 3 * ff]
+    edges = [0, ff, 2 * ff, 3 * ff, 3 * ff + mine, 3 * ff + 2 * mine]
 
     def piece(l, i):
         return rest_w[l][:, edges[i] : edges[i + 1]]
@@ -608,37 +701,40 @@
     raw_wide = widen(hidden_in)
     kept = []
     for l in range(layers):
-        w1, b1, w2, b2, g, h, pg, ps = inner[l]
         gain_one, gain_two = gains[l], gains[layers + l]
         res_one = residual
         if l == 0:
-            wide, _ = rms(raw_wide.astype(F32), gain_one)
+            wide_res = raw_wide.astype(F32)
+            wide, wide_scale = rms(wide_res, gain_one)
+            wide_unit = wide_res * wide_scale
             scale_one = lax.rsqrt(jnp.mean(residual * residual, axis=1, keepdims=True) + EPS)
         else:
             normed, scale_one = rms(residual, gain_one)
             wide = widen(normed)
         pack = dot(wide, mix_w[l]).astype(BF)
-        outs = forward_call(place, pack, w1, b1, w2, b2, g, h)
-        inner_out, saved = outs[0], outs[1:]
-        gate_pre = dot(wide, piece(l, 0))
+        outs = forward_call(place, pack, inner_in[l], heads, dp)
+        inner_out, saved, small = outs[0], outs[1:-1], outs[-1]
+        pg = small[3 * heads : 4 * heads].reshape(-1)
+        ps = small[4 * heads : 5 * heads].reshape(-1)
+        gate_pre = dot(wide, piece(l, 3))
         sums = jnp.stack([jnp.sum(inner_out, axis=1), jnp.sum(inner_out * inner_out, axis=1)])
         sums = order_sum(sums)
         mean_all = sums[0] / D
         inv = lax.rsqrt(sums[1] / D - mean_all * mean_all + EPS)[:, None]
         unit = (inner_out - mean_all[:, None]) * inv
-        post = unit * pg.reshape(-1) + ps.reshape(-1)
+        post = unit * pg + ps
         heads_out = (jax.nn.gelu(gate_pre, approximate=True) * post).astype(BF)
-        residual = residual + narrow(dot_t(heads_out, piece(l, 3)))
+        residual = residual + narrow(dot_t(heads_out, piece(l, 4)))
         res_two = residual
         normed, scale_two = rms(residual, gain_two)
         wide_two = widen(normed)
-        gate = dot(wide_two, piece(l, 1))
-        up = dot(wide_two, piece(l, 2))
+        gate = dot(wide_two, piece(l, 0))
+        up = dot(wide_two, piece(l, 1))
         hidden = (jax.nn.silu(gate) * up).astype(BF)
-        residual = residual + narrow(dot_t(hidden, piece(l, 4)))
+        residual = residual + narrow(dot_t(hidden, piece(l, 2)))
         kept.append(
             (res_one, scale_one, wide, pack, saved, gate_pre, unit, inv, heads_out, res_two, scale_two, wide_two,
-             gate, up, hidden)
+             gate, up, hidden, small, pg, ps)
         )
     block_out = residual.astype(BF)
 
@@ -646,60 +742,53 @@
     mix_grads, rest_grads = [None] * layers, [None] * layers
     gain_grads = [None] * (2 * layers)
     for l in reversed(range(layers)):
-        w1, b1, w2, b2, g, h, pg, ps = inner[l]
         gain_one, gain_two = gains[l], gains[layers + l]
         (res_one, scale_one, wide, pack, saved, gate_pre, unit, inv, heads_out, res_two, scale_two, wide_two,
-         gate, up, hidden) = kept[l]
+         gate, up, hidden, small, pg, ps) = kept[l]
         branch = widen(cotangent if l == layers - 1 else grad.astype(BF))
-        d_hidden = dot(branch, piece(l, 4))
+        d_hidden = dot(branch, piece(l, 2))
         q = jax.nn.sigmoid(gate)
         swish = gate * q
         d_gate = (d_hidden * up * (q + swish * (1.0 - q))).astype(BF)
         d_up = (d_hidden * swish).astype(BF)
-        d_down = t_dot(branch, hidden)
-        d_norm = narrow(dot_t(d_gate, piece(l, 1)) + dot_t(d_up, piece(l, 2)))
+        d_norm = narrow(dot_t(d_gate, piece(l, 0)) + dot_t(d_up, piece(l, 1)))
         back, gain_grads[layers + l] = rms_back(res_two, scale_two, gain_two, d_norm)
         grad = grad + back
         branch_two = widen(grad.astype(BF))
-        d_heads = dot(branch_two, piece(l, 3))
-        post = unit * pg.reshape(-1) + ps.reshape(-1)
+        d_heads = dot(branch_two, piece(l, 4))
+        post = unit * pg + ps
         ge, slope = gelu_two(gate_pre)
         d_pre = (d_heads * post * slope).astype(BF)
         d_post = d_heads * ge
         d_pg = jnp.sum(d_post * unit, axis=0)
         d_ps = jnp.sum(d_post, axis=0)
-        p = d_post * pg.reshape(-1)
+        p = d_post * pg
         sums = order_sum(jnp.stack([jnp.sum(p, axis=1), jnp.sum(p * unit, axis=1)])) / D
         d_inner = inv * (p - sums[0][:, None] - unit * sums[1][:, None])
-        rest_grads[l] = scatter(
-            jnp.concatenate(
-                [t_dot(wide, d_pre), t_dot(wide_two, d_gate), t_dot(wide_two, d_up), t_dot(branch_two, heads_out), d_down],
-                axis=1,
-            ).astype(BF)
-        )
-        d_pack, dw1, db1, dw2, db2, dg, dh = backward_call(place, pack, d_inner, saved, g, h)
-        d_norm = narrow(dot_t(d_pack, mix_w[l]) + dot_t(d_pre, piece(l, 0)))
+        rest_sum = weight_grads(wide, wide_two, branch, branch_two, d_pre, d_gate, d_up, hidden, heads_out)
+        rest_sum, d_inner = lax.optimization_barrier((rest_sum, d_inner))
+        rest_grads[l] = scatter(rest_sum)
+        d_pack, block = backward_call(place, pack, d_inner, saved, small, jnp.stack([d_pg, d_ps]), dp)
+        d_wide = dot_t(d_pack, mix_w[l]) + dot_t(d_pre, piece(l, 3))
+        d_norm = narrow(d_wide)
         back, gain_grads[l] = rms_back(res_one, scale_one, gain_one, d_norm)
+        if l == 0:
+            gain_grads[l] = jnp.sum(d_wide * wide_unit, axis=0)
         grad = grad + back
-        turned = jnp.concatenate([dw1.reshape(mine, INNER), dw2.reshape(mine, INNER), db1[:, 0]], axis=0).T
-        small = jnp.concatenate([db2[:, 0], dg[:, 0], dh[:, 0], d_pg.reshape(heads, HD), d_ps.reshape(heads, HD)], axis=0)
-        small = jnp.pad(small.T.reshape(dp, small_part, 5 * heads), ((0, 0), (0, inner_part - small_part), (0, 0)))
-        block = [turned.reshape(dp, inner_part, 2 * mine + heads), small]
+        if l > 0:
+            grad, rest_grads[l] = lax.optimization_barrier((grad, rest_grads[l]))
+        mats = t_dot(wide, d_pack)
         if l == 0:
-            all_gains = jnp.stack(gain_grads).reshape(2 * layers, dp, tp * gain_part)
-            block.append(all_gains.transpose(1, 0, 2).reshape(dp, inner_part, -1))
-        block = jnp.concatenate(block, axis=2)
-        block = jnp.pad(block, ((0, 0), (0, 0), (0, PACK - block.shape[2])))
-        mixed = jnp.concatenate([t_dot(wide, d_pack).reshape(dp, part, PACK), block], axis=1).astype(BF)
-        mix_grads[l] = exchange_sum(mixed) if l == 0 else scatter(mixed)[0]
+            mats = mats + jnp.pad(jnp.stack(gain_grads).T, ((0, 0), (heads, PACK - heads - 2 * layers)))
+        mixed = jnp.concatenate([mats.reshape(dp, part, PACK), block.reshape(dp, inner_part, PACK)], axis=1)
+        mix_grads[l] = exchange_sum(mixed.astype(BF))
     grad_in = grad
 
     both = jnp.stack(mix_grads)
     mats, block = both[:, :part], both[:, part:]
     rest = jnp.stack(rest_grads)
-    d_gains = mix_grads[0][part:, span : span + gains_group.size // inner_part].reshape(2 * layers, tp, gain_part)
-    d_gains = lax.psum(d_gains, "tensor")
-    d_gains = lax.dynamic_index_in_dim(d_gains, lax.axis_index("tensor"), axis=1, keepdims=False)
+    d_gains = lax.psum(mix_grads[0][:part, heads : heads + 2 * layers].T, "tensor")
+    d_gains = lax.dynamic_slice_in_dim(d_gains, lax.axis_index("tensor") * gain_part, gain_part, axis=1)
     small = block[:, :small_part, 2 * mine + heads : span].transpose(0, 2, 1).reshape(layers, 5, heads, small_part)
 
     def matrix(i):
@@ -708,7 +797,7 @@
     def tail_piece(i):
         return rest[:, :, edges[i] : edges[i + 1]]
 
-    def states(i):
+    def state_part(i):
         return block[:, :, mine * i : mine * (i + 1)].reshape(layers, inner_part, heads, HD)
 
     return (
@@ -717,12 +806,12 @@
         matrix(0),
         matrix(1),
         matrix(2),
-        tail_piece(0),
+        tail_piece(3),
         mats[:, :, :heads],
-        tail_piece(3).transpose(0, 2, 1),
-        states(0).transpose(0, 2, 3, 1),
+        tail_piece(4).transpose(0, 2, 1),
+        state_part(0).transpose(0, 2, 3, 1),
         block[:, :, 2 * mine : 2 * mine + heads].transpose(0, 2, 1),
-        states(1).transpose(0, 2, 1, 3),
+        state_part(1).transpose(0, 2, 1, 3),
         small[:, 0],
         small[:, 1],
         small[:, 2],
@@ -730,9 +819,9 @@
         small[:, 4],
         d_gains[:layers],
         d_gains[layers:],
+        tail_piece(0),
         tail_piece(1),
-        tail_piece(2),
-        tail_piece(4).transpose(0, 2, 1),
+        tail_piece(2).transpose(0, 2, 1),
     )
 
 
@@ -746,55 +835,57 @@
 
 
 def solution(mesh):
+    shape = (mesh.shape["dp"] // 2, 2, mesh.shape["tensor"])
+    mesh = jax.sharding.Mesh(mesh.devices.reshape(shape), ("line", "near", "tensor"))
     placed = (
-        P(("dp", "tensor"), None),
-        P(("dp", "tensor"), None),
-        P(None, "dp", "tensor"),
-        P(None, "dp", "tensor"),
-        P(None, "dp", "tensor"),
-        P(None, "dp", "tensor"),
-        P(None, "dp", "tensor"),
-        P(None, "tensor", "dp"),
-        P(None, "tensor", None, "dp"),
-        P(None, "tensor", "dp"),
-        P(None, "tensor", "dp", None),
-        P(None, "tensor", "dp"),
-        P(None, "tensor", "dp"),
-        P(None, "tensor", "dp"),
-        P(None, "tensor", "dp"),
-        P(None, "tensor", "dp"),
-        P(None, ("dp", "tensor")),
-        P(None, ("dp", "tensor")),
-        P(None, "dp", "tensor"),
-        P(None, "dp", "tensor"),
-        P(None, "tensor", "dp"),
+        P(("line", "near", "tensor"), None),
+        P(("line", "near", "tensor"), None),
+        P(None, DP, "tensor"),
+        P(None, DP, "tensor"),
+        P(None, DP, "tensor"),
+        P(None, DP, "tensor"),
+        P(None, DP, "tensor"),
+        P(None, "tensor", DP),
+        P(None, "tensor", None, DP),
+        P(None, "tensor", DP),
+        P(None, "tensor", DP, None),
+        P(None, "tensor", DP),
+        P(None, "tensor", DP),
+        P(None, "tensor", DP),
+        P(None, "tensor", DP),
+        P(None, "tensor", DP),
+        P(None, ("line", "near", "tensor")),
+        P(None, ("line", "near", "tensor")),
+        P(None, DP, "tensor"),
+        P(None, DP, "tensor"),
+        P(None, "tensor", DP),
     )
     return jax.shard_map(
         per_device,
         mesh=mesh,
         in_specs=placed,
         out_specs=(
-            P(("dp", "tensor"), None),
-            P(("dp", "tensor"), None),
-            P(None, "dp", "tensor"),
-            P(None, "dp", "tensor"),
-            P(None, "dp", "tensor"),
-            P(None, "dp", "tensor"),
-            P(None, "dp", "tensor"),
-            P(None, "tensor", "dp"),
-            P(None, "tensor", None, "dp"),
-            P(None, "tensor", "dp"),
-            P(None, "tensor", "dp", None),
-            P(None, "tensor", "dp"),
-            P(None, "tensor", "dp"),
-            P(None, "tensor", "dp"),
-            P(None, "tensor", "dp"),
-            P(None, "tensor", "dp"),
-            P(None, ("dp", "tensor")),
-            P(None, ("dp", "tensor")),
-            P(None, "dp", "tensor"),
-            P(None, "dp", "tensor"),
-            P(None, "tensor", "dp"),
+            P(("line", "near", "tensor"), None),
+            P(("line", "near", "tensor"), None),
+            P(None, DP, "tensor"),
+            P(None, DP, "tensor"),
+            P(None, DP, "tensor"),
+            P(None, DP, "tensor"),
+            P(None, DP, "tensor"),
+            P(None, "tensor", DP),
+            P(None, "tensor", None, DP),
+            P(None, "tensor", DP),
+            P(None, "tensor", DP, None),
+            P(None, "tensor", DP),
+            P(None, "tensor", DP),
+            P(None, "tensor", DP),
+            P(None, "tensor", DP),
+            P(None, "tensor", DP),
+            P(None, ("line", "near", "tensor")),
+            P(None, ("line", "near", "tensor")),
+            P(None, DP, "tensor"),
+            P(None, DP, "tensor"),
+            P(None, "tensor", DP),
         ),
         check_vma=False,
     )

time: 745 us -> 672 us (0.902)
  blocking collectives: 113 us -> 54 us
  local copies, waits for them, and re-layouts: 68.1 us -> 21.9 us
  starting transfers between devices: 32.4 us -> 58.4 us
  Pallas kernels: 206 us -> 227 us
  matrix products: 85.2 us -> 66.3 us
  other arithmetic: 36.6 us -> 51.3 us
    all_gather x3 -> x1, blocking collectives: 102 us -> 37.4 us  [gather(): return lax.all_gather(x, DP, axis=0, tiled=True)]
    unnamed x331 -> x192, local copies, waits for them, and re-layouts: 44.4 us -> 11.3 us
    dot_general x12 -> x2, matrix products: 27.3 us -> 5.33 us  [t_dot(): lax.dot_general(a, b, (((0,), (0,)), ((), ())), preferred_element_type=F32)]
    pallas_call x4 -> x7, Pallas kernels: 206 us -> 227 us  [the longest x2 115 us: backward_call(): pl.pallas_call(functools.partial(backward_kernel, heads, dp), grid_spec=p...]
    all_to_all x1 -> x2, waiting for transfers between devices: 26.4 us -> 10.3 us  [exchange_sum(): moved = lax.all_to_all(x, DP, split_axis=0, concat_axis=0, tiled=True)]
    ppermute x0 -> x4, waiting for transfers between devices: none -> 12.8 us  [the longest x3 12 us: gather_small(): lax.ppermute(pair, 'line', [(i, (i - k) % size) for i in range(size)])]
    ppermute x56, starting transfers between devices: 26.6 us -> 37.3 us  [swap(): return lax.ppermute(x, 'tensor', [(i, i ^ bit) for i in range(size)])]
    all_to_all x1 -> x2, starting transfers between devices: 5.07 us -> 14 us  [exchange_sum(): moved = lax.all_to_all(x, DP, split_axis=0, concat_axis=0, tiled=True)]
  transfers between devices with their start and end apart: 62 -> 66, of which waited for: 30 -> 35; matrix products, arithmetic and copies ran while one was open for 17% -> 12% of each run, Pallas kernels for 21% -> 34%
where the time goes in v2:
time: 672 us; the launch traced here: 667 us
  Pallas kernels  227 us (34%)
  waiting for transfers between devices  172 us (26%)
  matrix products  66.3 us (10%)
  starting transfers between devices  58.4 us (9%)
  blocking collectives  54 us (8%)
  other arithmetic  51.3 us (8%)
  local copies, waits for them, and re-layouts  21.9 us (3%)
  between operations  15.9 us (2%)
    ppermute x56, waiting for transfers between devices, swap(): return lax.ppermute(x, 'tensor', [(i, i ^ bit) for i in range(size)])  148 us
    pallas_call x2, Pallas kernels, backward_call(): pl.pallas_call(functools.partial(backward_kernel, heads, dp), grid_spec=p...  115 us
    pallas_call x2, Pallas kernels, forward_call(): pl.pallas_call(functools.partial(forward_kernel, heads, dp), grid_spec=pl...  98.6 us
    all_gather x1, blocking collectives, gather(): return lax.all_gather(x, DP, axis=0, tiled=True)  37.4 us
    ppermute x56, starting transfers between devices, swap(): return lax.ppermute(x, 'tensor', [(i, i ^ bit) for i in range(size)])  37.3 us
    dot_general x12, matrix products, dot(): lax.dot_general(a, b, (((1,), (0,)), ((), ())), preferred_element_type=F32)  35 us
    dot_general x12, matrix products, dot_t(): lax.dot_general(a, b, (((1,), (1,)), ((), ())), preferred_element_type=F32)  26 us
    all_to_all x2, starting transfers between devices, exchange_sum(): moved = lax.all_to_all(x, DP, split_axis=0, concat_axis=0, tiled=True)  14 us
  transfers between devices with their start and end apart: 66, of which 35 were waited for; matrix products, arithmetic and copies ran while one was open for 12% of the time, Pallas kernels for 34%

profile of v2, /device:TPU:0, one launch (start us, length us, event | category | flops | bytes accessed | tf_op | source)
XLA Modules:
  0.0 666.9 jit_solution(5858968764872248783)
XLA Ops:
  12.4 6.0 all-gather
  32.2 37.4 %all_gather.14 = bf16[768,640]{1,0:T(8,128)(2,1)} all-gather(bf16[96,640]{1,0:T(8,128)(2,1)} %get-tuple-element.55), channel_id=1, replica_groups=mesh['line'=4,'near'=2,'tensor'=4] {'line','near'}, dimensions={0}, use_global_device_ids=true | all-gather | bytes 1105920 | tf_op jit(solution)/shard_map/all_gather | solution.py:553
  70.6 12.0 %collective-permute-done.5 = bf16[64,816]{1,0:T(8,128)(2,1)S(1)} collective-permute-done((bf16[64,816]{1,0:T(8,128)(2,1)S(1)}, bf16[64,816]{1,0:T(8,128)(2,1)S(1)}, u32[]{:S(2)}, u32[]{:S(2)}) %collective-permute-start.5) | collective-permute-done | bytes 104480 | tf_op jit(solution)/shard_map/ppermute | solution.py:624
  88.8 49.2 %shard_map.365 = (f32[1024,192]{1,0:T(8,128)}, bf16[1024,768]{1,0:T(8,128)(2,1)}, bf16[1024,768]{1,0:T(8,128)(2,1)}, bf16[1024,768]{1,0:T(8,128)(2,1)}, bf16[3,1...) custom-call(s32[1]{0:T(128)} %bitcast.8.place_ref, ...), custom_call_target="tpu_custom_call" | custom-call | flops 65000001536 | bytes 25000000 | tf_op jit(solution)/shard_map/pallas_call | solution.py:202
  153.8 9.5 %collective-permute-done.11 = bf16[256,768]{1,0:T(8,128)(2,1)} collective-permute-done((bf16[256,768]{1,0:T(8,128)(2,1)S(1)}, bf16[256,768]{1,0:T(8,128)(2,1)}, u32[]{:S(2)}, u32[]{:S(2)}) %collective-permute-start.11) | collective-permute-done | bytes 393248 | tf_op jit(solution)/shard_map/ppermute | solution.py:513
  167.4 8.6 %collective-permute-done.13 = bf16[256,768]{1,0:T(8,128)(2,1)S(1)} collective-permute-done((bf16[256,768]{1,0:T(8,128)(2,1)S(1)}, bf16[256,768]{1,0:T(8,128)(2,1)S(1)}, u32[]{:S(2)}, u32[]{:S(2)}) %collective-permute-start.13) | collective-permute-done | bytes 393248 | tf_op jit(solution)/shard_map/ppermute | solution.py:513
  186.2 9.5 %collective-permute-done.17 = bf16[256,768]{1,0:T(8,128)(2,1)} collective-permute-done((bf16[256,768]{1,0:T(8,128)(2,1)S(1)}, bf16[256,768]{1,0:T(8,128)(2,1)}, u32[]{:S(2)}, u32[]{:S(2)}) %collective-permute-start.17) | collective-permute-done | bytes 393248 | tf_op jit(solution)/shard_map/ppermute | solution.py:513
  200.3 8.6 %collective-permute-done.19 = bf16[256,768]{1,0:T(8,128)(2,1)S(1)} collective-permute-done((bf16[256,768]{1,0:T(8,128)(2,1)S(1)}, bf16[256,768]{1,0:T(8,128)(2,1)S(1)}, u32[]{:S(2)}, u32[]{:S(2)}) %collective-permute-start.19) | collective-permute-done | bytes 393248 | tf_op jit(solution)/shard_map/ppermute | solution.py:513
  214.8 49.4 %shard_map.366 = (f32[1024,192]{1,0:T(8,128)}, bf16[1024,768]{1,0:T(8,128)(2,1)}, bf16[1024,768]{1,0:T(8,128)(2,1)}, bf16[1024,768]{1,0:T(8,128)(2,1)}, bf16[3,1...) custom-call(s32[1]{0:T(128)} %bitcast.8.place_ref, ...), custom_call_target="tpu_custom_call" | custom-call | flops 65000001536 | bytes 25000000 | tf_op jit(solution)/shard_map/pallas_call | solution.py:202
  283.6 10.2 %collective-permute-done.25 = bf16[256,768]{1,0:T(8,128)(2,1)} collective-permute-done((bf16[256,768]{1,0:T(8,128)(2,1)}, bf16[256,768]{1,0:T(8,128)(2,1)}, u32[]{:S(2)}, u32[]{:S(2)}) %collective-permute-start.25) | collective-permute-done | bytes 393248 | tf_op jit(solution)/shard_map/ppermute | solution.py:513
  297.1 5.1 collective-permute-done.33
  302.7 7.0 %collective-permute-done.27 = bf16[256,768]{1,0:T(8,128)(2,1)S(1)} collective-permute-done((bf16[256,768]{1,0:T(8,128)(2,1)S(1)}, bf16[256,768]{1,0:T(8,128)(2,1)S(1)}, u32[]{:S(2)}, u32[]{:S(2)}) %collective-permute-start.27) | collective-permute-done | bytes 393248 | tf_op jit(solution)/shard_map/ppermute | solution.py:513
  322.8 9.3 %collective-permute-done.37 = bf16[256,768]{1,0:T(8,128)(2,1)S(1)} collective-permute-done((bf16[256,768]{1,0:T(8,128)(2,1)S(1)}, bf16[256,768]{1,0:T(8,128)(2,1)S(1)}, u32[]{:S(2)}, u32[]{:S(2)}) %collective-permute-start.37) | collective-permute-done | bytes 393248 | tf_op jit(solution)/shard_map/ppermute | solution.py:513
  332.4 7.2 %collective-permute-done.31 = bf16[256,768]{1,0:T(8,128)(2,1)S(1)} collective-permute-done((bf16[256,768]{1,0:T(8,128)(2,1)S(1)}, bf16[256,768]{1,0:T(8,128)(2,1)S(1)}, u32[]{:S(2)}, u32[]{:S(2)}) %collective-permute-start.31) | collective-permute-done | bytes 393248 | tf_op jit(solution)/shard_map/ppermute | solution.py:513
  343.6 8.8 %collective-permute-done.39 = bf16[256,768]{1,0:T(8,128)(2,1)S(1)} collective-permute-done((bf16[256,768]{1,0:T(8,128)(2,1)S(1)}, bf16[256,768]{1,0:T(8,128)(2,1)S(1)}, u32[]{:S(2)}, u32[]{:S(2)}) %collective-permute-start.39) | collective-permute-done | bytes 393248 | tf_op jit(solution)/shard_map/ppermute | solution.py:513
  354.1 4.9 multiply_reduce_fusion.2
  359.3 5.5 shard_map.367
  371.5 57.3 %shard_map.368 = (bf16[1024,640]{1,0:T(8,128)(2,1)}, f32[256,640]{1,0:T(8,128)}) custom-call(s32[1]{0:T(128)} %bitcast.8.place_ref, bf16[1024,640]{1,0:T(8,128)(2,1)} %convolution_convert_fusion.pack_ref, f32[1024,192]{1,0:T(8,128)} %subtract_multiply_fusion.1.do_ref, bf16[1024,768]{1,0:T(8,128)(2,1)} %get-tuple-element.62.z1_ref, ...), custom_call_target="tpu_custom_call" | custom-call | flops 70000001024 | bytes 25000000 | tf_op jit(solution)/shard_map/pallas_call | solution.py:457
  437.0 9.7 %collective-permute-done.45 = bf16[256,768]{1,0:T(8,128)(2,1)S(1)} collective-permute-done((bf16[256,768]{1,0:T(8,128)(2,1)S(1)}, bf16[256,768]{1,0:T(8,128)(2,1)S(1)}, u32[]{:S(2)}, u32[]{:S(2)}) %collective-permute-start.45) | collective-permute-done | bytes 393248 | tf_op jit(solution)/shard_map/ppermute | solution.py:513
  450.9 8.9 %collective-permute-done.47 = bf16[256,768]{1,0:T(8,128)(2,1)S(1)} collective-permute-done((bf16[256,768]{1,0:T(8,128)(2,1)S(1)}, bf16[256,768]{1,0:T(8,128)(2,1)S(1)}, u32[]{:S(2)}, u32[]{:S(2)}) %collective-permute-start.47) | collective-permute-done | bytes 393248 | tf_op jit(solution)/shard_map/ppermute | solution.py:513
  461.5 5.3 multiply_convert_fusion
  475.4 9.7 %collective-permute-done.51 = bf16[256,768]{1,0:T(8,128)(2,1)S(1)} collective-permute-done((bf16[256,768]{1,0:T(8,128)(2,1)S(1)}, bf16[256,768]{1,0:T(8,128)(2,1)S(1)}, u32[]{:S(2)}, u32[]{:S(2)}) %collective-permute-start.51) | collective-permute-done | bytes 393248 | tf_op jit(solution)/shard_map/ppermute | solution.py:513
  488.9 8.2 %collective-permute-done.53 = bf16[256,768]{1,0:T(8,128)(2,1)} collective-permute-done((bf16[256,768]{1,0:T(8,128)(2,1)S(1)}, bf16[256,768]{1,0:T(8,128)(2,1)}, u32[]{:S(2)}, u32[]{:S(2)}) %collective-permute-start.53) | collective-permute-done | bytes 393248 | tf_op jit(solution)/shard_map/ppermute | solution.py:513
  501.1 7.8 %all-to-all-start.1 = ((bf16[8,128,640]{2,1,0:T(8,128)(2,1)}), bf16[8,128,640]{2,1,0:T(8,128)(2,1)}, u32[]{:S(2)}, u32[]{:S(2)}) async-start(bf16[8,128,640]{2,1,0:T(8,128)(2,1)} %pad_maximum_fusion.8), calls=%async_computation.2 | async-start | bytes 2621440 | tf_op jit(solution)/shard_map/all_to_all | solution.py:634
  511.7 4.5 multiply_reduce_fusion
  518.8 5.7 shard_map.369
  531.9 57.3 %shard_map.370 = (bf16[1024,640]{1,0:T(8,128)(2,1)}, f32[256,640]{1,0:T(8,128)}) custom-call(s32[1]{0:T(128)} %bitcast.8.place_ref, bf16[1024,640]{1,0:T(8,128)(2,1)} %convolution_convert_fusion.1.pack_ref, f32[1024,192]{1,0:T(8,128)} %subtract_multiply_fusion.do_ref, bf16[1024,768]{1,0:T(8,128)(2,1)} %get-tuple-element.73.z1_ref, ...), custom_call_target="tpu_custom_call" | custom-call | flops 70000001024 | bytes 25000000 | tf_op jit(solution)/shard_map/pallas_call | solution.py:457
  592.3 5.8 fusion.3
  602.3 6.3 all-to-all-start
  616.7 8.4 %collective-permute-done.59 = bf16[256,768]{1,0:T(8,128)(2,1)} collective-permute-done((bf16[256,768]{1,0:T(8,128)(2,1)}, bf16[256,768]{1,0:T(8,128)(2,1)}, u32[]{:S(2)}, u32[]{:S(2)}) %collective-permute-start.59) | collective-permute-done | bytes 393248 | tf_op jit(solution)/shard_map/ppermute | solution.py:513
  629.2 10.3 %all-to-all-done = bf16[8,128,640]{2,1,0:T(8,128)(2,1)S(1)} async-done(((bf16[8,128,640]{2,1,0:T(8,128)(2,1)}), bf16[8,128,640]{2,1,0:T(8,128)(2,1)S(1)}, u32[]{:S(2)}, u32[]{:S(2)}) %all-to-all-start) | async-done | bytes 1310752 | tf_op jit(solution)/shard_map/all_to_all | solution.py:634
  642.8 10.5 %psum.7 = f32[4,96]{0,1:T(8,128)S(1)} all-reduce(f32[4,96]{0,1:T(8,128)S(1)} %slice_bitcast_fusion), channel_id=1, replica_groups=mesh['line'=4,'near'=2,'tensor'=4] {'tensor'}, use_global_device_ids=true, to_apply=%region_29.30 | all-reduce | flops 384 | bytes 3072 | tf_op jit(solution)/shard_map/psum | solution.py:790
  (472 shorter events, 187.3 us)
Async XLA Ops:
  7.2 137.6 %all-gather.4.cloned.1.call-start = ((), (), s32[]{:S(2)}) async-start(), calls=%async_computation.4 | async-start | bytes 4423680 | tf_op jit(solution)/shard_map/all_gather | solution.py:553
  24.0 59.1 %collective-permute-start.1 = (bf16[256,768]{1,0:T(8,128)(2,1)}, bf16[256,768]{1,0:T(8,128)(2,1)S(1)}, u32[]{:S(2)}, u32[]{:S(2)}) collective-permute-start(bf16[256,768]{1,0:T(8,128)(2,1)} %param.21), channel_id=1, source_target_pairs={{0,2},{1,3},{2,0},{3,1},{4,6},{5,7},{6,4},{7,5},{8,10},{9,11},{10,... | collective-permute-start | bytes 1179656 | tf_op jit(solution)/shard_map/ppermute | solution.py:513
  25.5 59.9 %collective-permute-start = (bf16[256,768]{1,0:T(8,128)(2,1)}, bf16[256,768]{1,0:T(8,128)(2,1)S(1)}, u32[]{:S(2)}, u32[]{:S(2)}) collective-permute-start(bf16[256,768]{1,0:T(8,128)(2,1)} %param.21), channel_id=1, source_target_pairs={{0,1},{1,0},{2,3},{3,2},{4,5},{5,4},{6,7},{7,6},{8,9},{9,8},{10,11... | collective-permute-start | bytes 1179656 | tf_op jit(solution)/shard_map/ppermute | solution.py:513
  25.5 246.7 %all-gather.6.cloned.1.call-start = ((), (), s32[]{:S(2)}) async-start(), calls=%async_computation.5 | async-start | bytes 3317760 | tf_op jit(solution)/shard_map/all_gather | solution.py:553
  28.2 42.4 %collective-permute-start.4 = (bf16[64,816]{1,0:T(8,128)(2,1)S(1)}, bf16[64,816]{1,0:T(8,128)(2,1)S(1)}, u32[]{:S(2)}, u32[]{:S(2)}) collective-permute-start(bf16[64,816]{1,0:T(8,128)(2,1)S(1)} %pad_maximum_fusion.15), channel_id=1, source_target_pairs={{0,24},{8,0},{16,8},{24,16},{1,25},{9,1},{17,9},{25,17},{2,26},{10... | collective-permute-start | bytes 313352 | tf_op jit(solution)/shard_map/ppermute | solution.py:624
  69.6 13.0 %collective-permute-start.5 = (bf16[64,816]{1,0:T(8,128)(2,1)S(1)}, bf16[64,816]{1,0:T(8,128)(2,1)S(1)}, u32[]{:S(2)}, u32[]{:S(2)}) collective-permute-start(bf16[64,816]{1,0:T(8,128)(2,1)S(1)} %pad_maximum_fusion.15), channel_id=1, source_target_pairs={{0,16},{8,24},{16,0},{24,8},{1,17},{9,25},{17,1},{25,9},{2,18},{10... | collective-permute-start | bytes 313352 | tf_op jit(solution)/shard_map/ppermute | solution.py:624
  69.6 13.0 %collective-permute-start.6 = (bf16[64,816]{1,0:T(8,128)(2,1)S(1)}, bf16[64,816]{1,0:T(8,128)(2,1)S(1)}, u32[]{:S(2)}, u32[]{:S(2)}) collective-permute-start(bf16[64,816]{1,0:T(8,128)(2,1)S(1)} %pad_maximum_fusion.15), channel_id=1, source_target_pairs={{0,8},{8,16},{16,24},{24,0},{1,9},{9,17},{17,25},{25,1},{2,10},{10... | collective-permute-start | bytes 313352 | tf_op jit(solution)/shard_map/ppermute | solution.py:624
  152.0 11.3 %collective-permute-start.11 = (bf16[256,768]{1,0:T(8,128)(2,1)S(1)}, bf16[256,768]{1,0:T(8,128)(2,1)}, u32[]{:S(2)}, u32[]{:S(2)}) collective-permute-start(bf16[256,768]{1,0:T(8,128)(2,1)S(1)} %fusion.68), channel_id=1, source_target_pairs={{0,2},{1,3},{2,0},{3,1},{4,6},{5,7},{6,4},{7,5},{8,10},{9,11},{10,... | collective-permute-start | bytes 1179656 | tf_op jit(solution)/shard_map/ppermute | solution.py:513
  165.6 10.4 %collective-permute-start.13 = (bf16[256,768]{1,0:T(8,128)(2,1)S(1)}, bf16[256,768]{1,0:T(8,128)(2,1)S(1)}, u32[]{:S(2)}, u32[]{:S(2)}) collective-permute-start(bf16[256,768]{1,0:T(8,128)(2,1)S(1)} %multiply_convert_fusion.8), channel_id=1, source_target_pairs={{0,2},{1,3},{2,0},{3,1},{4,6},{5,7},{6,4},{7,5},{8,10},{9,11},{10,... | collective-permute-start | bytes 1179656 | tf_op jit(solution)/shard_map/ppermute | solution.py:513
  184.3 11.3 %collective-permute-start.17 = (bf16[256,768]{1,0:T(8,128)(2,1)S(1)}, bf16[256,768]{1,0:T(8,128)(2,1)}, u32[]{:S(2)}, u32[]{:S(2)}) collective-permute-start(bf16[256,768]{1,0:T(8,128)(2,1)S(1)} %fusion.65), channel_id=1, source_target_pairs={{0,2},{1,3},{2,0},{3,1},{4,6},{5,7},{6,4},{7,5},{8,10},{9,11},{10,... | collective-permute-start | bytes 1179656 | tf_op jit(solution)/shard_map/ppermute | solution.py:513
  198.6 10.4 %collective-permute-start.19 = (bf16[256,768]{1,0:T(8,128)(2,1)S(1)}, bf16[256,768]{1,0:T(8,128)(2,1)S(1)}, u32[]{:S(2)}, u32[]{:S(2)}) collective-permute-start(bf16[256,768]{1,0:T(8,128)(2,1)S(1)} %multiply_convert_fusion.7), channel_id=1, source_target_pairs={{0,2},{1,3},{2,0},{3,1},{4,6},{5,7},{6,4},{7,5},{8,10},{9,11},{10,... | collective-permute-start | bytes 1179656 | tf_op jit(solution)/shard_map/ppermute | solution.py:513
  200.3 10.4 %collective-permute-start.18 = (bf16[256,768]{1,0:T(8,128)(2,1)S(1)}, bf16[256,768]{1,0:T(8,128)(2,1)}, u32[]{:S(2)}, u32[]{:S(2)}) collective-permute-start(bf16[256,768]{1,0:T(8,128)(2,1)S(1)} %multiply_convert_fusion.7), channel_id=1, source_target_pairs={{0,1},{1,0},{2,3},{3,2},{4,5},{5,4},{6,7},{7,6},{8,9},{9,8},{10,11... | collective-permute-start | bytes 1179656 | tf_op jit(solution)/shard_map/ppermute | solution.py:513
  209.0 238.4 %reduce-scatter.3.cloned.1.call-start = ((), (), s32[]{:S(2)}) async-start(), calls=%async_computation.6 | async-start | bytes 3317760 | tf_op jit(solution)/shard_map/reduce_scatter | solution.py:630
  281.5 12.3 %collective-permute-start.25 = (bf16[256,768]{1,0:T(8,128)(2,1)}, bf16[256,768]{1,0:T(8,128)(2,1)}, u32[]{:S(2)}, u32[]{:S(2)}) collective-permute-start(bf16[256,768]{1,0:T(8,128)(2,1)} %fusion.62), channel_id=1, source_target_pairs={{0,2},{1,3},{2,0},{3,1},{4,6},{5,7},{6,4},{7,5},{8,10},{9,11},{10,... | collective-permute-start | bytes 1179656 | tf_op jit(solution)/shard_map/ppermute | solution.py:513
  282.9 19.2 %collective-permute-start.33 = (bf16[256,768]{1,0:T(8,128)(2,1)}, bf16[256,768]{1,0:T(8,128)(2,1)}, u32[]{:S(2)}, u32[]{:S(2)}) collective-permute-start(bf16[256,768]{1,0:T(8,128)(2,1)} %param.22), channel_id=1, source_target_pairs={{0,2},{1,3},{2,0},{3,1},{4,6},{5,7},{6,4},{7,5},{8,10},{9,11},{10,... | collective-permute-start | bytes 1179656 | tf_op jit(solution)/shard_map/ppermute | solution.py:513
  295.5 14.2 %collective-permute-start.27 = (bf16[256,768]{1,0:T(8,128)(2,1)S(1)}, bf16[256,768]{1,0:T(8,128)(2,1)S(1)}, u32[]{:S(2)}, u32[]{:S(2)}) collective-permute-start(bf16[256,768]{1,0:T(8,128)(2,1)S(1)} %multiply_convert_fusion.6), channel_id=1, source_target_pairs={{0,2},{1,3},{2,0},{3,1},{4,6},{5,7},{6,4},{7,5},{8,10},{9,11},{10,... | collective-permute-start | bytes 1179656 | tf_op jit(solution)/shard_map/ppermute | solution.py:513
  297.1 13.6 %collective-permute-start.32 = (bf16[256,768]{1,0:T(8,128)(2,1)}, bf16[256,768]{1,0:T(8,128)(2,1)S(1)}, u32[]{:S(2)}, u32[]{:S(2)}) collective-permute-start(bf16[256,768]{1,0:T(8,128)(2,1)} %param.22), channel_id=1, source_target_pairs={{0,1},{1,0},{2,3},{3,2},{4,5},{5,4},{6,7},{7,6},{8,9},{9,8},{10,11... | collective-permute-start | bytes 1179656 | tf_op jit(solution)/shard_map/ppermute | solution.py:513
  320.0 12.0 %collective-permute-start.37 = (bf16[256,768]{1,0:T(8,128)(2,1)S(1)}, bf16[256,768]{1,0:T(8,128)(2,1)S(1)}, u32[]{:S(2)}, u32[]{:S(2)}) collective-permute-start(bf16[256,768]{1,0:T(8,128)(2,1)S(1)} %fusion.56), channel_id=1, source_target_pairs={{0,2},{1,3},{2,0},{3,1},{4,6},{5,7},{6,4},{7,5},{8,10},{9,11},{10,... | collective-permute-start | bytes 1179656 | tf_op jit(solution)/shard_map/ppermute | solution.py:513
  321.6 10.8 %collective-permute-start.29 = (bf16[256,768]{1,0:T(8,128)(2,1)S(1)}, bf16[256,768]{1,0:T(8,128)(2,1)S(1)}, u32[]{:S(2)}, u32[]{:S(2)}) collective-permute-start(bf16[256,768]{1,0:T(8,128)(2,1)S(1)} %get-tuple-element.226), channel_id=1, source_target_pairs={{0,1},{1,0},{2,3},{3,2},{4,5},{5,4},{6,7},{7,6},{8,9},{9,8},{10,11... | collective-permute-start | bytes 1179656 | tf_op jit(solution)/shard_map/ppermute | solution.py:513
  321.6 18.0 %collective-permute-start.31 = (bf16[256,768]{1,0:T(8,128)(2,1)S(1)}, bf16[256,768]{1,0:T(8,128)(2,1)S(1)}, u32[]{:S(2)}, u32[]{:S(2)}) collective-permute-start(bf16[256,768]{1,0:T(8,128)(2,1)S(1)} %fusion.58), channel_id=1, source_target_pairs={{0,2},{1,3},{2,0},{3,1},{4,6},{5,7},{6,4},{7,5},{8,10},{9,11},{10,... | collective-permute-start | bytes 1179656 | tf_op jit(solution)/shard_map/ppermute | solution.py:513
  342.1 10.3 %collective-permute-start.39 = (bf16[256,768]{1,0:T(8,128)(2,1)S(1)}, bf16[256,768]{1,0:T(8,128)(2,1)S(1)}, u32[]{:S(2)}, u32[]{:S(2)}) collective-permute-start(bf16[256,768]{1,0:T(8,128)(2,1)S(1)} %get-tuple-element.197), channel_id=1, source_target_pairs={{0,2},{1,3},{2,0},{3,1},{4,6},{5,7},{6,4},{7,5},{8,10},{9,11},{10,... | collective-permute-start | bytes 1179656 | tf_op jit(solution)/shard_map/ppermute | solution.py:513
  343.6 10.1 %collective-permute-start.38 = (bf16[256,768]{1,0:T(8,128)(2,1)S(1)}, bf16[256,768]{1,0:T(8,128)(2,1)S(1)}, u32[]{:S(2)}, u32[]{:S(2)}) collective-permute-start(bf16[256,768]{1,0:T(8,128)(2,1)S(1)} %get-tuple-element.197), channel_id=1, source_target_pairs={{0,1},{1,0},{2,3},{3,2},{4,5},{5,4},{6,7},{7,6},{8,9},{9,8},{10,11... | collective-permute-start | bytes 1179656 | tf_op jit(solution)/shard_map/ppermute | solution.py:513
  435.4 11.2 %collective-permute-start.45 = (bf16[256,768]{1,0:T(8,128)(2,1)S(1)}, bf16[256,768]{1,0:T(8,128)(2,1)S(1)}, u32[]{:S(2)}, u32[]{:S(2)}) collective-permute-start(bf16[256,768]{1,0:T(8,128)(2,1)S(1)} %fusion.54), channel_id=1, source_target_pairs={{0,2},{1,3},{2,0},{3,1},{4,6},{5,7},{6,4},{7,5},{8,10},{9,11},{10,... | collective-permute-start | bytes 1179656 | tf_op jit(solution)/shard_map/ppermute | solution.py:513
  449.3 10.5 %collective-permute-start.47 = (bf16[256,768]{1,0:T(8,128)(2,1)S(1)}, bf16[256,768]{1,0:T(8,128)(2,1)S(1)}, u32[]{:S(2)}, u32[]{:S(2)}) collective-permute-start(bf16[256,768]{1,0:T(8,128)(2,1)S(1)} %convert_element_type.253), channel_id=1, source_target_pairs={{0,2},{1,3},{2,0},{3,1},{4,6},{5,7},{6,4},{7,5},{8,10},{9,11},{10,... | collective-permute-start | bytes 1179656 | tf_op jit(solution)/shard_map/ppermute | solution.py:513
  473.9 11.2 %collective-permute-start.51 = (bf16[256,768]{1,0:T(8,128)(2,1)S(1)}, bf16[256,768]{1,0:T(8,128)(2,1)S(1)}, u32[]{:S(2)}, u32[]{:S(2)}) collective-permute-start(bf16[256,768]{1,0:T(8,128)(2,1)S(1)} %fusion.52), channel_id=1, source_target_pairs={{0,2},{1,3},{2,0},{3,1},{4,6},{5,7},{6,4},{7,5},{8,10},{9,11},{10,... | collective-permute-start | bytes 1179656 | tf_op jit(solution)/shard_map/ppermute | solution.py:513
  486.7 10.4 %collective-permute-start.53 = (bf16[256,768]{1,0:T(8,128)(2,1)S(1)}, bf16[256,768]{1,0:T(8,128)(2,1)}, u32[]{:S(2)}, u32[]{:S(2)}) collective-permute-start(bf16[256,768]{1,0:T(8,128)(2,1)S(1)} %get-tuple-element.194), channel_id=1, source_target_pairs={{0,2},{1,3},{2,0},{3,1},{4,6},{5,7},{6,4},{7,5},{8,10},{9,11},{10,... | collective-permute-start | bytes 1179656 | tf_op jit(solution)/shard_map/ppermute | solution.py:513
  488.9 22.7 %collective-permute-start.52 = (bf16[256,768]{1,0:T(8,128)(2,1)S(1)}, bf16[256,768]{1,0:T(8,128)(2,1)}, u32[]{:S(2)}, u32[]{:S(2)}) collective-permute-start(bf16[256,768]{1,0:T(8,128)(2,1)S(1)} %get-tuple-element.194), channel_id=1, source_target_pairs={{0,1},{1,0},{2,3},{3,2},{4,5},{5,4},{6,7},{7,6},{8,9},{9,8},{10,11... | collective-permute-start | bytes 1179656 | tf_op jit(solution)/shard_map/ppermute | solution.py:513
  497.2 14.4 %collective-permute-start.54 = (bf16[256,768]{1,0:T(8,128)(2,1)}, bf16[256,768]{1,0:T(8,128)(2,1)}, u32[]{:S(2)}, u32[]{:S(2)}) collective-permute-start(bf16[256,768]{1,0:T(8,128)(2,1)} %collective-permute-done.53), channel_id=1, source_target_pairs={{0,1},{1,0},{2,3},{3,2},{4,5},{5,4},{6,7},{7,6},{8,9},{9,8},{10,11... | collective-permute-start | bytes 1179656 | tf_op jit(solution)/shard_map/ppermute | solution.py:513
  501.1 101.3 %all-to-all-start.1 = ((bf16[8,128,640]{2,1,0:T(8,128)(2,1)}), bf16[8,128,640]{2,1,0:T(8,128)(2,1)}, u32[]{:S(2)}, u32[]{:S(2)}) async-start(bf16[8,128,640]{2,1,0:T(8,128)(2,1)} %pad_maximum_fusion.8), calls=%async_computation.2 | async-start | bytes 2621440 | tf_op jit(solution)/shard_map/all_to_all | solution.py:634
  508.8 147.4 %reduce-scatter.5.cloned.1.call-start = ((), (), s32[]{:S(2)}) async-start(), calls=%async_computation.7 | async-start | bytes 3317760 | tf_op jit(solution)/shard_map/reduce_scatter | solution.py:630
  602.3 37.1 %all-to-all-start = ((bf16[8,128,640]{2,1,0:T(8,128)(2,1)}), bf16[8,128,640]{2,1,0:T(8,128)(2,1)S(1)}, u32[]{:S(2)}, u32[]{:S(2)}) async-start(bf16[8,128,640]{2,1,0:T(8,128)(2,1)} %pad_maximum_fusion.7), calls=%async_computation.1 | async-start | bytes 2621440 | tf_op jit(solution)/shard_map/all_to_all | solution.py:634
  613.6 11.5 %collective-permute-start.59 = (bf16[256,768]{1,0:T(8,128)(2,1)}, bf16[256,768]{1,0:T(8,128)(2,1)}, u32[]{:S(2)}, u32[]{:S(2)}) collective-permute-start(bf16[256,768]{1,0:T(8,128)(2,1)} %fusion.49), channel_id=1, source_target_pairs={{0,2},{1,3},{2,0},{3,1},{4,6},{5,7},{6,4},{7,5},{8,10},{9,11},{10,... | collective-permute-start | bytes 1179656 | tf_op jit(solution)/shard_map/ppermute | solution.py:513
  (119 other events, 1029.0 us)
Sparse Core Ops, SparseCore 0:
  25.7 80.3 all-gather.3
  209.1 63.1 all-gather.5
  371.6 75.6 reduce-scatter.2
  532.0 74.0 reduce-scatter.4

commit v3 on v2

--- a/solution.py
+++ b/solution.py
@@ -14,6 +14,7 @@
 CS = 16
 CH = 128
 STEPS = CH // CS
+UNIT = 128
 PACK = 640
 EPS = 1e-6
 K0 = 0.7978845608028654
@@ -61,10 +62,10 @@
 def masks():
     row = lax.broadcasted_iota(jnp.int32, (CH, CH), 0)
     col = lax.broadcasted_iota(jnp.int32, (CH, CH), 1)
-    row_block, col_block = row // CS, col // CS
+    row_block, col_block = row >> 4, col >> 4
     inside = (row_block == col_block) & (col <= row)
     earlier = col_block < row_block
-    own = 1.0 / ((row % CS) + 1).astype(F32)
+    own = 1.0 / ((row & (CS - 1)) + 1).astype(F32)
     coef = jnp.where(earlier, 1.0 / CS, jnp.where(inside, own, 0.0))
     return coef, jnp.where(earlier, 1.0, 0.0)
 
@@ -122,6 +123,27 @@
         mcc.append(mean(cval))
         ecol[h] = jnp.broadcast_to(rcol[h] * (1.0 / CS), (CH, HD))
         w1s_ref[0, h] = w1[h].astype(w1s_ref.dtype)
+    w1_start = [w1[h].astype(BF) for h in H]
+    w2_start = [w2[h].astype(BF) for h in H]
+    b1_start = [b1[h] for h in H]
+
+    def finish(k):
+        part, upto = slice(UNIT * k, UNIT * (k + 1)), UNIT * (k + 1)
+        mask = [coef[part, :upto] * rrow[h][:, :upto] for h in H]
+        score = [nt(xq[h][part], xk[h][:upto]) + 1.0 for h in H]
+        z1b = [nn(xq[h][part], w1_start[h]) + b1_start[h] - nn(score[h] * mask[h], g1buf[h, :upto, :]) for h in H]
+        x2q = [jax.nn.gelu(z1b[h], approximate=True).astype(BF) for h in H]
+        p = [nt(x2q[h], x2buf[h, :upto, :]) + 1.0 for h in H]
+        z2b = [nt(x2q[h], w2_start[h]) + b2_start[h] - nn(p[h] * mask[h], g2buf[h, :upto, :]) for h in H]
+        for h in H:
+            z1b_ref[part, INNER * h : INNER * (h + 1)] = z1b[h].astype(BF)
+            centred = z2b[h] - mean(z2b[h])
+            z2b_ref[h, part, :] = centred.astype(BF)
+            unit = centred * lax.rsqrt(mean(centred * centred) + EPS)
+            o_ref[part, HD * h : HD * (h + 1)] = (
+                xq[h][part] + unit * small_ref[heads + h : heads + h + 1] + small_ref[2 * heads + h : 2 * heads + h + 1]
+            )
+
     ma = [mean(small_ref[heads + h : heads + h + 1] * small_ref[heads + h : heads + h + 1]) for h in H]
     w2v = [w2[h] for h in H]
     b2v = list(b2_start)
@@ -162,19 +184,11 @@
             eg2 = ecol[h, rows, :] * g2[h]
             w2v[h] = w2v[h] - tn(eg2, x2b[h])
             b2v[h] = b2v[h] - jnp.sum(eg2, axis=0, keepdims=True)
-    for h in H:
-        mask = coef * rrow[h]
-        g1, g2, x2 = g1buf[h], g2buf[h], x2buf[h]
-        z1b = nn(xq[h], w1[h]) + b1[h] - nn((nt(xq[h], xk[h]) + 1.0) * mask, g1)
-        z1b_ref[:, INNER * h : INNER * (h + 1)] = z1b.astype(BF)
-        x2q = jax.nn.gelu(z1b, approximate=True).astype(BF)
-        z2b = nt(x2q, w2[h]) + b2_start[h] - nn((nt(x2q, x2) + 1.0) * mask, g2)
-        z2b = z2b - mean(z2b)
-        z2b_ref[h] = z2b.astype(BF)
-        unit = z2b * lax.rsqrt(mean(z2b * z2b) + EPS)
-        o_ref[:, HD * h : HD * (h + 1)] = xq[h] + unit * small_ref[heads + h : heads + h + 1] + small_ref[2 * heads + h : 2 * heads + h + 1]
-        ek = ecol[h] * xk[h]
-        w1[h] = w1[h] - tn(ek, g1)
+        if (i + 1) % (UNIT // CS) == 0:
+            finish(i // (UNIT // CS))
+    for h in H:
+        g1 = g1buf[h]
+        w1[h] = w1[h] - tn(ecol[h] * xk[h], g1)
         b1[h] = b1[h] - jnp.sum(ecol[h][:, :1] * g1.astype(F32), axis=0, keepdims=True)
         w2[h] = w2v[h]
         b2[h] = b2v[h]
@@ -268,23 +282,27 @@
 
     coef, before = masks()
     xq, xk, xv, rrow, rcol = split_pack(pack_ref[...], heads)
-    uv, yv, st = [], [], []
-    dxq, dxk, dr_row = [], [], []
-    dw1_out, db1_out, dw2_out, db2_out = [], [], [], []
-    x2_all, g1_all, g2_all, ccv = [], [], [], []
-    for h in H:
-        wide = slice(INNER * h, INNER * (h + 1))
-        g, sh = small_ref[heads + h : heads + h + 1], small_ref[2 * heads + h : 2 * heads + h + 1]
-        a = g * g
-        x2, d1, d2 = gelu_three(z1_ref[:, wide].astype(F32))
-        av = a_ref[:, wide].astype(F32)
-        d1v[h] = d1
-        ad2[h] = av * d2
-        x2 = x2.astype(BF)
-        x2buf[h] = x2
-        g1 = (av * d1).astype(BF)
+    wides = [slice(INNER * h, INNER * (h + 1)) for h in H]
+    gains = [small_ref[heads + h : heads + h + 1] for h in H]
+    shifts = [small_ref[2 * heads + h : 2 * heads + h + 1] for h in H]
+    w1_start = [w1s_ref[0, h] for h in H]
+    w2_start = [w2s_ref[0, h] for h in H]
+    mask = [coef * rrow[h] for h in H]
+    do = [do_ref[:, HD * h : HD * (h + 1)].astype(F32) for h in H]
+    dz2b = []
+    for h in H:
+        z2b = z2b_ref[h].astype(F32)
+        sb = lax.rsqrt(mean(z2b * z2b) + EPS)
+        ub = z2b * sb
+        dog = do[h] * gains[h]
+        dg_ref[h] += jnp.sum(do[h] * ub, axis=0, keepdims=True)
+        dh_ref[h] += jnp.sum(do[h], axis=0, keepdims=True)
+        dz2b.append(sb * (dog - mean(dog) - ub * mean(dog * ub)))
+    uv, yv, st, g2_all = [], [], [], []
+    for h in H:
+        a = gains[h] * gains[h]
         c = c_ref[h].astype(F32)
-        cch = (sh - xv[h] + xk[h]) * g
+        cch = (shifts[h] - xv[h] + xk[h]) * gains[h]
         ca = c * a
         q1, q2, q3, q4 = mean(c * c), mean(ca), mean(ca * c), mean(c * cch)
         s = lax.rsqrt(q1 + EPS)
@@ -297,45 +315,47 @@
         yv.append(y)
         st.append((s, m2, s * q2, s * s * q3, mean(y), mean(a)))
         g2v[h] = g2
-        x2_all.append(x2)
-        g1_all.append(g1)
-        g2_all.append(g2)
-        ccv.append(cch)
+        g2_all.append(g2.astype(BF))
         ecol[h] = jnp.broadcast_to(rcol[h] * (1.0 / CS), (CH, HD))
-        do = do_ref[:, HD * h : HD * (h + 1)].astype(F32)
-        z2b = z2b_ref[h].astype(F32)
-        sb = lax.rsqrt(mean(z2b * z2b) + EPS)
-        ub = z2b * sb
-        dog = do * g
-        dg_ref[h] += jnp.sum(do * ub, axis=0, keepdims=True)
-        dh_ref[h] += jnp.sum(do, axis=0, keepdims=True)
-        dz2b = sb * (dog - mean(dog) - ub * mean(dog * ub))
-        x2q, d1b = gelu_two(z1b_ref[:, wide].astype(F32))
-        x2q = x2q.astype(BF)
-        w2_start, w1_start = w2s_ref[0, h], w1s_ref[0, h]
-        mask = coef * rrow[h]
-        p = nt(x2q, x2) + 1.0
-        dm2 = -nt(dz2b, g2)
-        dp = (mask * dm2).astype(BF)
-        dg2b[h] = -tn(mask * p, dz2b)
-        dx2b[h] = tn(dp, x2q)
-        dx2q = nn(dz2b, w2_start) + nn(dp, x2)
-        dz1b = dx2q * d1b
-        sc = nt(xq[h], xk[h]) + 1.0
-        dm1 = -nt(dz1b, g1)
-        ds = (mask * dm1).astype(BF)
-        kk = nt(xk[h], xk[h]) + 1.0
-        kkt[h] = (kk * before.T).astype(BF)
-        k1 = nn(xk[h], dw1[h]) + db1[h]
-        k1v[h] = k1
-        dg1b[h] = -tn(mask * sc, dz1b)
-        dr_row.append(jnp.sum(coef * (sc * dm1 + p * dm2), axis=0, keepdims=True))
-        dxq.append(do + nt(dz1b, w1_start) + nn(ds, xk[h]))
-        dxk.append(tn(ds, xq[h]) - nt((rcol[h] * (1.0 / CS)) * g1.astype(F32), dw1[h]))
-        dw1_out.append(tn(xq[h], dz1b))
-        db1_out.append(jnp.sum(dz1b, axis=0, keepdims=True))
-        dw2_out.append(tn(dz2b, x2q))
-        db2_out.append(jnp.sum(dz2b, axis=0, keepdims=True))
+    x2_all, g1_all, x2q, d1b = [], [], [], []
+    for h in H:
+        x2, d1, slope2 = gelu_three(z1_ref[:, wides[h]].astype(F32))
+        av = a_ref[:, wides[h]].astype(F32)
+        d1v[h] = d1
+        ad2[h] = av * slope2
+        x2_all.append(x2.astype(BF))
+        x2buf[h] = x2_all[h]
+        g1_all.append((av * d1).astype(BF))
+    for h in H:
+        value, slope = gelu_two(z1b_ref[:, wides[h]].astype(F32))
+        x2q.append(value.astype(BF))
+        d1b.append(slope)
+    before_t = before.T
+    sc = [nt(xq[h], xk[h]) + 1.0 for h in H]
+    for h in H:
+        kkt[h] = ((nt(xk[h], xk[h]) + 1.0) * before_t).astype(BF)
+    p = [nt(x2q[h], x2_all[h]) + 1.0 for h in H]
+    dm2 = [-nt(dz2b[h], g2_all[h]) for h in H]
+    dpv = [(mask[h] * dm2[h]).astype(BF) for h in H]
+    dz1b = [(nn(dz2b[h], w2_start[h]) + nn(dpv[h], x2_all[h])) * d1b[h] for h in H]
+    for h in H:
+        dg2b[h] = -tn(mask[h] * p[h], dz2b[h])
+    for h in H:
+        dx2b[h] = tn(dpv[h], x2q[h])
+    dw2_out = [tn(dz2b[h], x2q[h]) for h in H]
+    db2_out = [jnp.sum(dz2b[h], axis=0, keepdims=True) for h in H]
+    db1_out = [jnp.sum(dz1b[h], axis=0, keepdims=True) for h in H]
+    dz1c = [dz1b[h].astype(BF) for h in H]
+    dm1 = [-nt(dz1c[h], g1_all[h]) for h in H]
+    dsv = [(mask[h] * dm1[h]).astype(BF) for h in H]
+    for h in H:
+        dg1b[h] = -tn(mask[h] * sc[h], dz1c[h])
+    for h in H:
+        k1v[h] = nn(xk[h], dw1[h]) + db1[h]
+    dr_row = [jnp.sum(coef * (sc[h] * dm1[h] + p[h] * dm2[h]), axis=0, keepdims=True) for h in H]
+    dxq = [do[h] + nt(dz1c[h], w1_start[h]) + nn(dsv[h], xk[h]) for h in H]
+    dxk = [tn(dsv[h], xq[h]) - nt((rcol[h] * (1.0 / CS)) * g1_all[h].astype(F32), dw1[h]) for h in H]
+    dw1_out = [tn(xq[h], dz1c[h]) for h in H]
     d2 = [dw2[h] for h in H]
     e2 = [db2[h] for h in H]
     for i in reversed(range(STEPS)):
@@ -377,27 +397,29 @@
                 jnp.concatenate([g2[h], dz2[h]], axis=0), jnp.concatenate([da[h], x2buf[h, rows, :]], axis=0)
             )
             e2[h] = e2[h] + jnp.sum(dz2[h], axis=0, keepdims=True)
-    dq_out, dk_out, dv_out, de_col = [], [], [], []
-    for h in H:
-        g = small_ref[heads + h : heads + h + 1]
-        dz1 = dz1buf[h]
-        dy = dyv[h]
-        g1, g2 = g1_all[h], g2_all[h]
-        k1 = k1v[h] + nn(kkt[h], dz1)
-        de_col.append(jnp.sum(g1.astype(F32) * k1, axis=1, keepdims=True) + jnp.sum(g2 * k2v[h], axis=1, keepdims=True))
-        dkk = (-nt(dz1, g1) * (before * (rrow[h] * (1.0 / CS)))).astype(BF)
-        dyg = dy * g
-        dk = dxk[h] + nn(dkk, xk[h]) + tn(dkk, xk[h]) + nt(dz1, w1s_ref[0, h]) + dyg
-        dg_ref[h] += jnp.sum(dy * (uv[h] * g * 2.0 + small_ref[2 * heads + h : 2 * heads + h + 1] - xv[h] + xk[h]), axis=0, keepdims=True)
-        dh_ref[h] += jnp.sum(dyg, axis=0, keepdims=True)
+    dz1 = [dz1buf[h] for h in H]
+    k1 = [k1v[h] + nn(kkt[h], dz1[h]) for h in H]
+    dkk = [(-nt(dz1[h], g1_all[h]) * (before * (rrow[h] * (1.0 / CS)))).astype(BF) for h in H]
+    dyg = [dyv[h] * gains[h] for h in H]
+    dk = [dxk[h] + nt(dz1[h], w1_start[h]) + dyg[h] for h in H]
+    dk = [dk[h] + nn(dkk[h], xk[h]) + tn(dkk[h], xk[h]) for h in H]
+    de_col = [
+        jnp.sum(g1_all[h].astype(F32) * k1[h], axis=1, keepdims=True)
+        + jnp.sum(g2v[h] * k2v[h], axis=1, keepdims=True)
+        for h in H
+    ]
+    for h in H:
+        dg_ref[h] += jnp.sum(dyv[h] * (uv[h] * gains[h] * 2.0 + shifts[h] - xv[h] + xk[h]), axis=0, keepdims=True)
+        dh_ref[h] += jnp.sum(dyg[h], axis=0, keepdims=True)
         off = HD + HD * h
-        dpack_ref[:, off : off + HD] = dxq[h].astype(dpack_ref.dtype)
+        dpack_ref[:, off : off + HD] = dxq[h].astype(BF)
         off += HD * heads
-        dpack_ref[:, off : off + HD] = dk.astype(dpack_ref.dtype)
+        dpack_ref[:, off : off + HD] = dk[h].astype(BF)
         off += HD * heads
-        dpack_ref[:, off : off + HD] = (-dyg).astype(dpack_ref.dtype)
-        dw1[h] = dw1[h] + dw1_out[h] + tn(xk[h], dz1)
-        db1[h] = db1[h] + db1_out[h] + jnp.sum(dz1.astype(F32), axis=0, keepdims=True)
+        dpack_ref[:, off : off + HD] = (-dyg[h]).astype(BF)
+    for h in H:
+        dw1[h] = dw1[h] + dw1_out[h] + tn(xk[h], dz1[h])
+        db1[h] = db1[h] + db1_out[h] + jnp.sum(dz1[h].astype(F32), axis=0, keepdims=True)
         dw2[h] = d2[h] + dw2_out[h]
         db2[h] = e2[h] + db2_out[h]
     sub = lax.broadcasted_iota(jnp.int32, (CH, CH), 0)
@@ -518,12 +540,25 @@
     return jnp.concatenate([x, swap(x, 1), far, swap(far, 1)], axis=0)
 
 
-def narrow(total):
+def narrow_start(total):
     quarter = total.shape[0] // 4
     near, pair, far, cross = [total[quarter * i : quarter * (i + 1)] for i in range(4)]
     far = (far + swap(cross.astype(BF), 1).astype(F32)).astype(BF)
-    far = swap(far, 2)
-    return near + swap(pair.astype(BF), 1).astype(F32) + far.astype(F32)
+    return near + swap(pair.astype(BF), 1).astype(F32), far
+
+
+def narrow(total):
+    near, far = narrow_start(total)
+    return near + swap(far, 2).astype(F32)
+
+
+def sum_all(x):
+    for axis in ("tensor", "near", "line"):
+        size, bit = lax.axis_size(axis), 1
+        while bit < size:
+            x = x + lax.ppermute(x, axis, [(i, i ^ bit) for i in range(size)])
+            bit *= 2
+    return x
 
 
 def dot(a, b):
@@ -673,7 +708,10 @@
     smalls = jnp.pad(smalls.reshape(layers * 5 * heads, small_part), ((0, 0), (0, inner_part - small_part)))
     biases = init_first_bias.reshape(layers * heads, inner_part)
     thin = jnp.concatenate([biases, smalls], axis=0).T
+    raw_near, raw_far = swap(hidden_in, 1), swap(hidden_in, 2)
+    thin, raw_near, raw_far = lax.optimization_barrier((thin, raw_near, raw_far))
     inner_all = gather_small(jnp.concatenate([inner_here, thin, gains_group.reshape(inner_part, -1)], axis=1))
+    mix_here, early, inner_all = lax.optimization_barrier((mix_here, early, inner_all))
     mix_w = [gather(mix_here)]
     first_group, last_group = gather(early), gather(late)
     mix_w.append(first_group[:, rest_cols:])
@@ -698,7 +736,8 @@
         return rest_w[l][:, edges[i] : edges[i + 1]]
 
     residual = hidden_in.astype(F32)
-    raw_wide = widen(hidden_in)
+    raw_wide = jnp.concatenate([hidden_in, raw_near, raw_far, swap(raw_far, 1)], axis=0)
+    top_near, top_far = swap(cotangent, 1), swap(cotangent, 2)
     kept = []
     for l in range(layers):
         gain_one, gain_two = gains[l], gains[layers + l]
@@ -714,6 +753,8 @@
         pack = dot(wide, mix_w[l]).astype(BF)
         outs = forward_call(place, pack, inner_in[l], heads, dp)
         inner_out, saved, small = outs[0], outs[1:-1], outs[-1]
+        if l == 0:
+            inner_out, top_near, top_far = lax.optimization_barrier((inner_out, top_near, top_far))
         pg = small[3 * heads : 4 * heads].reshape(-1)
         ps = small[4 * heads : 5 * heads].reshape(-1)
         gate_pre = dot(wide, piece(l, 3))
@@ -731,13 +772,13 @@
         gate = dot(wide_two, piece(l, 0))
         up = dot(wide_two, piece(l, 1))
         hidden = (jax.nn.silu(gate) * up).astype(BF)
-        residual = residual + narrow(dot_t(hidden, piece(l, 2)))
+        near, far = narrow_start(dot_t(hidden, piece(l, 2)))
+        if l < layers - 1:
+            residual = residual + near + swap(far, 2).astype(F32)
         kept.append(
             (res_one, scale_one, wide, pack, saved, gate_pre, unit, inv, heads_out, res_two, scale_two, wide_two,
              gate, up, hidden, small, pg, ps)
         )
-    block_out = residual.astype(BF)
-
     grad = cotangent.astype(F32)
     mix_grads, rest_grads = [None] * layers, [None] * layers
     gain_grads = [None] * (2 * layers)
@@ -745,7 +786,10 @@
         gain_one, gain_two = gains[l], gains[layers + l]
         (res_one, scale_one, wide, pack, saved, gate_pre, unit, inv, heads_out, res_two, scale_two, wide_two,
          gate, up, hidden, small, pg, ps) = kept[l]
-        branch = widen(cotangent if l == layers - 1 else grad.astype(BF))
+        if l == layers - 1:
+            branch = jnp.concatenate([cotangent, top_near, top_far, swap(top_far, 1)], axis=0)
+        else:
+            branch = widen(grad.astype(BF))
         d_hidden = dot(branch, piece(l, 2))
         q = jax.nn.sigmoid(gate)
         swish = gate * q
@@ -768,27 +812,38 @@
         rest_sum = weight_grads(wide, wide_two, branch, branch_two, d_pre, d_gate, d_up, hidden, heads_out)
         rest_sum, d_inner = lax.optimization_barrier((rest_sum, d_inner))
         rest_grads[l] = scatter(rest_sum)
+        if l == layers - 1:
+            near, far, d_inner = lax.optimization_barrier((near, far, d_inner))
+            moved = swap(far, 2)
         d_pack, block = backward_call(place, pack, d_inner, saved, small, jnp.stack([d_pg, d_ps]), dp)
+        if l == layers - 1:
+            d_pack, moved = lax.optimization_barrier((d_pack, moved))
+            residual = residual + near + moved.astype(F32)
+        mats = t_dot(wide, d_pack)
+        mixed = jnp.concatenate([mats.reshape(dp, part, PACK), block.reshape(dp, inner_part, PACK)], axis=1).astype(BF)
+        mixed, d_pack = lax.optimization_barrier((mixed, d_pack))
+        mix_grads[l] = exchange_sum(mixed)
         d_wide = dot_t(d_pack, mix_w[l]) + dot_t(d_pre, piece(l, 3))
-        d_norm = narrow(d_wide)
+        near, far = narrow_start(d_wide)
+        if l == 0:
+            first_gain = jnp.sum(d_wide * wide_unit, axis=0)
+            far, first_gain = lax.optimization_barrier((far, first_gain))
+        d_norm = near + swap(far, 2).astype(F32)
         back, gain_grads[l] = rms_back(res_one, scale_one, gain_one, d_norm)
         if l == 0:
-            gain_grads[l] = jnp.sum(d_wide * wide_unit, axis=0)
+            gain_grads[l] = first_gain
         grad = grad + back
         if l > 0:
-            grad, rest_grads[l] = lax.optimization_barrier((grad, rest_grads[l]))
-        mats = t_dot(wide, d_pack)
-        if l == 0:
-            mats = mats + jnp.pad(jnp.stack(gain_grads).T, ((0, 0), (heads, PACK - heads - 2 * layers)))
-        mixed = jnp.concatenate([mats.reshape(dp, part, PACK), block.reshape(dp, inner_part, PACK)], axis=1)
-        mix_grads[l] = exchange_sum(mixed.astype(BF))
+            grad, rest_grads[l], residual = lax.optimization_barrier((grad, rest_grads[l], residual))
     grad_in = grad
+    block_out = residual.astype(BF)
 
     both = jnp.stack(mix_grads)
     mats, block = both[:, :part], both[:, part:]
     rest = jnp.stack(rest_grads)
-    d_gains = lax.psum(mix_grads[0][:part, heads : heads + 2 * layers].T, "tensor")
-    d_gains = lax.dynamic_slice_in_dim(d_gains, lax.axis_index("tensor") * gain_part, gain_part, axis=1)
+    d_gains = sum_all(jnp.stack(gain_grads))
+    spot = lax.axis_index(DP) * tp + lax.axis_index("tensor")
+    d_gains = lax.dynamic_slice_in_dim(d_gains, spot * gain_part, gain_part, axis=1)
     small = block[:, :small_part, 2 * mine + heads : span].transpose(0, 2, 1).reshape(layers, 5, heads, small_part)
 
     def matrix(i):

time: 672 us -> 635 us (0.945); the launches traced: 667 us -> 623 us
  Pallas kernels: 227 us -> 203 us
  blocking collectives: 54 us -> 40.7 us
  waiting for transfers between devices: 172 us -> 165 us
    ppermute x0 -> x5, waiting for transfers between devices: none -> 20.1 us  [sum_all(): x = x + lax.ppermute(x, axis, [(i, i ^ bit) for i in range(size)])]
    ppermute x56, waiting for transfers between devices: 148 us -> 131 us  [swap(): return lax.ppermute(x, 'tensor', [(i, i ^ bit) for i in range(size)])]
    pallas_call x2, Pallas kernels: 98.6 us -> 84.7 us  [forward_call(): pl.pallas_call(functools.partial(forward_kernel, heads, dp), grid_spec=pl...]
    psum x1 -> x0, blocking collectives: 10.5 us -> none  [per_device(): lax.psum(mix_grads[0][:part, heads:heads + 2 * layers].T, 'tensor')]
    all_to_all x2, waiting for transfers between devices: 10.3 us -> 0.01 us  [exchange_sum(): moved = lax.all_to_all(x, DP, split_axis=0, concat_axis=0, tiled=True)]
    pallas_call x2, Pallas kernels: 115 us -> 105 us  [backward_call(): pl.pallas_call(functools.partial(backward_kernel, heads, dp), grid_spec=p...]
    ppermute x0 -> x5, starting transfers between devices: none -> 7.51 us  [sum_all(): x = x + lax.ppermute(x, axis, [(i, i ^ bit) for i in range(size)])]
  transfers between devices with their start and end apart: 66 -> 71, of which waited for: 35 -> 37; matrix products, arithmetic and copies ran while one was open for 12% -> 13% of each run, Pallas kernels for 34% -> 33%
where the time goes in v3:
time: 635 us; the launch traced here: 623 us
  Pallas kernels  203 us (32%)
  waiting for transfers between devices  165 us (26%)
  matrix products  63.8 us (10%)
  other arithmetic  57.3 us (9%)
  starting transfers between devices  55.3 us (9%)
  blocking collectives  40.7 us (6%)
  local copies, waits for them, and re-layouts  21.9 us (3%)
  between operations  15.8 us (2%)
    ppermute x56, waiting for transfers between devices, swap(): return lax.ppermute(x, 'tensor', [(i, i ^ bit) for i in range(size)])  131 us
    pallas_call x2, Pallas kernels, backward_call(): pl.pallas_call(functools.partial(backward_kernel, heads, dp), grid_spec=p...  105 us
    pallas_call x2, Pallas kernels, forward_call(): pl.pallas_call(functools.partial(forward_kernel, heads, dp), grid_spec=pl...  84.7 us
    dot_general x12, matrix products, dot(): lax.dot_general(a, b, (((1,), (0,)), ((), ())), preferred_element_type=F32)  37.1 us
    all_gather x1, blocking collectives, gather(): return lax.all_gather(x, DP, axis=0, tiled=True)  35 us
    ppermute x56, starting transfers between devices, swap(): return lax.ppermute(x, 'tensor', [(i, i ^ bit) for i in range(size)])  30.8 us
    dot_general x12, matrix products, dot_t(): lax.dot_general(a, b, (((1,), (1,)), ((), ())), preferred_element_type=F32)  20.9 us
    ppermute x5, waiting for transfers between devices, sum_all(): x = x + lax.ppermute(x, axis, [(i, i ^ bit) for i in range(size)])  20.1 us
  transfers between devices with their start and end apart: 71, of which 37 were waited for; matrix products, arithmetic and copies ran while one was open for 13% of the time, Pallas kernels for 33%

profile of v3, /device:TPU:0, one launch (start us, length us, event | category | flops | bytes accessed | tf_op | source)
XLA Modules:
  0.0 622.9 jit_solution(15107088257809686788)
XLA Ops:
  15.5 5.7 all-gather
  30.8 3.9 collective-permute-start.4
  37.5 8.0 %collective-permute-done.5 = bf16[64,816]{1,0:T(8,128)(2,1)S(1)} collective-permute-done((bf16[64,816]{1,0:T(8,128)(2,1)S(1)}, bf16[64,816]{1,0:T(8,128)(2,1)S(1)}, u32[]{:S(2)}, u32[]{:S(2)}) %collective-permute-start.5) | collective-permute-done | bytes 104480 | tf_op jit(solution)/shard_map/ppermute | solution.py:659
  48.3 35.0 %all_gather.14 = bf16[768,640]{1,0:T(8,128)(2,1)S(1)} all-gather(bf16[96,640]{1,0:T(8,128)(2,1)S(1)} %copy-done.54), channel_id=1, replica_groups=mesh['line'=4,'near'=2,'tensor'=4] {'line','near'}, dimensions={0}, use_global_device_ids=true | all-gather | bytes 1105920 | tf_op jit(solution)/shard_map/all_gather | solution.py:588
  86.7 42.4 %shard_map.365 = (f32[1024,192]{1,0:T(8,128)}, bf16[1024,768]{1,0:T(8,128)(2,1)}, bf16[1024,768]{1,0:T(8,128)(2,1)}, bf16[1024,768]{1,0:T(8,128)(2,1)}, bf16[3,1...) custom-call(s32[1]{0:T(128)} %bitcast.8.place_ref, ...), custom_call_target="tpu_custom_call" | custom-call | flops 65000001536 | bytes 25000000 | tf_op jit(solution)/shard_map/pallas_call | solution.py:216
  144.3 9.9 %collective-permute-done.13 = bf16[256,768]{1,0:T(8,128)(2,1)} collective-permute-done((bf16[256,768]{1,0:T(8,128)(2,1)S(1)}, bf16[256,768]{1,0:T(8,128)(2,1)}, u32[]{:S(2)}, u32[]{:S(2)}) %collective-permute-start.13) | collective-permute-done | bytes 393248 | tf_op jit(solution)/shard_map/ppermute | solution.py:535
  157.9 9.1 %collective-permute-done.15 = bf16[256,768]{1,0:T(8,128)(2,1)S(1)} collective-permute-done((bf16[256,768]{1,0:T(8,128)(2,1)S(1)}, bf16[256,768]{1,0:T(8,128)(2,1)S(1)}, u32[]{:S(2)}, u32[]{:S(2)}) %collective-permute-start.15) | collective-permute-done | bytes 393248 | tf_op jit(solution)/shard_map/ppermute | solution.py:535
  176.7 9.9 %collective-permute-done.19 = bf16[256,768]{1,0:T(8,128)(2,1)} collective-permute-done((bf16[256,768]{1,0:T(8,128)(2,1)S(1)}, bf16[256,768]{1,0:T(8,128)(2,1)}, u32[]{:S(2)}, u32[]{:S(2)}) %collective-permute-start.19) | collective-permute-done | bytes 393248 | tf_op jit(solution)/shard_map/ppermute | solution.py:535
  190.8 9.1 %collective-permute-done.21 = bf16[256,768]{1,0:T(8,128)(2,1)S(1)} collective-permute-done((bf16[256,768]{1,0:T(8,128)(2,1)S(1)}, bf16[256,768]{1,0:T(8,128)(2,1)S(1)}, u32[]{:S(2)}, u32[]{:S(2)}) %collective-permute-start.21) | collective-permute-done | bytes 393248 | tf_op jit(solution)/shard_map/ppermute | solution.py:535
  201.8 3.9 convolution_convert_fusion.pack_ref
  205.8 42.4 %shard_map.366 = (f32[1024,192]{1,0:T(8,128)}, bf16[1024,768]{1,0:T(8,128)(2,1)}, bf16[1024,768]{1,0:T(8,128)(2,1)}, bf16[1024,768]{1,0:T(8,128)(2,1)}, bf16[3,1...) custom-call(s32[1]{0:T(128)} %bitcast.8.place_ref, ...), custom_call_target="tpu_custom_call" | custom-call | flops 65000001536 | bytes 25000000 | tf_op jit(solution)/shard_map/pallas_call | solution.py:216
  257.8 3.5 fusion.32
  268.6 10.0 %collective-permute-done.27 = bf16[256,768]{1,0:T(8,128)(2,1)} collective-permute-done((bf16[256,768]{1,0:T(8,128)(2,1)}, bf16[256,768]{1,0:T(8,128)(2,1)}, u32[]{:S(2)}, u32[]{:S(2)}) %collective-permute-start.27) | collective-permute-done | bytes 393248 | tf_op jit(solution)/shard_map/ppermute | solution.py:535
  284.5 6.2 %collective-permute-done.30 = bf16[256,768]{1,0:T(8,128)(2,1)S(1)} collective-permute-done((bf16[256,768]{1,0:T(8,128)(2,1)S(1)}, bf16[256,768]{1,0:T(8,128)(2,1)S(1)}, u32[]{:S(2)}, u32[]{:S(2)}) %collective-permute-start.30) | collective-permute-done | bytes 393248 | tf_op jit(solution)/shard_map/ppermute | solution.py:535
  293.4 3.8 multiply_convert_fusion.2
  303.8 8.7 %collective-permute-done.34 = bf16[256,768]{1,0:T(8,128)(2,1)S(1)} collective-permute-done((bf16[256,768]{1,0:T(8,128)(2,1)S(1)}, bf16[256,768]{1,0:T(8,128)(2,1)S(1)}, u32[]{:S(2)}, u32[]{:S(2)}) %collective-permute-start.34) | collective-permute-done | bytes 393248 | tf_op jit(solution)/shard_map/ppermute | solution.py:535
  318.0 6.9 %collective-permute-done.38 = bf16[256,768]{1,0:T(8,128)(2,1)S(1)} collective-permute-done((bf16[256,768]{1,0:T(8,128)(2,1)S(1)}, bf16[256,768]{1,0:T(8,128)(2,1)S(1)}, u32[]{:S(2)}, u32[]{:S(2)}) %collective-permute-start.38) | collective-permute-done | bytes 393248 | tf_op jit(solution)/shard_map/ppermute | solution.py:535
  326.6 4.7 multiply_reduce_fusion.2
  331.7 5.5 shard_map.367
  345.3 52.6 %shard_map.368 = (bf16[1024,640]{1,0:T(8,128)(2,1)}, f32[256,640]{1,0:T(8,128)}) custom-call(s32[1]{0:T(128)} %bitcast.8.place_ref, bf16[1024,640]{1,0:T(8,128)(2,1)} %convolution_convert_fusion.pack_ref, f32[1024,192]{1,0:T(8,128)} %subtract_multiply_fusion.1.do_ref, bf16[1024,768]{1,0:T(8,128)(2,1)} %get-tuple-element.93.z1_ref, ...), custom_call_target="tpu_custom_call" | custom-call | flops 70000001024 | bytes 25000000 | tf_op jit(solution)/shard_map/pallas_call | solution.py:479
  412.7 8.8 %collective-permute-done.45 = bf16[256,768]{1,0:T(8,128)(2,1)S(1)} collective-permute-done((bf16[256,768]{1,0:T(8,128)(2,1)S(1)}, bf16[256,768]{1,0:T(8,128)(2,1)S(1)}, u32[]{:S(2)}, u32[]{:S(2)}) %collective-permute-start.45) | collective-permute-done | bytes 393248 | tf_op jit(solution)/shard_map/ppermute | solution.py:535
  424.7 9.9 %collective-permute-done.47 = bf16[256,768]{1,0:T(8,128)(2,1)S(1)} collective-permute-done((bf16[256,768]{1,0:T(8,128)(2,1)S(1)}, bf16[256,768]{1,0:T(8,128)(2,1)S(1)}, u32[]{:S(2)}, u32[]{:S(2)}) %collective-permute-start.47) | collective-permute-done | bytes 393248 | tf_op jit(solution)/shard_map/ppermute | solution.py:535
  436.3 5.5 multiply_convert_fusion
  449.3 10.7 %collective-permute-done.51 = bf16[256,768]{1,0:T(8,128)(2,1)S(1)} collective-permute-done((bf16[256,768]{1,0:T(8,128)(2,1)S(1)}, bf16[256,768]{1,0:T(8,128)(2,1)S(1)}, u32[]{:S(2)}, u32[]{:S(2)}) %collective-permute-start.51) | collective-permute-done | bytes 393248 | tf_op jit(solution)/shard_map/ppermute | solution.py:535
  462.7 10.0 %collective-permute-done.53 = bf16[256,768]{1,0:T(8,128)(2,1)} collective-permute-done((bf16[256,768]{1,0:T(8,128)(2,1)S(1)}, bf16[256,768]{1,0:T(8,128)(2,1)}, u32[]{:S(2)}, u32[]{:S(2)}) %collective-permute-start.53) | collective-permute-done | bytes 393248 | tf_op jit(solution)/shard_map/ppermute | solution.py:535
  472.8 4.3 all-to-all-start.1
  479.1 4.5 multiply_reduce_fusion
  486.2 5.5 shard_map.369
  499.1 52.5 %shard_map.370 = (bf16[1024,640]{1,0:T(8,128)(2,1)}, f32[256,640]{1,0:T(8,128)}) custom-call(s32[1]{0:T(128)} %bitcast.8.place_ref, bf16[1024,640]{1,0:T(8,128)(2,1)} %convolution_convert_fusion.1.pack_ref, f32[1024,192]{1,0:T(8,128)} %subtract_multiply_fusion.do_ref, bf16[1024,768]{1,0:T(8,128)(2,1)} %get-tuple-element.111.z1_ref, ...), custom_call_target="tpu_custom_call" | custom-call | flops 70000001024 | bytes 25000000 | tf_op jit(solution)/shard_map/pallas_call | solution.py:479
  562.7 6.3 %all-to-all-start = ((bf16[8,128,640]{2,1,0:T(8,128)(2,1)}), bf16[8,128,640]{2,1,0:T(8,128)(2,1)}, u32[]{:S(2)}, u32[]{:S(2)}) async-start(bf16[8,128,640]{2,1,0:T(8,128)(2,1)} %pad_maximum_fusion.8), calls=%async_computation.1 | async-start | bytes 2621440 | tf_op jit(solution)/shard_map/all_to_all | solution.py:669
  583.0 9.2 %collective-permute-done.63 = f32[4,768]{1,0:T(4,128)S(1)} collective-permute-done((f32[4,768]{1,0:T(4,128)S(1)}, f32[4,768]{1,0:T(4,128)S(1)}, u32[]{:S(2)}, u32[]{:S(2)}) %collective-permute-start.63) | collective-permute-done | bytes 12320 | tf_op jit(solution)/shard_map/ppermute | solution.py:559
  597.2 4.2 collective-permute-done.64
  (490 shorter events, 194.7 us)
Async XLA Ops:
  7.2 128.6 %all-gather.4.cloned.1.call-start = ((), (), s32[]{:S(2)}) async-start(), calls=%async_computation.4 | async-start | bytes 4423680 | tf_op jit(solution)/shard_map/all_gather | solution.py:588
  7.2 16.7 %collective-permute-start = (bf16[256,768]{1,0:T(8,128)(2,1)}, bf16[256,768]{1,0:T(8,128)(2,1)S(1)}, u32[]{:S(2)}, u32[]{:S(2)}) collective-permute-start(bf16[256,768]{1,0:T(8,128)(2,1)} %param.21), channel_id=1, source_target_pairs={{0,1},{1,0},{2,3},{3,2},{4,5},{5,4},{6,7},{7,6},{8,9},{9,8},{10,11... | collective-permute-start | bytes 1179656 | tf_op jit(solution)/shard_map/ppermute | solution.py:535
  7.8 16.1 %collective-permute-start.1 = (bf16[256,768]{1,0:T(8,128)(2,1)}, bf16[256,768]{1,0:T(8,128)(2,1)S(1)}, u32[]{:S(2)}, u32[]{:S(2)}) collective-permute-start(bf16[256,768]{1,0:T(8,128)(2,1)} %param.21), channel_id=1, source_target_pairs={{0,2},{1,3},{2,0},{3,1},{4,6},{5,7},{6,4},{7,5},{8,10},{9,11},{10,... | collective-permute-start | bytes 1179656 | tf_op jit(solution)/shard_map/ppermute | solution.py:535
  34.7 94.4 %collective-permute-start.7 = (bf16[256,768]{1,0:T(8,128)(2,1)}, bf16[256,768]{1,0:T(8,128)(2,1)}, u32[]{:S(2)}, u32[]{:S(2)}) collective-permute-start(bf16[256,768]{1,0:T(8,128)(2,1)} %param.22), channel_id=1, source_target_pairs={{0,1},{1,0},{2,3},{3,2},{4,5},{5,4},{6,7},{7,6},{8,9},{9,8},{10,11... | collective-permute-start | bytes 1179656 | tf_op jit(solution)/shard_map/ppermute | solution.py:535
  34.7 94.4 %collective-permute-start.8 = (bf16[256,768]{1,0:T(8,128)(2,1)}, bf16[256,768]{1,0:T(8,128)(2,1)}, u32[]{:S(2)}, u32[]{:S(2)}) collective-permute-start(bf16[256,768]{1,0:T(8,128)(2,1)} %param.22), channel_id=1, source_target_pairs={{0,2},{1,3},{2,0},{3,1},{4,6},{5,7},{6,4},{7,5},{8,10},{9,11},{10,... | collective-permute-start | bytes 1179656 | tf_op jit(solution)/shard_map/ppermute | solution.py:535
  36.3 47.1 %collective-permute-start.2 = (bf16[256,768]{1,0:T(8,128)(2,1)S(1)}, bf16[256,768]{1,0:T(8,128)(2,1)S(1)}, u32[]{:S(2)}, u32[]{:S(2)}) collective-permute-start(bf16[256,768]{1,0:T(8,128)(2,1)S(1)} %collective-permute-done.1), channel_id=1, source_target_pairs={{0,1},{1,0},{2,3},{3,2},{4,5},{5,4},{6,7},{7,6},{8,9},{9,8},{10,11... | collective-permute-start | bytes 1179656 | tf_op jit(solution)/shard_map/ppermute | solution.py:535
  47.5 210.4 %all-gather.6.cloned.1.call-start = ((), (), s32[]{:S(2)}) async-start(), calls=%async_computation.5 | async-start | bytes 3317760 | tf_op jit(solution)/shard_map/all_gather | solution.py:588
  142.9 11.3 %collective-permute-start.13 = (bf16[256,768]{1,0:T(8,128)(2,1)S(1)}, bf16[256,768]{1,0:T(8,128)(2,1)}, u32[]{:S(2)}, u32[]{:S(2)}) collective-permute-start(bf16[256,768]{1,0:T(8,128)(2,1)S(1)} %fusion.65), channel_id=1, source_target_pairs={{0,2},{1,3},{2,0},{3,1},{4,6},{5,7},{6,4},{7,5},{8,10},{9,11},{10,... | collective-permute-start | bytes 1179656 | tf_op jit(solution)/shard_map/ppermute | solution.py:535
  156.6 10.4 %collective-permute-start.15 = (bf16[256,768]{1,0:T(8,128)(2,1)S(1)}, bf16[256,768]{1,0:T(8,128)(2,1)S(1)}, u32[]{:S(2)}, u32[]{:S(2)}) collective-permute-start(bf16[256,768]{1,0:T(8,128)(2,1)S(1)} %multiply_convert_fusion.8), channel_id=1, source_target_pairs={{0,2},{1,3},{2,0},{3,1},{4,6},{5,7},{6,4},{7,5},{8,10},{9,11},{10,... | collective-permute-start | bytes 1179656 | tf_op jit(solution)/shard_map/ppermute | solution.py:535
  157.9 9.1 %collective-permute-start.14 = (bf16[256,768]{1,0:T(8,128)(2,1)S(1)}, bf16[256,768]{1,0:T(8,128)(2,1)S(1)}, u32[]{:S(2)}, u32[]{:S(2)}) collective-permute-start(bf16[256,768]{1,0:T(8,128)(2,1)S(1)} %multiply_convert_fusion.8), channel_id=1, source_target_pairs={{0,1},{1,0},{2,3},{3,2},{4,5},{5,4},{6,7},{7,6},{8,9},{9,8},{10,11... | collective-permute-start | bytes 1179656 | tf_op jit(solution)/shard_map/ppermute | solution.py:535
  175.2 11.3 %collective-permute-start.19 = (bf16[256,768]{1,0:T(8,128)(2,1)S(1)}, bf16[256,768]{1,0:T(8,128)(2,1)}, u32[]{:S(2)}, u32[]{:S(2)}) collective-permute-start(bf16[256,768]{1,0:T(8,128)(2,1)S(1)} %fusion.62), channel_id=1, source_target_pairs={{0,2},{1,3},{2,0},{3,1},{4,6},{5,7},{6,4},{7,5},{8,10},{9,11},{10,... | collective-permute-start | bytes 1179656 | tf_op jit(solution)/shard_map/ppermute | solution.py:535
  189.5 10.4 %collective-permute-start.21 = (bf16[256,768]{1,0:T(8,128)(2,1)S(1)}, bf16[256,768]{1,0:T(8,128)(2,1)S(1)}, u32[]{:S(2)}, u32[]{:S(2)}) collective-permute-start(bf16[256,768]{1,0:T(8,128)(2,1)S(1)} %multiply_convert_fusion.7), channel_id=1, source_target_pairs={{0,2},{1,3},{2,0},{3,1},{4,6},{5,7},{6,4},{7,5},{8,10},{9,11},{10,... | collective-permute-start | bytes 1179656 | tf_op jit(solution)/shard_map/ppermute | solution.py:535
  190.8 11.0 %collective-permute-start.20 = (bf16[256,768]{1,0:T(8,128)(2,1)S(1)}, bf16[256,768]{1,0:T(8,128)(2,1)}, u32[]{:S(2)}, u32[]{:S(2)}) collective-permute-start(bf16[256,768]{1,0:T(8,128)(2,1)S(1)} %multiply_convert_fusion.7), channel_id=1, source_target_pairs={{0,1},{1,0},{2,3},{3,2},{4,5},{5,4},{6,7},{7,6},{8,9},{9,8},{10,11... | collective-permute-start | bytes 1179656 | tf_op jit(solution)/shard_map/ppermute | solution.py:535
  199.9 222.3 %reduce-scatter.3.cloned.1.call-start = ((), (), s32[]{:S(2)}) async-start(), calls=%async_computation.6 | async-start | bytes 3317760 | tf_op jit(solution)/shard_map/reduce_scatter | solution.py:665
  267.1 11.5 %collective-permute-start.27 = (bf16[256,768]{1,0:T(8,128)(2,1)}, bf16[256,768]{1,0:T(8,128)(2,1)}, u32[]{:S(2)}, u32[]{:S(2)}) collective-permute-start(bf16[256,768]{1,0:T(8,128)(2,1)} %fusion.59), channel_id=1, source_target_pairs={{0,2},{1,3},{2,0},{3,1},{4,6},{5,7},{6,4},{7,5},{8,10},{9,11},{10,... | collective-permute-start | bytes 1179656 | tf_op jit(solution)/shard_map/ppermute | solution.py:535
  280.3 10.4 %collective-permute-start.30 = (bf16[256,768]{1,0:T(8,128)(2,1)S(1)}, bf16[256,768]{1,0:T(8,128)(2,1)S(1)}, u32[]{:S(2)}, u32[]{:S(2)}) collective-permute-start(bf16[256,768]{1,0:T(8,128)(2,1)S(1)} %multiply_convert_fusion.6), channel_id=1, source_target_pairs={{0,2},{1,3},{2,0},{3,1},{4,6},{5,7},{6,4},{7,5},{8,10},{9,11},{10,... | collective-permute-start | bytes 1179656 | tf_op jit(solution)/shard_map/ppermute | solution.py:535
  301.2 11.2 %collective-permute-start.34 = (bf16[256,768]{1,0:T(8,128)(2,1)S(1)}, bf16[256,768]{1,0:T(8,128)(2,1)S(1)}, u32[]{:S(2)}, u32[]{:S(2)}) collective-permute-start(bf16[256,768]{1,0:T(8,128)(2,1)S(1)} %fusion.57), channel_id=1, source_target_pairs={{0,2},{1,3},{2,0},{3,1},{4,6},{5,7},{6,4},{7,5},{8,10},{9,11},{10,... | collective-permute-start | bytes 1179656 | tf_op jit(solution)/shard_map/ppermute | solution.py:535
  314.6 10.3 %collective-permute-start.38 = (bf16[256,768]{1,0:T(8,128)(2,1)S(1)}, bf16[256,768]{1,0:T(8,128)(2,1)S(1)}, u32[]{:S(2)}, u32[]{:S(2)}) collective-permute-start(bf16[256,768]{1,0:T(8,128)(2,1)S(1)} %get-tuple-element.239), channel_id=1, source_target_pairs={{0,2},{1,3},{2,0},{3,1},{4,6},{5,7},{6,4},{7,5},{8,10},{9,11},{10,... | collective-permute-start | bytes 1179656 | tf_op jit(solution)/shard_map/ppermute | solution.py:535
  343.8 55.2 %collective-permute-start.42 = (bf16[256,768]{1,0:T(8,128)(2,1)}, bf16[256,768]{1,0:T(8,128)(2,1)}, u32[]{:S(2)}, u32[]{:S(2)}) collective-permute-start(bf16[256,768]{1,0:T(8,128)(2,1)} %get-tuple-element.101), channel_id=1, source_target_pairs={{0,2},{1,3},{2,0},{3,1},{4,6},{5,7},{6,4},{7,5},{8,10},{9,11},{10,... | collective-permute-start | bytes 1179656 | tf_op jit(solution)/shard_map/ppermute | solution.py:535
  410.3 11.2 %collective-permute-start.45 = (bf16[256,768]{1,0:T(8,128)(2,1)S(1)}, bf16[256,768]{1,0:T(8,128)(2,1)S(1)}, u32[]{:S(2)}, u32[]{:S(2)}) collective-permute-start(bf16[256,768]{1,0:T(8,128)(2,1)S(1)} %fusion.54), channel_id=1, source_target_pairs={{0,2},{1,3},{2,0},{3,1},{4,6},{5,7},{6,4},{7,5},{8,10},{9,11},{10,... | collective-permute-start | bytes 1179656 | tf_op jit(solution)/shard_map/ppermute | solution.py:535
  424.2 10.4 %collective-permute-start.47 = (bf16[256,768]{1,0:T(8,128)(2,1)S(1)}, bf16[256,768]{1,0:T(8,128)(2,1)S(1)}, u32[]{:S(2)}, u32[]{:S(2)}) collective-permute-start(bf16[256,768]{1,0:T(8,128)(2,1)S(1)} %convert_element_type.251), channel_id=1, source_target_pairs={{0,2},{1,3},{2,0},{3,1},{4,6},{5,7},{6,4},{7,5},{8,10},{9,11},{10,... | collective-permute-start | bytes 1179656 | tf_op jit(solution)/shard_map/ppermute | solution.py:535
  424.7 9.9 %collective-permute-start.46 = (bf16[256,768]{1,0:T(8,128)(2,1)S(1)}, bf16[256,768]{1,0:T(8,128)(2,1)S(1)}, u32[]{:S(2)}, u32[]{:S(2)}) collective-permute-start(bf16[256,768]{1,0:T(8,128)(2,1)S(1)} %convert_element_type.251), channel_id=1, source_target_pairs={{0,1},{1,0},{2,3},{3,2},{4,5},{5,4},{6,7},{7,6},{8,9},{9,8},{10,11... | collective-permute-start | bytes 1179656 | tf_op jit(solution)/shard_map/ppermute | solution.py:535
  448.8 11.2 %collective-permute-start.51 = (bf16[256,768]{1,0:T(8,128)(2,1)S(1)}, bf16[256,768]{1,0:T(8,128)(2,1)S(1)}, u32[]{:S(2)}, u32[]{:S(2)}) collective-permute-start(bf16[256,768]{1,0:T(8,128)(2,1)S(1)} %fusion.52), channel_id=1, source_target_pairs={{0,2},{1,3},{2,0},{3,1},{4,6},{5,7},{6,4},{7,5},{8,10},{9,11},{10,... | collective-permute-start | bytes 1179656 | tf_op jit(solution)/shard_map/ppermute | solution.py:535
  462.2 10.4 %collective-permute-start.53 = (bf16[256,768]{1,0:T(8,128)(2,1)S(1)}, bf16[256,768]{1,0:T(8,128)(2,1)}, u32[]{:S(2)}, u32[]{:S(2)}) collective-permute-start(bf16[256,768]{1,0:T(8,128)(2,1)S(1)} %get-tuple-element.236), channel_id=1, source_target_pairs={{0,2},{1,3},{2,0},{3,1},{4,6},{5,7},{6,4},{7,5},{8,10},{9,11},{10,... | collective-permute-start | bytes 1179656 | tf_op jit(solution)/shard_map/ppermute | solution.py:535
  462.6 16.1 %collective-permute-start.52 = (bf16[256,768]{1,0:T(8,128)(2,1)S(1)}, bf16[256,768]{1,0:T(8,128)(2,1)}, u32[]{:S(2)}, u32[]{:S(2)}) collective-permute-start(bf16[256,768]{1,0:T(8,128)(2,1)S(1)} %get-tuple-element.236), channel_id=1, source_target_pairs={{0,1},{1,0},{2,3},{3,2},{4,5},{5,4},{6,7},{7,6},{8,9},{9,8},{10,11... | collective-permute-start | bytes 1179656 | tf_op jit(solution)/shard_map/ppermute | solution.py:535
  472.8 89.9 %all-to-all-start.1 = ((bf16[8,128,640]{2,1,0:T(8,128)(2,1)}), bf16[8,128,640]{2,1,0:T(8,128)(2,1)}, u32[]{:S(2)}, u32[]{:S(2)}) async-start(bf16[8,128,640]{2,1,0:T(8,128)(2,1)} %pad_maximum_fusion.7), calls=%async_computation.2 | async-start | bytes 2621440 | tf_op jit(solution)/shard_map/all_to_all | solution.py:669
  477.1 135.3 %reduce-scatter.5.cloned.1.call-start = ((), (), s32[]{:S(2)}) async-start(), calls=%async_computation.7 | async-start | bytes 3317760 | tf_op jit(solution)/shard_map/reduce_scatter | solution.py:665
  562.7 43.5 %all-to-all-start = ((bf16[8,128,640]{2,1,0:T(8,128)(2,1)}), bf16[8,128,640]{2,1,0:T(8,128)(2,1)}, u32[]{:S(2)}, u32[]{:S(2)}) async-start(bf16[8,128,640]{2,1,0:T(8,128)(2,1)} %pad_maximum_fusion.8), calls=%async_computation.1 | async-start | bytes 2621440 | tf_op jit(solution)/shard_map/all_to_all | solution.py:669
  581.2 11.0 %collective-permute-start.63 = (f32[4,768]{1,0:T(4,128)S(1)}, f32[4,768]{1,0:T(4,128)S(1)}, u32[]{:S(2)}, u32[]{:S(2)}) collective-permute-start(f32[4,768]{1,0:T(4,128)S(1)} %add.390), channel_id=1, source_target_pairs={{0,8},{8,0},{16,24},{24,16},{1,9},{9,1},{17,25},{25,17},{2,10},{10... | collective-permute-start | bytes 36872 | tf_op jit(solution)/shard_map/ppermute | solution.py:559
  582.4 19.6 %collective-permute-start.57 = (bf16[256,768]{1,0:T(8,128)(2,1)}, bf16[256,768]{1,0:T(8,128)(2,1)S(1)}, u32[]{:S(2)}, u32[]{:S(2)}) collective-permute-start(bf16[256,768]{1,0:T(8,128)(2,1)} %get-tuple-element.262), channel_id=1, source_target_pairs={{0,1},{1,0},{2,3},{3,2},{4,5},{5,4},{6,7},{7,6},{8,9},{9,8},{10,11... | collective-permute-start | bytes 1179656 | tf_op jit(solution)/shard_map/ppermute | solution.py:535
  582.4 19.6 %collective-permute-start.59 = (bf16[256,768]{1,0:T(8,128)(2,1)}, bf16[256,768]{1,0:T(8,128)(2,1)S(1)}, u32[]{:S(2)}, u32[]{:S(2)}) collective-permute-start(bf16[256,768]{1,0:T(8,128)(2,1)} %fusion.49), channel_id=1, source_target_pairs={{0,2},{1,3},{2,0},{3,1},{4,6},{5,7},{6,4},{7,5},{8,10},{9,11},{10,... | collective-permute-start | bytes 1179656 | tf_op jit(solution)/shard_map/ppermute | solution.py:535
  592.2 9.2 %collective-permute-start.64 = (f32[4,768]{1,0:T(4,128)S(1)}, f32[4,768]{1,0:T(4,128)S(1)}, u32[]{:S(2)}, u32[]{:S(2)}) collective-permute-start(f32[4,768]{1,0:T(4,128)S(1)} %add.391), channel_id=1, source_target_pairs={{0,16},{8,24},{16,0},{24,8},{1,17},{9,25},{17,1},{25,9},{2,18},{10... | collective-permute-start | bytes 36872 | tf_op jit(solution)/shard_map/ppermute | solution.py:559
  (127 other events, 1166.4 us)
Sparse Core Ops, SparseCore 0:
  47.6 78.3 all-gather.3
  200.0 57.7 all-gather.5
  345.4 70.4 reduce-scatter.2
  499.2 72.8 reduce-scatter.4

commit v4 on v3

--- a/solution.py
+++ b/solution.py
@@ -547,18 +547,17 @@
     return near + swap(pair.astype(BF), 1).astype(F32), far
 
 
-def narrow(total):
+def narrow(total, beside=None):
     near, far = narrow_start(total)
-    return near + swap(far, 2).astype(F32)
-
-
-def sum_all(x):
-    for axis in ("tensor", "near", "line"):
-        size, bit = lax.axis_size(axis), 1
-        while bit < size:
-            x = x + lax.ppermute(x, axis, [(i, i ^ bit) for i in range(size)])
-            bit *= 2
-    return x
+    moved = swap(far, 2)
+    if beside is None:
+        return near + moved.astype(F32)
+    moved, beside = lax.optimization_barrier((moved, beside))
+    return near + moved.astype(F32), beside
+
+
+def sum_group(x):
+    return x + swap(x, 1) + swap(x, 2) + swap(x, 3)
 
 
 def dot(a, b):
@@ -618,35 +617,60 @@
             inner_ref[:, base + mine + HD * h : base + mine + HD * (h + 1)] = i2_ref[l, h]
 
 
-def weight_grad_kernel(wide_ref, two_ref, branch_ref, other_ref, pre_ref, gate_ref, up_ref, hid_ref, ho_ref, out_ref):
+def feed_grad_kernel(two_ref, branch_ref, gate_ref, up_ref, hid_ref, out_ref):
     ff = gate_ref.shape[1]
-    mine = pre_ref.shape[1]
     two = two_ref[...]
     out_ref[:, :ff] = tn(two, gate_ref[...]).astype(BF)
     out_ref[:, ff : 2 * ff] = tn(two, up_ref[...]).astype(BF)
-    out_ref[:, 2 * ff : 3 * ff] = tn(branch_ref[...], hid_ref[...]).astype(BF)
-    out_ref[:, 3 * ff : 3 * ff + mine] = tn(wide_ref[...], pre_ref[...]).astype(BF)
-    out_ref[:, 3 * ff + mine :] = tn(other_ref[...], ho_ref[...]).astype(BF)
-
-
-def weight_grads(wide, two, branch, other, pre, gate, up, hid, ho):
+    out_ref[:, 2 * ff :] = tn(branch_ref[...], hid_ref[...]).astype(BF)
+
+
+def mixer_grad_kernel(wide_ref, other_ref, pre_ref, ho_ref, held_ref, out_ref):
+    mine = pre_ref.shape[1]
+    out_ref[:, :mine] = tn(wide_ref[...], pre_ref[...]).astype(BF)
+    out_ref[:, mine:] = tn(other_ref[...], ho_ref[...]).astype(BF)
+
+
+def feed_grads(two, branch, gate, up, hid, extra):
+    rows, width = two.shape
+    step = 256
+    left = pl.BlockSpec((rows, step), lambda i: (0, i))
+    cols = 3 * gate.shape[1]
+
+    def whole(x):
+        return pl.BlockSpec(x.shape, lambda i: (0, 0))
+
+    return pl.pallas_call(
+        feed_grad_kernel,
+        grid=(width // step,),
+        in_specs=[left, left, whole(gate), whole(up), whole(hid)],
+        out_specs=pl.BlockSpec((step, cols), lambda i: (i, 0)),
+        out_shape=jax.ShapeDtypeStruct((width, cols + extra), BF),
+        compiler_params=pltpu.CompilerParams(vmem_limit_bytes=32 * 2**20),
+        cost_estimate=pl.CostEstimate(flops=2 * rows * width * cols, bytes_accessed=10 * 10**6, transcendentals=0),
+    )(two, branch, gate, up, hid)
+
+
+def mixer_grads(wide, other, pre, ho, held):
     rows, width = wide.shape
     step = 256
     left = pl.BlockSpec((rows, step), lambda i: (0, i))
+    cols = 2 * pre.shape[1]
+    at = held.shape[1] // cols - 1
 
     def whole(x):
         return pl.BlockSpec(x.shape, lambda i: (0, 0))
 
-    cols = 3 * gate.shape[1] + 2 * pre.shape[1]
     return pl.pallas_call(
-        weight_grad_kernel,
+        mixer_grad_kernel,
         grid=(width // step,),
-        in_specs=[left] * 4 + [whole(x) for x in (pre, gate, up, hid, ho)],
-        out_specs=pl.BlockSpec((step, cols), lambda i: (i, 0)),
-        out_shape=jax.ShapeDtypeStruct((width, cols), BF),
+        in_specs=[left, left, whole(pre), whole(ho), pl.BlockSpec(memory_space=pl.ANY)],
+        out_specs=pl.BlockSpec((step, cols), lambda i: (i, at)),
+        out_shape=jax.ShapeDtypeStruct(held.shape, BF),
+        input_output_aliases={4: 0},
         compiler_params=pltpu.CompilerParams(vmem_limit_bytes=32 * 2**20),
-        cost_estimate=pl.CostEstimate(flops=2 * rows * width * cols, bytes_accessed=12 * 10**6, transcendentals=0),
-    )(wide, two, branch, other, pre, gate, up, hid, ho)
+        cost_estimate=pl.CostEstimate(flops=2 * rows * width * cols, bytes_accessed=4 * 10**6, transcendentals=0),
+    )(wide, other, pre, ho, held)
 
 
 def gather_small(x):
@@ -688,7 +712,11 @@
     lead = HD - heads
 
     gains_here = jnp.concatenate([mixer_gain, mlp_gain], axis=0)
-    gains_group = lax.all_gather(gains_here, "tensor", axis=1, tiled=True)
+    found = [gains_here] + [swap(gains_here, bit) for bit in (1, 2, 3)]
+    for bit in (1, 2):
+        flip = (lax.axis_index("tensor") & bit) > 0
+        found = [jnp.where(flip, found[i ^ bit], found[i]) for i in range(4)]
+    gains_group = jnp.concatenate(found, axis=1)
     span = 2 * mine + 6 * heads
     sds = jax.ShapeDtypeStruct
     rest_cols = 3 * ff + 2 * mine
@@ -795,7 +823,8 @@
         swish = gate * q
         d_gate = (d_hidden * up * (q + swish * (1.0 - q))).astype(BF)
         d_up = (d_hidden * swish).astype(BF)
-        d_norm = narrow(dot_t(d_gate, piece(l, 0)) + dot_t(d_up, piece(l, 1)))
+        held = feed_grads(wide_two, branch, d_gate, d_up, hidden, 2 * mine)
+        d_norm, held = narrow(dot_t(d_gate, piece(l, 0)) + dot_t(d_up, piece(l, 1)), held)
         back, gain_grads[layers + l] = rms_back(res_two, scale_two, gain_two, d_norm)
         grad = grad + back
         branch_two = widen(grad.astype(BF))
@@ -808,8 +837,8 @@
         d_ps = jnp.sum(d_post, axis=0)
         p = d_post * pg
         sums = order_sum(jnp.stack([jnp.sum(p, axis=1), jnp.sum(p * unit, axis=1)])) / D
+        rest_sum = mixer_grads(wide, branch_two, d_pre, heads_out, held)
         d_inner = inv * (p - sums[0][:, None] - unit * sums[1][:, None])
-        rest_sum = weight_grads(wide, wide_two, branch, branch_two, d_pre, d_gate, d_up, hidden, heads_out)
         rest_sum, d_inner = lax.optimization_barrier((rest_sum, d_inner))
         rest_grads[l] = scatter(rest_sum)
         if l == layers - 1:
@@ -820,18 +849,20 @@
             d_pack, moved = lax.optimization_barrier((d_pack, moved))
             residual = residual + near + moved.astype(F32)
         mats = t_dot(wide, d_pack)
+        if l == 0:
+            d_wide = dot_t(d_pack, mix_w[l]) + dot_t(d_pre, piece(l, 3))
+            gain_grads[l] = jnp.sum(d_wide * wide_unit, axis=0)
+            mats = mats + jnp.pad(jnp.stack(gain_grads).T, ((0, 0), (heads, PACK - heads - 2 * layers)))
         mixed = jnp.concatenate([mats.reshape(dp, part, PACK), block.reshape(dp, inner_part, PACK)], axis=1).astype(BF)
-        mixed, d_pack = lax.optimization_barrier((mixed, d_pack))
+        if l == 0:
+            mixed, d_pack = lax.optimization_barrier((mixed, d_pack))
+            d_norm = narrow(d_wide)
+        else:
+            d_norm, mixed = narrow(dot_t(d_pack, mix_w[l]) + dot_t(d_pre, piece(l, 3)), mixed)
         mix_grads[l] = exchange_sum(mixed)
-        d_wide = dot_t(d_pack, mix_w[l]) + dot_t(d_pre, piece(l, 3))
-        near, far = narrow_start(d_wide)
-        if l == 0:
-            first_gain = jnp.sum(d_wide * wide_unit, axis=0)
-            far, first_gain = lax.optimization_barrier((far, first_gain))
-        d_norm = near + swap(far, 2).astype(F32)
-        back, gain_grads[l] = rms_back(res_one, scale_one, gain_one, d_norm)
-        if l == 0:
-            gain_grads[l] = first_gain
+        back, gain = rms_back(res_one, scale_one, gain_one, d_norm)
+        if l > 0:
+            gain_grads[l] = gain
         grad = grad + back
         if l > 0:
             grad, rest_grads[l], residual = lax.optimization_barrier((grad, rest_grads[l], residual))
@@ -841,9 +872,8 @@
     both = jnp.stack(mix_grads)
     mats, block = both[:, :part], both[:, part:]
     rest = jnp.stack(rest_grads)
-    d_gains = sum_all(jnp.stack(gain_grads))
-    spot = lax.axis_index(DP) * tp + lax.axis_index("tensor")
-    d_gains = lax.dynamic_slice_in_dim(d_gains, spot * gain_part, gain_part, axis=1)
+    d_gains = sum_group(mix_grads[0][:part, heads : heads + 2 * layers].T)
+    d_gains = lax.dynamic_slice_in_dim(d_gains, lax.axis_index("tensor") * gain_part, gain_part, axis=1)
     small = block[:, :small_part, 2 * mine + heads : span].transpose(0, 2, 1).reshape(layers, 5, heads, small_part)
 
     def matrix(i):

time: 635 us -> 614 us (0.967); the launches traced: 623 us -> 609 us
  waiting for transfers between devices: 165 us -> 157 us
    ppermute x5 -> x0, waiting for transfers between devices: 20.1 us -> none  [sum_all(): x = x + lax.ppermute(x, axis, [(i, i ^ bit) for i in range(size)])]
    all_to_all x2, waiting for transfers between devices: 0.01 us -> 18.7 us  [exchange_sum(): moved = lax.all_to_all(x, DP, split_axis=0, concat_axis=0, tiled=True)]
    ppermute x56 -> x62, starting transfers between devices: 30.8 us -> 40.4 us  [swap(): return lax.ppermute(x, 'tensor', [(i, i ^ bit) for i in range(size)])]
    ppermute x5 -> x0, starting transfers between devices: 7.51 us -> none  [sum_all(): x = x + lax.ppermute(x, axis, [(i, i ^ bit) for i in range(size)])]
    ppermute x56 -> x62, waiting for transfers between devices: 131 us -> 124 us  [swap(): return lax.ppermute(x, 'tensor', [(i, i ^ bit) for i in range(size)])]
    pallas_call x2 -> x4, Pallas kernels: 11 us -> 14.1 us  [the longest x2 8.52 us: feed_grads(): pl.pallas_call(feed_grad_kernel, grid=(width // step,), in_specs=[left, l...]
  transfers between devices with their start and end apart: 71 -> 72, of which waited for: 37 -> 33; matrix products, arithmetic and copies ran while one was open for 13% -> 13% of each run, Pallas kernels for 33% -> 34%
where the time goes in v4:
time: 614 us; the launch traced here: 609 us
  Pallas kernels  207 us (34%)
  waiting for transfers between devices  157 us (26%)
  matrix products  67.4 us (11%)
  starting transfers between devices  57 us (9%)
  other arithmetic  51.3 us (8%)
  blocking collectives  35.4 us (6%)
  local copies, waits for them, and re-layouts  19.2 us (3%)
  between operations  15.5 us (3%)
    ppermute x62, waiting for transfers between devices, swap(): return lax.ppermute(x, 'tensor', [(i, i ^ bit) for i in range(size)])  124 us
    pallas_call x2, Pallas kernels, backward_call(): pl.pallas_call(functools.partial(backward_kernel, heads, dp), grid_spec=p...  105 us
    pallas_call x2, Pallas kernels, forward_call(): pl.pallas_call(functools.partial(forward_kernel, heads, dp), grid_spec=pl...  85.3 us
    ppermute x62, starting transfers between devices, swap(): return lax.ppermute(x, 'tensor', [(i, i ^ bit) for i in range(size)])  40.4 us
    dot_general x12, matrix products, dot(): lax.dot_general(a, b, (((1,), (0,)), ((), ())), preferred_element_type=F32)  36 us
    all_gather x1, blocking collectives, gather(): return lax.all_gather(x, DP, axis=0, tiled=True)  35.4 us
    dot_general x12, matrix products, dot_t(): lax.dot_general(a, b, (((1,), (1,)), ((), ())), preferred_element_type=F32)  26.1 us
    all_to_all x2, waiting for transfers between devices, exchange_sum(): moved = lax.all_to_all(x, DP, split_axis=0, concat_axis=0, tiled=True)  18.7 us
  transfers between devices with their start and end apart: 72, of which 33 were waited for; matrix products, arithmetic and copies ran while one was open for 13% of the time, Pallas kernels for 34%

profile of v4, /device:TPU:0, one launch (start us, length us, event | category | flops | bytes accessed | tf_op | source)
XLA Modules:
  0.0 609.5 jit_solution(2270846678953307718)
XLA Ops:
  29.7 3.9 collective-permute-start.7
  36.4 8.0 %collective-permute-done.8 = bf16[64,816]{1,0:T(8,128)(2,1)S(1)} collective-permute-done((bf16[64,816]{1,0:T(8,128)(2,1)S(1)}, bf16[64,816]{1,0:T(8,128)(2,1)S(1)}, u32[]{:S(2)}, u32[]{:S(2)}) %collective-permute-start.8) | collective-permute-done | bytes 104480 | tf_op jit(solution)/shard_map/ppermute | solution.py:683
  47.2 35.4 %all_gather.10 = bf16[768,640]{1,0:T(8,128)(2,1)S(1)} all-gather(bf16[96,640]{1,0:T(8,128)(2,1)S(1)} %copy-done.50), channel_id=1, replica_groups=mesh['line'=4,'near'=2,'tensor'=4] {'line','near'}, dimensions={0}, use_global_device_ids=true | all-gather | bytes 1105920 | tf_op jit(solution)/shard_map/all_gather | solution.py:587
  85.9 42.4 %shard_map.365 = (f32[1024,192]{1,0:T(8,128)}, bf16[1024,768]{1,0:T(8,128)(2,1)}, bf16[1024,768]{1,0:T(8,128)(2,1)}, bf16[1024,768]{1,0:T(8,128)(2,1)}, bf16[3,1...) custom-call(s32[1]{0:T(128)} %bitcast.5.place_ref, ...), custom_call_target="tpu_custom_call" | custom-call | flops 65000001536 | bytes 25000000 | tf_op jit(solution)/shard_map/pallas_call | solution.py:216
  143.6 9.7 %collective-permute-done.16 = bf16[256,768]{1,0:T(8,128)(2,1)} collective-permute-done((bf16[256,768]{1,0:T(8,128)(2,1)S(1)}, bf16[256,768]{1,0:T(8,128)(2,1)}, u32[]{:S(2)}, u32[]{:S(2)}) %collective-permute-start.16) | collective-permute-done | bytes 393248 | tf_op jit(solution)/shard_map/ppermute | solution.py:535
  157.2 8.9 %collective-permute-done.18 = bf16[256,768]{1,0:T(8,128)(2,1)S(1)} collective-permute-done((bf16[256,768]{1,0:T(8,128)(2,1)S(1)}, bf16[256,768]{1,0:T(8,128)(2,1)S(1)}, u32[]{:S(2)}, u32[]{:S(2)}) %collective-permute-start.18) | collective-permute-done | bytes 393248 | tf_op jit(solution)/shard_map/ppermute | solution.py:535
  176.0 9.8 %collective-permute-done.22 = bf16[256,768]{1,0:T(8,128)(2,1)} collective-permute-done((bf16[256,768]{1,0:T(8,128)(2,1)S(1)}, bf16[256,768]{1,0:T(8,128)(2,1)}, u32[]{:S(2)}, u32[]{:S(2)}) %collective-permute-start.22) | collective-permute-done | bytes 393248 | tf_op jit(solution)/shard_map/ppermute | solution.py:535
  190.2 8.9 %collective-permute-done.24 = bf16[256,768]{1,0:T(8,128)(2,1)S(1)} collective-permute-done((bf16[256,768]{1,0:T(8,128)(2,1)S(1)}, bf16[256,768]{1,0:T(8,128)(2,1)S(1)}, u32[]{:S(2)}, u32[]{:S(2)}) %collective-permute-start.24) | collective-permute-done | bytes 393248 | tf_op jit(solution)/shard_map/ppermute | solution.py:535
  200.9 3.9 convolution_convert_fusion.pack_ref
  204.8 42.9 %shard_map.366 = (f32[1024,192]{1,0:T(8,128)}, bf16[1024,768]{1,0:T(8,128)(2,1)}, bf16[1024,768]{1,0:T(8,128)(2,1)}, bf16[1024,768]{1,0:T(8,128)(2,1)}, bf16[3,1...) custom-call(s32[1]{0:T(128)} %bitcast.5.place_ref, ...), custom_call_target="tpu_custom_call" | custom-call | flops 65000001536 | bytes 25000000 | tf_op jit(solution)/shard_map/pallas_call | solution.py:216
  256.8 3.5 fusion.32
  267.6 9.9 %collective-permute-done.30 = bf16[256,768]{1,0:T(8,128)(2,1)} collective-permute-done((bf16[256,768]{1,0:T(8,128)(2,1)}, bf16[256,768]{1,0:T(8,128)(2,1)}, u32[]{:S(2)}, u32[]{:S(2)}) %collective-permute-start.30) | collective-permute-done | bytes 393248 | tf_op jit(solution)/shard_map/ppermute | solution.py:535
  283.5 6.2 %collective-permute-done.33 = bf16[256,768]{1,0:T(8,128)(2,1)S(1)} collective-permute-done((bf16[256,768]{1,0:T(8,128)(2,1)S(1)}, bf16[256,768]{1,0:T(8,128)(2,1)S(1)}, u32[]{:S(2)}, u32[]{:S(2)}) %collective-permute-start.33) | collective-permute-done | bytes 393248 | tf_op jit(solution)/shard_map/ppermute | solution.py:535
  292.4 3.4 multiply_convert_fusion.2
  301.3 4.3 shard_map.367.held_ref
  306.7 4.3 collective-permute-done.37
  314.8 8.1 %collective-permute-done.41 = bf16[256,768]{1,0:T(8,128)(2,1)S(1)} collective-permute-done((bf16[256,768]{1,0:T(8,128)(2,1)S(1)}, bf16[256,768]{1,0:T(8,128)(2,1)S(1)}, u32[]{:S(2)}, u32[]{:S(2)}) %collective-permute-start.41) | collective-permute-done | bytes 393248 | tf_op jit(solution)/shard_map/ppermute | solution.py:535
  325.2 4.7 multiply_reduce_fusion.2
  341.6 52.8 %shard_map.369 = (bf16[1024,640]{1,0:T(8,128)(2,1)}, f32[256,640]{1,0:T(8,128)}) custom-call(s32[1]{0:T(128)} %bitcast.5.place_ref, bf16[1024,640]{1,0:T(8,128)(2,1)} %convolution_convert_fusion.pack_ref, f32[1024,192]{1,0:T(8,128)} %subtract_multiply_fusion.1.do_ref, bf16[1024,768]{1,0:T(8,128)(2,1)} %get-tuple-element.96.z1_ref, ...), custom_call_target="tpu_custom_call" | custom-call | flops 70000001024 | bytes 25000000 | tf_op jit(solution)/shard_map/pallas_call | solution.py:479
  405.6 7.7 %collective-permute-done.48 = bf16[256,768]{1,0:T(8,128)(2,1)S(1)} collective-permute-done((bf16[256,768]{1,0:T(8,128)(2,1)S(1)}, bf16[256,768]{1,0:T(8,128)(2,1)S(1)}, u32[]{:S(2)}, u32[]{:S(2)}) %collective-permute-start.48) | collective-permute-done | bytes 393248 | tf_op jit(solution)/shard_map/ppermute | solution.py:535
  417.3 9.0 %collective-permute-done.50 = bf16[256,768]{1,0:T(8,128)(2,1)S(1)} collective-permute-done((bf16[256,768]{1,0:T(8,128)(2,1)S(1)}, bf16[256,768]{1,0:T(8,128)(2,1)S(1)}, u32[]{:S(2)}, u32[]{:S(2)}) %collective-permute-start.50) | collective-permute-done | bytes 393248 | tf_op jit(solution)/shard_map/ppermute | solution.py:535
  428.0 5.1 multiply_convert_fusion
  441.0 4.2 shard_map.370.held_ref
  445.2 5.4 collective-permute-done.54
  453.5 9.1 %collective-permute-done.56 = bf16[256,768]{1,0:T(8,128)(2,1)S(1)} collective-permute-done((bf16[256,768]{1,0:T(8,128)(2,1)S(1)}, bf16[256,768]{1,0:T(8,128)(2,1)S(1)}, u32[]{:S(2)}, u32[]{:S(2)}) %collective-permute-start.56) | collective-permute-done | bytes 393248 | tf_op jit(solution)/shard_map/ppermute | solution.py:535
  463.1 4.3 all-to-all-start.1
  467.5 4.3 multiply_reduce_fusion
  481.2 52.5 %shard_map.372 = (bf16[1024,640]{1,0:T(8,128)(2,1)}, f32[256,640]{1,0:T(8,128)}) custom-call(s32[1]{0:T(128)} %bitcast.5.place_ref, bf16[1024,640]{1,0:T(8,128)(2,1)} %convolution_convert_fusion.1.pack_ref, f32[1024,192]{1,0:T(8,128)} %subtract_multiply_fusion.do_ref, bf16[1024,768]{1,0:T(8,128)(2,1)} %get-tuple-element.116.z1_ref, ...), custom_call_target="tpu_custom_call" | custom-call | flops 70000001024 | bytes 25000000 | tf_op jit(solution)/shard_map/pallas_call | solution.py:479
  536.7 5.7 fusion.3
  546.7 6.1 all-to-all-start
  558.2 8.9 %collective-permute-done.62 = bf16[256,768]{1,0:T(8,128)(2,1)S(1)} collective-permute-done((bf16[256,768]{1,0:T(8,128)(2,1)S(1)}, bf16[256,768]{1,0:T(8,128)(2,1)S(1)}, u32[]{:S(2)}, u32[]{:S(2)}) %collective-permute-start.62) | collective-permute-done | bytes 393248 | tf_op jit(solution)/shard_map/ppermute | solution.py:535
  570.9 18.7 %all-to-all-done = bf16[8,128,640]{2,1,0:T(8,128)(2,1)} async-done(((bf16[8,128,640]{2,1,0:T(8,128)(2,1)}), bf16[8,128,640]{2,1,0:T(8,128)(2,1)}, u32[]{:S(2)}, u32[]{:S(2)}) %all-to-all-start) | async-done | bytes 1310752 | tf_op jit(solution)/shard_map/all_to_all | solution.py:693
  (469 shorter events, 182.1 us)
Async XLA Ops:
  7.2 127.7 %all-gather.3.cloned.1.call-start = ((), (), s32[]{:S(2)}) async-start(), calls=%async_computation.4 | async-start | bytes 4423680 | tf_op jit(solution)/shard_map/all_gather | solution.py:587
  7.9 12.0 %collective-permute-start.3 = (bf16[4,24]{1,0:T(4,128)(2,1)S(1)}, bf16[4,24]{1,0:T(4,128)(2,1)S(1)}, u32[]{:S(2)}, u32[]{:S(2)}) collective-permute-start(bf16[4,24]{1,0:T(4,128)(2,1)S(1)} %pad_maximum_fusion.25), channel_id=1, source_target_pairs={{0,3},{1,2},{2,1},{3,0},{4,7},{5,6},{6,5},{7,4},{8,11},{9,10},{10,... | collective-permute-start | bytes 584 | tf_op jit(solution)/shard_map/ppermute | solution.py:535
  11.5 11.3 %collective-permute-start.1 = (bf16[256,768]{1,0:T(8,128)(2,1)}, bf16[256,768]{1,0:T(8,128)(2,1)S(1)}, u32[]{:S(2)}, u32[]{:S(2)}) collective-permute-start(bf16[256,768]{1,0:T(8,128)(2,1)} %param.21), channel_id=1, source_target_pairs={{0,2},{1,3},{2,0},{3,1},{4,6},{5,7},{6,4},{7,5},{8,10},{9,11},{10,... | collective-permute-start | bytes 1179656 | tf_op jit(solution)/shard_map/ppermute | solution.py:535
  33.6 94.7 %collective-permute-start.10 = (bf16[256,768]{1,0:T(8,128)(2,1)}, bf16[256,768]{1,0:T(8,128)(2,1)}, u32[]{:S(2)}, u32[]{:S(2)}) collective-permute-start(bf16[256,768]{1,0:T(8,128)(2,1)} %param.22), channel_id=1, source_target_pairs={{0,1},{1,0},{2,3},{3,2},{4,5},{5,4},{6,7},{7,6},{8,9},{9,8},{10,11... | collective-permute-start | bytes 1179656 | tf_op jit(solution)/shard_map/ppermute | solution.py:535
  33.6 94.7 %collective-permute-start.11 = (bf16[256,768]{1,0:T(8,128)(2,1)}, bf16[256,768]{1,0:T(8,128)(2,1)}, u32[]{:S(2)}, u32[]{:S(2)}) collective-permute-start(bf16[256,768]{1,0:T(8,128)(2,1)} %param.22), channel_id=1, source_target_pairs={{0,2},{1,3},{2,0},{3,1},{4,6},{5,7},{6,4},{7,5},{8,10},{9,11},{10,... | collective-permute-start | bytes 1179656 | tf_op jit(solution)/shard_map/ppermute | solution.py:535
  35.1 47.4 %collective-permute-start.2 = (bf16[256,768]{1,0:T(8,128)(2,1)S(1)}, bf16[256,768]{1,0:T(8,128)(2,1)S(1)}, u32[]{:S(2)}, u32[]{:S(2)}) collective-permute-start(bf16[256,768]{1,0:T(8,128)(2,1)S(1)} %collective-permute-done.1), channel_id=1, source_target_pairs={{0,1},{1,0},{2,3},{3,2},{4,5},{5,4},{6,7},{7,6},{8,9},{9,8},{10,11... | collective-permute-start | bytes 1179656 | tf_op jit(solution)/shard_map/ppermute | solution.py:535
  46.3 210.4 %all-gather.5.cloned.1.call-start = ((), (), s32[]{:S(2)}) async-start(), calls=%async_computation.5 | async-start | bytes 3317760 | tf_op jit(solution)/shard_map/all_gather | solution.py:587
  142.1 11.3 %collective-permute-start.16 = (bf16[256,768]{1,0:T(8,128)(2,1)S(1)}, bf16[256,768]{1,0:T(8,128)(2,1)}, u32[]{:S(2)}, u32[]{:S(2)}) collective-permute-start(bf16[256,768]{1,0:T(8,128)(2,1)S(1)} %fusion.64), channel_id=1, source_target_pairs={{0,2},{1,3},{2,0},{3,1},{4,6},{5,7},{6,4},{7,5},{8,10},{9,11},{10,... | collective-permute-start | bytes 1179656 | tf_op jit(solution)/shard_map/ppermute | solution.py:535
  155.7 10.4 %collective-permute-start.18 = (bf16[256,768]{1,0:T(8,128)(2,1)S(1)}, bf16[256,768]{1,0:T(8,128)(2,1)S(1)}, u32[]{:S(2)}, u32[]{:S(2)}) collective-permute-start(bf16[256,768]{1,0:T(8,128)(2,1)S(1)} %multiply_convert_fusion.8), channel_id=1, source_target_pairs={{0,2},{1,3},{2,0},{3,1},{4,6},{5,7},{6,4},{7,5},{8,10},{9,11},{10,... | collective-permute-start | bytes 1179656 | tf_op jit(solution)/shard_map/ppermute | solution.py:535
  174.4 11.3 %collective-permute-start.22 = (bf16[256,768]{1,0:T(8,128)(2,1)S(1)}, bf16[256,768]{1,0:T(8,128)(2,1)}, u32[]{:S(2)}, u32[]{:S(2)}) collective-permute-start(bf16[256,768]{1,0:T(8,128)(2,1)S(1)} %fusion.61), channel_id=1, source_target_pairs={{0,2},{1,3},{2,0},{3,1},{4,6},{5,7},{6,4},{7,5},{8,10},{9,11},{10,... | collective-permute-start | bytes 1179656 | tf_op jit(solution)/shard_map/ppermute | solution.py:535
  188.7 10.4 %collective-permute-start.24 = (bf16[256,768]{1,0:T(8,128)(2,1)S(1)}, bf16[256,768]{1,0:T(8,128)(2,1)S(1)}, u32[]{:S(2)}, u32[]{:S(2)}) collective-permute-start(bf16[256,768]{1,0:T(8,128)(2,1)S(1)} %multiply_convert_fusion.7), channel_id=1, source_target_pairs={{0,2},{1,3},{2,0},{3,1},{4,6},{5,7},{6,4},{7,5},{8,10},{9,11},{10,... | collective-permute-start | bytes 1179656 | tf_op jit(solution)/shard_map/ppermute | solution.py:535
  190.2 10.7 %collective-permute-start.23 = (bf16[256,768]{1,0:T(8,128)(2,1)S(1)}, bf16[256,768]{1,0:T(8,128)(2,1)}, u32[]{:S(2)}, u32[]{:S(2)}) collective-permute-start(bf16[256,768]{1,0:T(8,128)(2,1)S(1)} %multiply_convert_fusion.7), channel_id=1, source_target_pairs={{0,1},{1,0},{2,3},{3,2},{4,5},{5,4},{6,7},{7,6},{8,9},{9,8},{10,11... | collective-permute-start | bytes 1179656 | tf_op jit(solution)/shard_map/ppermute | solution.py:535
  199.1 215.0 %reduce-scatter.3.cloned.1.call-start = ((), (), s32[]{:S(2)}) async-start(), calls=%async_computation.6 | async-start | bytes 3317760 | tf_op jit(solution)/shard_map/reduce_scatter | solution.py:689
  266.0 11.5 %collective-permute-start.30 = (bf16[256,768]{1,0:T(8,128)(2,1)}, bf16[256,768]{1,0:T(8,128)(2,1)}, u32[]{:S(2)}, u32[]{:S(2)}) collective-permute-start(bf16[256,768]{1,0:T(8,128)(2,1)} %fusion.58), channel_id=1, source_target_pairs={{0,2},{1,3},{2,0},{3,1},{4,6},{5,7},{6,4},{7,5},{8,10},{9,11},{10,... | collective-permute-start | bytes 1179656 | tf_op jit(solution)/shard_map/ppermute | solution.py:535
  279.3 10.4 %collective-permute-start.33 = (bf16[256,768]{1,0:T(8,128)(2,1)S(1)}, bf16[256,768]{1,0:T(8,128)(2,1)S(1)}, u32[]{:S(2)}, u32[]{:S(2)}) collective-permute-start(bf16[256,768]{1,0:T(8,128)(2,1)S(1)} %multiply_convert_fusion.6), channel_id=1, source_target_pairs={{0,2},{1,3},{2,0},{3,1},{4,6},{5,7},{6,4},{7,5},{8,10},{9,11},{10,... | collective-permute-start | bytes 1179656 | tf_op jit(solution)/shard_map/ppermute | solution.py:535
  298.1 12.9 %collective-permute-start.35 = (bf16[256,768]{1,0:T(8,128)(2,1)S(1)}, bf16[256,768]{1,0:T(8,128)(2,1)S(1)}, u32[]{:S(2)}, u32[]{:S(2)}) collective-permute-start(bf16[256,768]{1,0:T(8,128)(2,1)S(1)} %get-tuple-element.272), channel_id=1, source_target_pairs={{0,1},{1,0},{2,3},{3,2},{4,5},{5,4},{6,7},{7,6},{8,9},{9,8},{10,11... | collective-permute-start | bytes 1179656 | tf_op jit(solution)/shard_map/ppermute | solution.py:535
  299.8 11.2 %collective-permute-start.37 = (bf16[256,768]{1,0:T(8,128)(2,1)S(1)}, bf16[256,768]{1,0:T(8,128)(2,1)S(1)}, u32[]{:S(2)}, u32[]{:S(2)}) collective-permute-start(bf16[256,768]{1,0:T(8,128)(2,1)S(1)} %fusion.56), channel_id=1, source_target_pairs={{0,2},{1,3},{2,0},{3,1},{4,6},{5,7},{6,4},{7,5},{8,10},{9,11},{10,... | collective-permute-start | bytes 1179656 | tf_op jit(solution)/shard_map/ppermute | solution.py:535
  312.6 10.3 %collective-permute-start.41 = (bf16[256,768]{1,0:T(8,128)(2,1)S(1)}, bf16[256,768]{1,0:T(8,128)(2,1)S(1)}, u32[]{:S(2)}, u32[]{:S(2)}) collective-permute-start(bf16[256,768]{1,0:T(8,128)(2,1)S(1)} %get-tuple-element.241), channel_id=1, source_target_pairs={{0,2},{1,3},{2,0},{3,1},{4,6},{5,7},{6,4},{7,5},{8,10},{9,11},{10,... | collective-permute-start | bytes 1179656 | tf_op jit(solution)/shard_map/ppermute | solution.py:535
  314.1 10.0 %collective-permute-start.38 = (bf16[256,768]{1,0:T(8,128)(2,1)S(1)}, bf16[256,768]{1,0:T(8,128)(2,1)S(1)}, u32[]{:S(2)}, u32[]{:S(2)}) collective-permute-start(bf16[256,768]{1,0:T(8,128)(2,1)S(1)} %get-tuple-element.271), channel_id=1, source_target_pairs={{0,1},{1,0},{2,3},{3,2},{4,5},{5,4},{6,7},{7,6},{8,9},{9,8},{10,11... | collective-permute-start | bytes 1179656 | tf_op jit(solution)/shard_map/ppermute | solution.py:535
  314.7 10.5 %collective-permute-start.40 = (bf16[256,768]{1,0:T(8,128)(2,1)S(1)}, bf16[256,768]{1,0:T(8,128)(2,1)S(1)}, u32[]{:S(2)}, u32[]{:S(2)}) collective-permute-start(bf16[256,768]{1,0:T(8,128)(2,1)S(1)} %get-tuple-element.241), channel_id=1, source_target_pairs={{0,1},{1,0},{2,3},{3,2},{4,5},{5,4},{6,7},{7,6},{8,9},{9,8},{10,11... | collective-permute-start | bytes 1179656 | tf_op jit(solution)/shard_map/ppermute | solution.py:535
  340.6 54.9 %collective-permute-start.45 = (bf16[256,768]{1,0:T(8,128)(2,1)S(1)}, bf16[256,768]{1,0:T(8,128)(2,1)S(1)}, u32[]{:S(2)}, u32[]{:S(2)}) collective-permute-start(bf16[256,768]{1,0:T(8,128)(2,1)S(1)} %get-tuple-element.104), channel_id=1, source_target_pairs={{0,2},{1,3},{2,0},{3,1},{4,6},{5,7},{6,4},{7,5},{8,10},{9,11},{10,... | collective-permute-start | bytes 1179656 | tf_op jit(solution)/shard_map/ppermute | solution.py:535
  399.0 14.4 %collective-permute-start.46 = (bf16[256,768]{1,0:T(8,128)(2,1)S(1)}, bf16[256,768]{1,0:T(8,128)(2,1)S(1)}, u32[]{:S(2)}, u32[]{:S(2)}) collective-permute-start(bf16[256,768]{1,0:T(8,128)(2,1)S(1)} %get-tuple-element.268), channel_id=1, source_target_pairs={{0,1},{1,0},{2,3},{3,2},{4,5},{5,4},{6,7},{7,6},{8,9},{9,8},{10,11... | collective-permute-start | bytes 1179656 | tf_op jit(solution)/shard_map/ppermute | solution.py:535
  402.2 11.2 %collective-permute-start.48 = (bf16[256,768]{1,0:T(8,128)(2,1)S(1)}, bf16[256,768]{1,0:T(8,128)(2,1)S(1)}, u32[]{:S(2)}, u32[]{:S(2)}) collective-permute-start(bf16[256,768]{1,0:T(8,128)(2,1)S(1)} %fusion.53), channel_id=1, source_target_pairs={{0,2},{1,3},{2,0},{3,1},{4,6},{5,7},{6,4},{7,5},{8,10},{9,11},{10,... | collective-permute-start | bytes 1179656 | tf_op jit(solution)/shard_map/ppermute | solution.py:535
  416.0 10.3 %collective-permute-start.50 = (bf16[256,768]{1,0:T(8,128)(2,1)S(1)}, bf16[256,768]{1,0:T(8,128)(2,1)S(1)}, u32[]{:S(2)}, u32[]{:S(2)}) collective-permute-start(bf16[256,768]{1,0:T(8,128)(2,1)S(1)} %convert_element_type.253), channel_id=1, source_target_pairs={{0,2},{1,3},{2,0},{3,1},{4,6},{5,7},{6,4},{7,5},{8,10},{9,11},{10,... | collective-permute-start | bytes 1179656 | tf_op jit(solution)/shard_map/ppermute | solution.py:535
  437.7 12.9 %collective-permute-start.52 = (bf16[256,768]{1,0:T(8,128)(2,1)S(1)}, bf16[256,768]{1,0:T(8,128)(2,1)S(1)}, u32[]{:S(2)}, u32[]{:S(2)}) collective-permute-start(bf16[256,768]{1,0:T(8,128)(2,1)S(1)} %get-tuple-element.266), channel_id=1, source_target_pairs={{0,1},{1,0},{2,3},{3,2},{4,5},{5,4},{6,7},{7,6},{8,9},{9,8},{10,11... | collective-permute-start | bytes 1179656 | tf_op jit(solution)/shard_map/ppermute | solution.py:535
  439.4 11.2 %collective-permute-start.54 = (bf16[256,768]{1,0:T(8,128)(2,1)S(1)}, bf16[256,768]{1,0:T(8,128)(2,1)S(1)}, u32[]{:S(2)}, u32[]{:S(2)}) collective-permute-start(bf16[256,768]{1,0:T(8,128)(2,1)S(1)} %fusion.51), channel_id=1, source_target_pairs={{0,2},{1,3},{2,0},{3,1},{4,6},{5,7},{6,4},{7,5},{8,10},{9,11},{10,... | collective-permute-start | bytes 1179656 | tf_op jit(solution)/shard_map/ppermute | solution.py:535
  452.2 10.3 %collective-permute-start.56 = (bf16[256,768]{1,0:T(8,128)(2,1)S(1)}, bf16[256,768]{1,0:T(8,128)(2,1)S(1)}, u32[]{:S(2)}, u32[]{:S(2)}) collective-permute-start(bf16[256,768]{1,0:T(8,128)(2,1)S(1)} %get-tuple-element.238), channel_id=1, source_target_pairs={{0,2},{1,3},{2,0},{3,1},{4,6},{5,7},{6,4},{7,5},{8,10},{9,11},{10,... | collective-permute-start | bytes 1179656 | tf_op jit(solution)/shard_map/ppermute | solution.py:535
  453.5 14.0 %collective-permute-start.55 = (bf16[256,768]{1,0:T(8,128)(2,1)S(1)}, bf16[256,768]{1,0:T(8,128)(2,1)}, u32[]{:S(2)}, u32[]{:S(2)}) collective-permute-start(bf16[256,768]{1,0:T(8,128)(2,1)S(1)} %get-tuple-element.238), channel_id=1, source_target_pairs={{0,1},{1,0},{2,3},{3,2},{4,5},{5,4},{6,7},{7,6},{8,9},{9,8},{10,11... | collective-permute-start | bytes 1179656 | tf_op jit(solution)/shard_map/ppermute | solution.py:535
  463.1 83.6 %all-to-all-start.1 = ((bf16[8,128,640]{2,1,0:T(8,128)(2,1)}), bf16[8,128,640]{2,1,0:T(8,128)(2,1)}, u32[]{:S(2)}, u32[]{:S(2)}) async-start(bf16[8,128,640]{2,1,0:T(8,128)(2,1)} %pad_maximum_fusion.7), calls=%async_computation.2 | async-start | bytes 2621440 | tf_op jit(solution)/shard_map/all_to_all | solution.py:693
  467.4 131.8 %reduce-scatter.5.cloned.1.call-start = ((), (), s32[]{:S(2)}) async-start(), calls=%async_computation.7 | async-start | bytes 3317760 | tf_op jit(solution)/shard_map/reduce_scatter | solution.py:689
  546.7 43.0 %all-to-all-start = ((bf16[8,128,640]{2,1,0:T(8,128)(2,1)}), bf16[8,128,640]{2,1,0:T(8,128)(2,1)}, u32[]{:S(2)}, u32[]{:S(2)}) async-start(bf16[8,128,640]{2,1,0:T(8,128)(2,1)} %pad_maximum_fusion.8), calls=%async_computation.1 | async-start | bytes 2621440 | tf_op jit(solution)/shard_map/all_to_all | solution.py:693
  555.9 11.2 %collective-permute-start.62 = (bf16[256,768]{1,0:T(8,128)(2,1)S(1)}, bf16[256,768]{1,0:T(8,128)(2,1)S(1)}, u32[]{:S(2)}, u32[]{:S(2)}) collective-permute-start(bf16[256,768]{1,0:T(8,128)(2,1)S(1)} %fusion.48), channel_id=1, source_target_pairs={{0,2},{1,3},{2,0},{3,1},{4,6},{5,7},{6,4},{7,5},{8,10},{9,11},{10,... | collective-permute-start | bytes 1179656 | tf_op jit(solution)/shard_map/ppermute | solution.py:535
  (116 other events, 1115.5 us)
Sparse Core Ops, SparseCore 0:
  46.4 78.4 all-gather.2
  199.2 57.5 all-gather.4
  341.8 70.5 reduce-scatter.2
  481.3 83.8 reduce-scatter.4

commit v5 on v4

--- a/solution.py
+++ b/solution.py
@@ -265,7 +265,7 @@
 
 def backward_kernel(
     heads, shares, place_ref, pack_ref, do_ref, z1_ref, a_ref, z1b_ref, c_ref, z2b_ref, w1s_ref, w2s_ref, small_ref, post_ref,
-    dpack_ref, block_ref, dw1, db1, dw2, db2, dg_ref, dh_ref,
+    dpack_ref, packed_ref, block_ref, dw1, db1, dw2, db2, dg_ref, dh_ref,
     dg1b, dg2b, dx2b, d1v, ad2, g2v, kkt, dz1buf, k1v, k2v, dyv, ecol, x2buf,
 ):
     H = range(heads)
@@ -452,6 +452,7 @@
             block_ref[step * d : step * d + few, 2 * mine + heads : 2 * mine + 6 * heads] = small[
                 few * d : few * (d + 1), : 5 * heads
             ]
+        packed_ref[...] = block_ref[...].astype(BF)
 
 
 def backward_call(place, pack, do, saved, small, post, dp):
@@ -496,6 +497,7 @@
             ],
             out_specs=[moved(PACK), whole(INNER, PACK)],
             scratch_shapes=[
+                pltpu.VMEM((INNER, PACK), F32),
                 pltpu.VMEM((heads, HD, INNER), F32),
                 pltpu.VMEM((heads, 1, INNER), F32),
                 pltpu.VMEM((heads, HD, INNER), F32),
@@ -519,7 +521,7 @@
         ),
         out_shape=[
             sds((rows, PACK), BF),
-            sds((INNER, PACK), F32),
+            sds((INNER, PACK), BF),
         ],
         compiler_params=pltpu.CompilerParams(vmem_limit_bytes=56 * 2**20),
         cost_estimate=pl.CostEstimate(flops=70 * 10**9, bytes_accessed=25 * 10**6, transcendentals=0),
@@ -787,13 +789,18 @@
         ps = small[4 * heads : 5 * heads].reshape(-1)
         gate_pre = dot(wide, piece(l, 3))
         sums = jnp.stack([jnp.sum(inner_out, axis=1), jnp.sum(inner_out * inner_out, axis=1)])
-        sums = order_sum(sums)
+        sums = order_sum(sums, True)
         mean_all = sums[0] / D
         inv = lax.rsqrt(sums[1] / D - mean_all * mean_all + EPS)[:, None]
         unit = (inner_out - mean_all[:, None]) * inv
         post = unit * pg + ps
         heads_out = (jax.nn.gelu(gate_pre, approximate=True) * post).astype(BF)
-        residual = residual + narrow(dot_t(heads_out, piece(l, 4)))
+        partial = dot_t(heads_out, piece(l, 4))
+        if l + 1 < layers:
+            branch, inner_in[l + 1] = narrow(partial, inner_in[l + 1])
+        else:
+            branch = narrow(partial)
+        residual = residual + branch
         res_two = residual
         normed, scale_two = rms(residual, gain_two)
         wide_two = widen(normed)
@@ -836,7 +843,7 @@
         d_pg = jnp.sum(d_post * unit, axis=0)
         d_ps = jnp.sum(d_post, axis=0)
         p = d_post * pg
-        sums = order_sum(jnp.stack([jnp.sum(p, axis=1), jnp.sum(p * unit, axis=1)])) / D
+        sums = order_sum(jnp.stack([jnp.sum(p, axis=1), jnp.sum(p * unit, axis=1)]), False) / D
         rest_sum = mixer_grads(wide, branch_two, d_pre, heads_out, held)
         d_inner = inv * (p - sums[0][:, None] - unit * sums[1][:, None])
         rest_sum, d_inner = lax.optimization_barrier((rest_sum, d_inner))
@@ -853,7 +860,7 @@
             d_wide = dot_t(d_pack, mix_w[l]) + dot_t(d_pre, piece(l, 3))
             gain_grads[l] = jnp.sum(d_wide * wide_unit, axis=0)
             mats = mats + jnp.pad(jnp.stack(gain_grads).T, ((0, 0), (heads, PACK - heads - 2 * layers)))
-        mixed = jnp.concatenate([mats.reshape(dp, part, PACK), block.reshape(dp, inner_part, PACK)], axis=1).astype(BF)
+        mixed = jnp.concatenate([mats.astype(BF).reshape(dp, part, PACK), block.reshape(dp, inner_part, PACK)], axis=1)
         if l == 0:
             mixed, d_pack = lax.optimization_barrier((mixed, d_pack))
             d_norm = narrow(d_wide)
@@ -910,11 +917,13 @@
     )
 
 
-def order_sum(sums):
+def order_sum(sums, at_once):
     def turn(x, bit):
         parts = jnp.split(x, 4, axis=1)
         return jnp.concatenate([parts[i ^ bit] for i in range(4)], axis=1)
 
+    if at_once:
+        return sums + turn(swap(sums, 1), 1) + turn(swap(sums, 2), 2) + turn(swap(sums, 3), 3)
     sums = sums + turn(swap(sums, 1), 1)
     return sums + turn(swap(sums, 2), 2)
 

time: 614 us -> 610 us (level)
    ppermute x62 -> x64, starting transfers between devices: 40.4 us -> 38.9 us  [swap(): return lax.ppermute(x, 'tensor', [(i, i ^ bit) for i in range(size)])]
    ppermute x62 -> x64, waiting for transfers between devices: 124 us -> 125 us  [swap(): return lax.ppermute(x, 'tensor', [(i, i ^ bit) for i in range(size)])]
  transfers between devices with their start and end apart: 72 -> 74, of which waited for: 33 -> 33; matrix products, arithmetic and copies ran while one was open for 13% -> 13% of each run, Pallas kernels for 34% -> 34%
where the time goes in v5:
time: 610 us; the launch traced here: 606 us
  Pallas kernels  207 us (34%)
  waiting for transfers between devices  158 us (26%)
  matrix products  67.4 us (11%)
  starting transfers between devices  55.4 us (9%)
  other arithmetic  49 us (8%)
  blocking collectives  35.4 us (6%)
  local copies, waits for them, and re-layouts  18 us (3%)
  between operations  15.5 us (3%)
    ppermute x64, waiting for transfers between devices, swap(): return lax.ppermute(x, 'tensor', [(i, i ^ bit) for i in range(size)])  125 us
    pallas_call x2, Pallas kernels, backward_call(): pl.pallas_call(functools.partial(backward_kernel, heads, dp), grid_spec=p...  105 us
    pallas_call x2, Pallas kernels, forward_call(): pl.pallas_call(functools.partial(forward_kernel, heads, dp), grid_spec=pl...  85.3 us
    ppermute x64, starting transfers between devices, swap(): return lax.ppermute(x, 'tensor', [(i, i ^ bit) for i in range(size)])  38.9 us
    dot_general x12, matrix products, dot(): lax.dot_general(a, b, (((1,), (0,)), ((), ())), preferred_element_type=F32)  36 us
    all_gather x1, blocking collectives, gather(): return lax.all_gather(x, DP, axis=0, tiled=True)  35.4 us
    dot_general x12, matrix products, dot_t(): lax.dot_general(a, b, (((1,), (1,)), ((), ())), preferred_element_type=F32)  26 us
    all_to_all x2, waiting for transfers between devices, exchange_sum(): moved = lax.all_to_all(x, DP, split_axis=0, concat_axis=0, tiled=True)  18.9 us
  transfers between devices with their start and end apart: 74, of which 33 were waited for; matrix products, arithmetic and copies ran while one was open for 13% of the time, Pallas kernels for 34%

profile of v5, /device:TPU:0, one launch (start us, length us, event | category | flops | bytes accessed | tf_op | source)
XLA Modules:
  0.0 605.9 jit_solution(17978741539841443303)
XLA Ops:
  29.7 3.9 collective-permute-start.7
  36.4 8.0 %collective-permute-done.8 = bf16[64,816]{1,0:T(8,128)(2,1)S(1)} collective-permute-done((bf16[64,816]{1,0:T(8,128)(2,1)S(1)}, bf16[64,816]{1,0:T(8,128)(2,1)S(1)}, u32[]{:S(2)}, u32[]{:S(2)}) %collective-permute-start.8) | collective-permute-done | bytes 104480 | tf_op jit(solution)/shard_map/ppermute | solution.py:685
  46.6 35.4 %all_gather.10 = bf16[768,640]{1,0:T(8,128)(2,1)S(1)} all-gather(bf16[96,640]{1,0:T(8,128)(2,1)S(1)} %copy-done.51), channel_id=1, replica_groups=mesh['line'=4,'near'=2,'tensor'=4] {'line','near'}, dimensions={0}, use_global_device_ids=true | all-gather | bytes 1105920 | tf_op jit(solution)/shard_map/all_gather | solution.py:589
  85.3 42.4 %shard_map.365 = (f32[1024,192]{1,0:T(8,128)}, bf16[1024,768]{1,0:T(8,128)(2,1)}, bf16[1024,768]{1,0:T(8,128)(2,1)}, bf16[1024,768]{1,0:T(8,128)(2,1)}, bf16[3,1...) custom-call(s32[1]{0:T(128)} %bitcast.5.place_ref, ...), custom_call_target="tpu_custom_call" | custom-call | flops 65000001536 | bytes 25000000 | tf_op jit(solution)/shard_map/pallas_call | solution.py:216
  142.7 9.0 %collective-permute-done.17 = bf16[256,768]{1,0:T(8,128)(2,1)S(1)} collective-permute-done((bf16[256,768]{1,0:T(8,128)(2,1)S(1)}, bf16[256,768]{1,0:T(8,128)(2,1)S(1)}, u32[]{:S(2)}, u32[]{:S(2)}) %collective-permute-start.17) | collective-permute-done | bytes 393248 | tf_op jit(solution)/shard_map/ppermute | solution.py:537
  155.3 9.3 %collective-permute-done.19 = bf16[256,768]{1,0:T(8,128)(2,1)S(1)} collective-permute-done((bf16[256,768]{1,0:T(8,128)(2,1)S(1)}, bf16[256,768]{1,0:T(8,128)(2,1)S(1)}, u32[]{:S(2)}, u32[]{:S(2)}) %collective-permute-start.19) | collective-permute-done | bytes 393248 | tf_op jit(solution)/shard_map/ppermute | solution.py:537
  174.1 10.1 %collective-permute-done.23 = bf16[256,768]{1,0:T(8,128)(2,1)} collective-permute-done((bf16[256,768]{1,0:T(8,128)(2,1)S(1)}, bf16[256,768]{1,0:T(8,128)(2,1)}, u32[]{:S(2)}, u32[]{:S(2)}) %collective-permute-start.23) | collective-permute-done | bytes 393248 | tf_op jit(solution)/shard_map/ppermute | solution.py:537
  187.6 9.3 %collective-permute-done.25 = bf16[256,768]{1,0:T(8,128)(2,1)S(1)} collective-permute-done((bf16[256,768]{1,0:T(8,128)(2,1)S(1)}, bf16[256,768]{1,0:T(8,128)(2,1)S(1)}, u32[]{:S(2)}, u32[]{:S(2)}) %collective-permute-start.25) | collective-permute-done | bytes 393248 | tf_op jit(solution)/shard_map/ppermute | solution.py:537
  198.7 3.9 convolution_convert_fusion.pack_ref
  202.7 42.9 %shard_map.366 = (f32[1024,192]{1,0:T(8,128)}, bf16[1024,768]{1,0:T(8,128)(2,1)}, bf16[1024,768]{1,0:T(8,128)(2,1)}, bf16[1024,768]{1,0:T(8,128)(2,1)}, bf16[3,1...) custom-call(s32[1]{0:T(128)} %bitcast.5.place_ref, ...), custom_call_target="tpu_custom_call" | custom-call | flops 65000001536 | bytes 25000000 | tf_op jit(solution)/shard_map/pallas_call | solution.py:216
  254.5 3.5 fusion.32
  265.2 9.9 %collective-permute-done.32 = bf16[256,768]{1,0:T(8,128)(2,1)} collective-permute-done((bf16[256,768]{1,0:T(8,128)(2,1)}, bf16[256,768]{1,0:T(8,128)(2,1)}, u32[]{:S(2)}, u32[]{:S(2)}) %collective-permute-start.32) | collective-permute-done | bytes 393248 | tf_op jit(solution)/shard_map/ppermute | solution.py:537
  281.1 6.2 %collective-permute-done.35 = bf16[256,768]{1,0:T(8,128)(2,1)S(1)} collective-permute-done((bf16[256,768]{1,0:T(8,128)(2,1)S(1)}, bf16[256,768]{1,0:T(8,128)(2,1)S(1)}, u32[]{:S(2)}, u32[]{:S(2)}) %collective-permute-start.35) | collective-permute-done | bytes 393248 | tf_op jit(solution)/shard_map/ppermute | solution.py:537
  290.0 3.4 multiply_convert_fusion.2
  299.0 4.3 shard_map.367.held_ref
  304.3 4.4 collective-permute-done.39
  312.4 8.1 %collective-permute-done.43 = bf16[256,768]{1,0:T(8,128)(2,1)S(1)} collective-permute-done((bf16[256,768]{1,0:T(8,128)(2,1)S(1)}, bf16[256,768]{1,0:T(8,128)(2,1)S(1)}, u32[]{:S(2)}, u32[]{:S(2)}) %collective-permute-start.43) | collective-permute-done | bytes 393248 | tf_op jit(solution)/shard_map/ppermute | solution.py:537
  322.9 4.7 multiply_reduce_fusion.2
  339.3 52.7 %shard_map.369 = (bf16[1024,640]{1,0:T(8,128)(2,1)}, bf16[256,640]{1,0:T(8,128)(2,1)}) custom-call(s32[1]{0:T(128)} %bitcast.5.place_ref, bf16[1024,640]{1,0:T(8,128)(2,1)} %convolution_convert_fusion.pack_ref, f32[1024,192]{1,0:T(8,128)} %subtract_multiply_fusion.1.do_ref, bf16[1024,768]{1,0:T(8,128)(2,1)} %get-tuple-element.100.z1_ref, ...), custom_call_target="tpu_custom_call" | custom-call | flops 70000001024 | bytes 25000000 | tf_op jit(solution)/shard_map/pallas_call | solution.py:480
  401.8 8.0 %collective-permute-done.50 = bf16[256,768]{1,0:T(8,128)(2,1)S(1)} collective-permute-done((bf16[256,768]{1,0:T(8,128)(2,1)S(1)}, bf16[256,768]{1,0:T(8,128)(2,1)S(1)}, u32[]{:S(2)}, u32[]{:S(2)}) %collective-permute-start.50) | collective-permute-done | bytes 393248 | tf_op jit(solution)/shard_map/ppermute | solution.py:537
  413.8 9.1 %collective-permute-done.52 = bf16[256,768]{1,0:T(8,128)(2,1)S(1)} collective-permute-done((bf16[256,768]{1,0:T(8,128)(2,1)S(1)}, bf16[256,768]{1,0:T(8,128)(2,1)S(1)}, u32[]{:S(2)}, u32[]{:S(2)}) %collective-permute-start.52) | collective-permute-done | bytes 393248 | tf_op jit(solution)/shard_map/ppermute | solution.py:537
  424.6 5.1 multiply_convert_fusion
  437.4 4.2 shard_map.370.held_ref
  441.6 5.6 collective-permute-done.56
  449.9 9.2 %collective-permute-done.58 = bf16[256,768]{1,0:T(8,128)(2,1)S(1)} collective-permute-done((bf16[256,768]{1,0:T(8,128)(2,1)S(1)}, bf16[256,768]{1,0:T(8,128)(2,1)S(1)}, u32[]{:S(2)}, u32[]{:S(2)}) %collective-permute-start.58) | collective-permute-done | bytes 393248 | tf_op jit(solution)/shard_map/ppermute | solution.py:537
  459.7 4.3 all-to-all-start.1
  464.1 4.3 multiply_reduce_fusion
  477.6 52.5 %shard_map.372 = (bf16[1024,640]{1,0:T(8,128)(2,1)}, bf16[256,640]{1,0:T(8,128)(2,1)}) custom-call(s32[1]{0:T(128)} %bitcast.5.place_ref, bf16[1024,640]{1,0:T(8,128)(2,1)} %convolution_convert_fusion.1.pack_ref, f32[1024,192]{1,0:T(8,128)} %subtract_multiply_fusion.do_ref, bf16[1024,768]{1,0:T(8,128)(2,1)} %get-tuple-element.120.z1_ref, ...), custom_call_target="tpu_custom_call" | custom-call | flops 70000001024 | bytes 25000000 | tf_op jit(solution)/shard_map/pallas_call | solution.py:480
  533.1 5.7 fusion.3
  543.0 6.1 %all-to-all-start = ((bf16[8,128,640]{2,1,0:T(8,128)(2,1)}), bf16[8,128,640]{2,1,0:T(8,128)(2,1)}, u32[]{:S(2)}, u32[]{:S(2)}) async-start(bf16[8,128,640]{2,1,0:T(8,128)(2,1)} %pad_maximum_fusion.8), calls=%async_computation.1 | async-start | bytes 2621440 | tf_op jit(solution)/shard_map/all_to_all | solution.py:695
  554.7 8.7 %collective-permute-done.64 = bf16[256,768]{1,0:T(8,128)(2,1)S(1)} collective-permute-done((bf16[256,768]{1,0:T(8,128)(2,1)S(1)}, bf16[256,768]{1,0:T(8,128)(2,1)S(1)}, u32[]{:S(2)}, u32[]{:S(2)}) %collective-permute-start.64) | collective-permute-done | bytes 393248 | tf_op jit(solution)/shard_map/ppermute | solution.py:537
  567.2 18.9 %all-to-all-done = bf16[8,128,640]{2,1,0:T(8,128)(2,1)} async-done(((bf16[8,128,640]{2,1,0:T(8,128)(2,1)}), bf16[8,128,640]{2,1,0:T(8,128)(2,1)}, u32[]{:S(2)}, u32[]{:S(2)}) %all-to-all-start) | async-done | bytes 1310752 | tf_op jit(solution)/shard_map/all_to_all | solution.py:695
  (473 shorter events, 177.3 us)
Async XLA Ops:
  7.2 126.0 %all-gather.3.cloned.1.call-start = ((), (), s32[]{:S(2)}) async-start(), calls=%async_computation.4 | async-start | bytes 4423680 | tf_op jit(solution)/shard_map/all_gather | solution.py:589
  7.9 12.0 %collective-permute-start.3 = (bf16[4,24]{1,0:T(4,128)(2,1)S(1)}, bf16[4,24]{1,0:T(4,128)(2,1)S(1)}, u32[]{:S(2)}, u32[]{:S(2)}) collective-permute-start(bf16[4,24]{1,0:T(4,128)(2,1)S(1)} %pad_maximum_fusion.25), channel_id=1, source_target_pairs={{0,3},{1,2},{2,1},{3,0},{4,7},{5,6},{6,5},{7,4},{8,11},{9,10},{10,... | collective-permute-start | bytes 584 | tf_op jit(solution)/shard_map/ppermute | solution.py:537
  11.5 11.3 %collective-permute-start.1 = (bf16[256,768]{1,0:T(8,128)(2,1)}, bf16[256,768]{1,0:T(8,128)(2,1)S(1)}, u32[]{:S(2)}, u32[]{:S(2)}) collective-permute-start(bf16[256,768]{1,0:T(8,128)(2,1)} %param.21), channel_id=1, source_target_pairs={{0,2},{1,3},{2,0},{3,1},{4,6},{5,7},{6,4},{7,5},{8,10},{9,11},{10,... | collective-permute-start | bytes 1179656 | tf_op jit(solution)/shard_map/ppermute | solution.py:537
  33.6 94.1 %collective-permute-start.10 = (bf16[256,768]{1,0:T(8,128)(2,1)}, bf16[256,768]{1,0:T(8,128)(2,1)}, u32[]{:S(2)}, u32[]{:S(2)}) collective-permute-start(bf16[256,768]{1,0:T(8,128)(2,1)} %param.22), channel_id=1, source_target_pairs={{0,1},{1,0},{2,3},{3,2},{4,5},{5,4},{6,7},{7,6},{8,9},{9,8},{10,11... | collective-permute-start | bytes 1179656 | tf_op jit(solution)/shard_map/ppermute | solution.py:537
  33.6 94.1 %collective-permute-start.11 = (bf16[256,768]{1,0:T(8,128)(2,1)}, bf16[256,768]{1,0:T(8,128)(2,1)}, u32[]{:S(2)}, u32[]{:S(2)}) collective-permute-start(bf16[256,768]{1,0:T(8,128)(2,1)} %param.22), channel_id=1, source_target_pairs={{0,2},{1,3},{2,0},{3,1},{4,6},{5,7},{6,4},{7,5},{8,10},{9,11},{10,... | collective-permute-start | bytes 1179656 | tf_op jit(solution)/shard_map/ppermute | solution.py:537
  35.1 46.8 %collective-permute-start.2 = (bf16[256,768]{1,0:T(8,128)(2,1)S(1)}, bf16[256,768]{1,0:T(8,128)(2,1)S(1)}, u32[]{:S(2)}, u32[]{:S(2)}) collective-permute-start(bf16[256,768]{1,0:T(8,128)(2,1)S(1)} %collective-permute-done.1), channel_id=1, source_target_pairs={{0,1},{1,0},{2,3},{3,2},{4,5},{5,4},{6,7},{7,6},{8,9},{9,8},{10,11... | collective-permute-start | bytes 1179656 | tf_op jit(solution)/shard_map/ppermute | solution.py:537
  45.7 208.8 %all-gather.5.cloned.1.call-start = ((), (), s32[]{:S(2)}) async-start(), calls=%async_computation.5 | async-start | bytes 3317760 | tf_op jit(solution)/shard_map/all_gather | solution.py:589
  140.3 11.4 %collective-permute-start.17 = (bf16[256,768]{1,0:T(8,128)(2,1)S(1)}, bf16[256,768]{1,0:T(8,128)(2,1)S(1)}, u32[]{:S(2)}, u32[]{:S(2)}) collective-permute-start(bf16[256,768]{1,0:T(8,128)(2,1)S(1)} %fusion.64), channel_id=1, source_target_pairs={{0,2},{1,3},{2,0},{3,1},{4,6},{5,7},{6,4},{7,5},{8,10},{9,11},{10,... | collective-permute-start | bytes 1179656 | tf_op jit(solution)/shard_map/ppermute | solution.py:537
  154.0 10.6 %collective-permute-start.19 = (bf16[256,768]{1,0:T(8,128)(2,1)S(1)}, bf16[256,768]{1,0:T(8,128)(2,1)S(1)}, u32[]{:S(2)}, u32[]{:S(2)}) collective-permute-start(bf16[256,768]{1,0:T(8,128)(2,1)S(1)} %multiply_convert_fusion.8), channel_id=1, source_target_pairs={{0,2},{1,3},{2,0},{3,1},{4,6},{5,7},{6,4},{7,5},{8,10},{9,11},{10,... | collective-permute-start | bytes 1179656 | tf_op jit(solution)/shard_map/ppermute | solution.py:537
  172.9 11.3 %collective-permute-start.23 = (bf16[256,768]{1,0:T(8,128)(2,1)S(1)}, bf16[256,768]{1,0:T(8,128)(2,1)}, u32[]{:S(2)}, u32[]{:S(2)}) collective-permute-start(bf16[256,768]{1,0:T(8,128)(2,1)S(1)} %fusion.61), channel_id=1, source_target_pairs={{0,2},{1,3},{2,0},{3,1},{4,6},{5,7},{6,4},{7,5},{8,10},{9,11},{10,... | collective-permute-start | bytes 1179656 | tf_op jit(solution)/shard_map/ppermute | solution.py:537
  186.5 10.4 %collective-permute-start.25 = (bf16[256,768]{1,0:T(8,128)(2,1)S(1)}, bf16[256,768]{1,0:T(8,128)(2,1)S(1)}, u32[]{:S(2)}, u32[]{:S(2)}) collective-permute-start(bf16[256,768]{1,0:T(8,128)(2,1)S(1)} %multiply_convert_fusion.7), channel_id=1, source_target_pairs={{0,2},{1,3},{2,0},{3,1},{4,6},{5,7},{6,4},{7,5},{8,10},{9,11},{10,... | collective-permute-start | bytes 1179656 | tf_op jit(solution)/shard_map/ppermute | solution.py:537
  196.9 213.6 %reduce-scatter.3.cloned.1.call-start = ((), (), s32[]{:S(2)}) async-start(), calls=%async_computation.6 | async-start | bytes 3317760 | tf_op jit(solution)/shard_map/reduce_scatter | solution.py:691
  263.7 11.5 %collective-permute-start.32 = (bf16[256,768]{1,0:T(8,128)(2,1)}, bf16[256,768]{1,0:T(8,128)(2,1)}, u32[]{:S(2)}, u32[]{:S(2)}) collective-permute-start(bf16[256,768]{1,0:T(8,128)(2,1)} %fusion.58), channel_id=1, source_target_pairs={{0,2},{1,3},{2,0},{3,1},{4,6},{5,7},{6,4},{7,5},{8,10},{9,11},{10,... | collective-permute-start | bytes 1179656 | tf_op jit(solution)/shard_map/ppermute | solution.py:537
  276.9 10.4 %collective-permute-start.35 = (bf16[256,768]{1,0:T(8,128)(2,1)S(1)}, bf16[256,768]{1,0:T(8,128)(2,1)S(1)}, u32[]{:S(2)}, u32[]{:S(2)}) collective-permute-start(bf16[256,768]{1,0:T(8,128)(2,1)S(1)} %multiply_convert_fusion.6), channel_id=1, source_target_pairs={{0,2},{1,3},{2,0},{3,1},{4,6},{5,7},{6,4},{7,5},{8,10},{9,11},{10,... | collective-permute-start | bytes 1179656 | tf_op jit(solution)/shard_map/ppermute | solution.py:537
  295.8 12.9 %collective-permute-start.37 = (bf16[256,768]{1,0:T(8,128)(2,1)S(1)}, bf16[256,768]{1,0:T(8,128)(2,1)S(1)}, u32[]{:S(2)}, u32[]{:S(2)}) collective-permute-start(bf16[256,768]{1,0:T(8,128)(2,1)S(1)} %get-tuple-element.276), channel_id=1, source_target_pairs={{0,1},{1,0},{2,3},{3,2},{4,5},{5,4},{6,7},{7,6},{8,9},{9,8},{10,11... | collective-permute-start | bytes 1179656 | tf_op jit(solution)/shard_map/ppermute | solution.py:537
  297.4 11.2 %collective-permute-start.39 = (bf16[256,768]{1,0:T(8,128)(2,1)S(1)}, bf16[256,768]{1,0:T(8,128)(2,1)S(1)}, u32[]{:S(2)}, u32[]{:S(2)}) collective-permute-start(bf16[256,768]{1,0:T(8,128)(2,1)S(1)} %fusion.56), channel_id=1, source_target_pairs={{0,2},{1,3},{2,0},{3,1},{4,6},{5,7},{6,4},{7,5},{8,10},{9,11},{10,... | collective-permute-start | bytes 1179656 | tf_op jit(solution)/shard_map/ppermute | solution.py:537
  310.2 10.3 %collective-permute-start.43 = (bf16[256,768]{1,0:T(8,128)(2,1)S(1)}, bf16[256,768]{1,0:T(8,128)(2,1)S(1)}, u32[]{:S(2)}, u32[]{:S(2)}) collective-permute-start(bf16[256,768]{1,0:T(8,128)(2,1)S(1)} %get-tuple-element.245), channel_id=1, source_target_pairs={{0,2},{1,3},{2,0},{3,1},{4,6},{5,7},{6,4},{7,5},{8,10},{9,11},{10,... | collective-permute-start | bytes 1179656 | tf_op jit(solution)/shard_map/ppermute | solution.py:537
  311.8 10.0 %collective-permute-start.40 = (bf16[256,768]{1,0:T(8,128)(2,1)S(1)}, bf16[256,768]{1,0:T(8,128)(2,1)S(1)}, u32[]{:S(2)}, u32[]{:S(2)}) collective-permute-start(bf16[256,768]{1,0:T(8,128)(2,1)S(1)} %get-tuple-element.275), channel_id=1, source_target_pairs={{0,1},{1,0},{2,3},{3,2},{4,5},{5,4},{6,7},{7,6},{8,9},{9,8},{10,11... | collective-permute-start | bytes 1179656 | tf_op jit(solution)/shard_map/ppermute | solution.py:537
  311.9 10.0 %collective-permute-start.41 = (bf16[256,768]{1,0:T(8,128)(2,1)S(1)}, bf16[256,768]{1,0:T(8,128)(2,1)S(1)}, u32[]{:S(2)}, u32[]{:S(2)}) collective-permute-start(bf16[256,768]{1,0:T(8,128)(2,1)S(1)} %get-tuple-element.274), channel_id=1, source_target_pairs={{0,1},{1,0},{2,3},{3,2},{4,5},{5,4},{6,7},{7,6},{8,9},{9,8},{10,11... | collective-permute-start | bytes 1179656 | tf_op jit(solution)/shard_map/ppermute | solution.py:537
  312.3 10.5 %collective-permute-start.42 = (bf16[256,768]{1,0:T(8,128)(2,1)S(1)}, bf16[256,768]{1,0:T(8,128)(2,1)S(1)}, u32[]{:S(2)}, u32[]{:S(2)}) collective-permute-start(bf16[256,768]{1,0:T(8,128)(2,1)S(1)} %get-tuple-element.245), channel_id=1, source_target_pairs={{0,1},{1,0},{2,3},{3,2},{4,5},{5,4},{6,7},{7,6},{8,9},{9,8},{10,11... | collective-permute-start | bytes 1179656 | tf_op jit(solution)/shard_map/ppermute | solution.py:537
  338.2 53.8 %collective-permute-start.47 = (bf16[256,768]{1,0:T(8,128)(2,1)S(1)}, bf16[256,768]{1,0:T(8,128)(2,1)S(1)}, u32[]{:S(2)}, u32[]{:S(2)}) collective-permute-start(bf16[256,768]{1,0:T(8,128)(2,1)S(1)} %get-tuple-element.108), channel_id=1, source_target_pairs={{0,2},{1,3},{2,0},{3,1},{4,6},{5,7},{6,4},{7,5},{8,10},{9,11},{10,... | collective-permute-start | bytes 1179656 | tf_op jit(solution)/shard_map/ppermute | solution.py:537
  395.4 14.4 %collective-permute-start.48 = (bf16[256,768]{1,0:T(8,128)(2,1)S(1)}, bf16[256,768]{1,0:T(8,128)(2,1)S(1)}, u32[]{:S(2)}, u32[]{:S(2)}) collective-permute-start(bf16[256,768]{1,0:T(8,128)(2,1)S(1)} %get-tuple-element.272), channel_id=1, source_target_pairs={{0,1},{1,0},{2,3},{3,2},{4,5},{5,4},{6,7},{7,6},{8,9},{9,8},{10,11... | collective-permute-start | bytes 1179656 | tf_op jit(solution)/shard_map/ppermute | solution.py:537
  398.6 11.2 %collective-permute-start.50 = (bf16[256,768]{1,0:T(8,128)(2,1)S(1)}, bf16[256,768]{1,0:T(8,128)(2,1)S(1)}, u32[]{:S(2)}, u32[]{:S(2)}) collective-permute-start(bf16[256,768]{1,0:T(8,128)(2,1)S(1)} %fusion.53), channel_id=1, source_target_pairs={{0,2},{1,3},{2,0},{3,1},{4,6},{5,7},{6,4},{7,5},{8,10},{9,11},{10,... | collective-permute-start | bytes 1179656 | tf_op jit(solution)/shard_map/ppermute | solution.py:537
  412.4 10.4 %collective-permute-start.52 = (bf16[256,768]{1,0:T(8,128)(2,1)S(1)}, bf16[256,768]{1,0:T(8,128)(2,1)S(1)}, u32[]{:S(2)}, u32[]{:S(2)}) collective-permute-start(bf16[256,768]{1,0:T(8,128)(2,1)S(1)} %convert_element_type.258), channel_id=1, source_target_pairs={{0,2},{1,3},{2,0},{3,1},{4,6},{5,7},{6,4},{7,5},{8,10},{9,11},{10,... | collective-permute-start | bytes 1179656 | tf_op jit(solution)/shard_map/ppermute | solution.py:537
  434.3 12.9 %collective-permute-start.54 = (bf16[256,768]{1,0:T(8,128)(2,1)S(1)}, bf16[256,768]{1,0:T(8,128)(2,1)S(1)}, u32[]{:S(2)}, u32[]{:S(2)}) collective-permute-start(bf16[256,768]{1,0:T(8,128)(2,1)S(1)} %get-tuple-element.270), channel_id=1, source_target_pairs={{0,1},{1,0},{2,3},{3,2},{4,5},{5,4},{6,7},{7,6},{8,9},{9,8},{10,11... | collective-permute-start | bytes 1179656 | tf_op jit(solution)/shard_map/ppermute | solution.py:537
  436.0 11.2 %collective-permute-start.56 = (bf16[256,768]{1,0:T(8,128)(2,1)S(1)}, bf16[256,768]{1,0:T(8,128)(2,1)S(1)}, u32[]{:S(2)}, u32[]{:S(2)}) collective-permute-start(bf16[256,768]{1,0:T(8,128)(2,1)S(1)} %fusion.51), channel_id=1, source_target_pairs={{0,2},{1,3},{2,0},{3,1},{4,6},{5,7},{6,4},{7,5},{8,10},{9,11},{10,... | collective-permute-start | bytes 1179656 | tf_op jit(solution)/shard_map/ppermute | solution.py:537
  448.8 10.3 %collective-permute-start.58 = (bf16[256,768]{1,0:T(8,128)(2,1)S(1)}, bf16[256,768]{1,0:T(8,128)(2,1)S(1)}, u32[]{:S(2)}, u32[]{:S(2)}) collective-permute-start(bf16[256,768]{1,0:T(8,128)(2,1)S(1)} %get-tuple-element.242), channel_id=1, source_target_pairs={{0,2},{1,3},{2,0},{3,1},{4,6},{5,7},{6,4},{7,5},{8,10},{9,11},{10,... | collective-permute-start | bytes 1179656 | tf_op jit(solution)/shard_map/ppermute | solution.py:537
  449.8 14.2 %collective-permute-start.57 = (bf16[256,768]{1,0:T(8,128)(2,1)S(1)}, bf16[256,768]{1,0:T(8,128)(2,1)}, u32[]{:S(2)}, u32[]{:S(2)}) collective-permute-start(bf16[256,768]{1,0:T(8,128)(2,1)S(1)} %get-tuple-element.242), channel_id=1, source_target_pairs={{0,1},{1,0},{2,3},{3,2},{4,5},{5,4},{6,7},{7,6},{8,9},{9,8},{10,11... | collective-permute-start | bytes 1179656 | tf_op jit(solution)/shard_map/ppermute | solution.py:537
  459.7 83.3 %all-to-all-start.1 = ((bf16[8,128,640]{2,1,0:T(8,128)(2,1)}), bf16[8,128,640]{2,1,0:T(8,128)(2,1)}, u32[]{:S(2)}, u32[]{:S(2)}) async-start(bf16[8,128,640]{2,1,0:T(8,128)(2,1)} %pad_maximum_fusion.7), calls=%async_computation.2 | async-start | bytes 2621440 | tf_op jit(solution)/shard_map/all_to_all | solution.py:695
  464.0 131.6 %reduce-scatter.5.cloned.1.call-start = ((), (), s32[]{:S(2)}) async-start(), calls=%async_computation.7 | async-start | bytes 3317760 | tf_op jit(solution)/shard_map/reduce_scatter | solution.py:691
  543.0 43.1 %all-to-all-start = ((bf16[8,128,640]{2,1,0:T(8,128)(2,1)}), bf16[8,128,640]{2,1,0:T(8,128)(2,1)}, u32[]{:S(2)}, u32[]{:S(2)}) async-start(bf16[8,128,640]{2,1,0:T(8,128)(2,1)} %pad_maximum_fusion.8), calls=%async_computation.1 | async-start | bytes 2621440 | tf_op jit(solution)/shard_map/all_to_all | solution.py:695
  552.2 11.2 %collective-permute-start.64 = (bf16[256,768]{1,0:T(8,128)(2,1)S(1)}, bf16[256,768]{1,0:T(8,128)(2,1)S(1)}, u32[]{:S(2)}, u32[]{:S(2)}) collective-permute-start(bf16[256,768]{1,0:T(8,128)(2,1)S(1)} %fusion.48), channel_id=1, source_target_pairs={{0,2},{1,3},{2,0},{3,1},{4,6},{5,7},{6,4},{7,5},{8,10},{9,11},{10,... | collective-permute-start | bytes 1179656 | tf_op jit(solution)/shard_map/ppermute | solution.py:537
  (119 other events, 1145.0 us)
Sparse Core Ops, SparseCore 0:
  45.8 78.3 all-gather.2
  197.0 57.4 all-gather.4
  339.4 70.8 reduce-scatter.2
  477.7 83.9 reduce-scatter.4
